TPU v7x, 32 devices: a whole 2x2x4 slice. The times are simulated.
32 devices in a mesh: row: 4 (over y, x), col: 8 (over z, core).
Axes of the slice: x: 2, y: 2, z: 4, core: 2. Of those that a mesh axis runs over, the one named last changes fastest.
Arguments:
- pair: float32 [256, 256, 128], P('row', 'col'), may hold values from -6 to 6
- norm_in_gain: float32 [2, 128], replicated, may hold values from 0.1 to 1.9
- w_proj: bfloat16 [2, 128, 512], replicated, may hold values from -0.5 to 0.5
- w_gate: bfloat16 [2, 128, 128], replicated, may hold values from -0.5 to 0.5
- norm_out_gain: float32 [2, 128], replicated, may hold values from 0.1 to 1.9
- w_out: bfloat16 [2, 128, 128], replicated, may hold values from -0.5 to 0.5
Outputs:
- updated: float32 [256, 256, 128], P('row', 'col')
All inputs are finite; a program needn't handle non-finite values.
Results may differ from a plain program's by a relative error of at most 0.0049.
Values may be sent and summed in bfloat16 or wider, within the bound.
No kernel may reach another device: no remote copies, remote signals or barrier semaphores. Data moves between devices by JAX's collectives and lax.ppermute only.
A program may use at most 128 MiB of HBM per device.

v0:
```python
import jax
import jax.numpy as jnp
from jax import lax
from jax.sharding import PartitionSpec as P


def layer_norm(values, gain):
    center = values - jnp.mean(values, axis=-1, keepdims=True)
    spread = jnp.mean(center * center, axis=-1, keepdims=True)
    return center * lax.rsqrt(spread + 1e-05) * gain


def branches(pair, gain, w_proj, w_gate):
    first_dim, second_dim, chans = pair.shape
    normed = layer_norm(pair, gain).astype(jnp.bfloat16).reshape(first_dim * second_dim, chans)
    proj = jnp.dot(normed, w_proj, preferred_element_type=jnp.float32)
    hidden = w_proj.shape[1] // 4
    left = (jax.nn.sigmoid(proj[:, :hidden]) * proj[:, hidden : 2 * hidden]).astype(jnp.bfloat16)
    right = (jax.nn.sigmoid(proj[:, 2 * hidden : 3 * hidden]) * proj[:, 3 * hidden :]).astype(
        jnp.bfloat16
    )
    gate = jax.nn.sigmoid(jnp.dot(normed, w_gate, preferred_element_type=jnp.float32))
    shape = (first_dim, second_dim, hidden)
    return (left.reshape(shape), right.reshape(shape), gate.reshape(pair.shape))


def finish(pair, summed, gate, gain, w_out):
    mixed = layer_norm(summed, gain).astype(jnp.bfloat16)
    hidden = summed.shape[-1]
    out = jnp.dot(mixed.reshape(-1, hidden), w_out, preferred_element_type=jnp.float32)
    return pair + gate * out.reshape(pair.shape)


def body(pair, norm_in_gain, w_proj, w_gate, norm_out_gain, w_out):
    left, right, gate = branches(pair, norm_in_gain[0], w_proj[0], w_gate[0])
    right_all = lax.all_gather(right, "row", axis=0, tiled=True)
    piece = right_all
    summed = lax.psum_scatter(
        jnp.einsum("jkh,ikh->jih", piece, left, preferred_element_type=jnp.float32),
        "col",
        scatter_dimension=0,
        tiled=True,
    )
    summed = jnp.transpose(summed, (1, 0, 2))
    first = finish(pair, summed, gate, norm_out_gain[0], w_out[0])
    left, right, gate = branches(first, norm_in_gain[1], w_proj[1], w_gate[1])
    left_all = lax.all_gather(left, "col", axis=1, tiled=True)
    piece = left_all
    summed = lax.psum_scatter(
        jnp.einsum("kih,kjh->ijh", piece, right, preferred_element_type=jnp.float32),
        "row",
        scatter_dimension=0,
        tiled=True,
    )
    return finish(first, summed, gate, norm_out_gain[1], w_out[1])


def solution(mesh):
    placed = (P("row", "col", None), P(), P(), P(), P(), P())
    return jax.shard_map(
        body, mesh=mesh, in_specs=placed, out_specs=P("row", "col", None), check_vma=False
    )
```

profile of v0, /device:TPU:0, one launch (start us, length us, event | category | flops | bytes accessed | tf_op | source)
XLA Modules:
  0.0 332.8 jit_solution(5892656797539689878)
XLA Ops:
  6.5 1.6 reduce_sum.72
  8.3 1.9 multiply_reduce_fusion.3
  11.1 1.8 multiply_convert_fusion.3
  13.7 1.6 fusion.30
  15.3 1.4 fusion.16
  16.7 1.7 copy.62
  18.4 36.4 %all-gather.3.cloned.1.call-done = bf16[256,32,128]{2,1,0:T(8,128)(2,1)} async-done(((bf16[64,32,128]{2,1,0:T(8,128)(2,1)}), bf16[256,32,128]{2,1,0:T(8,128)(2,1)}) %all-gather.3.cloned.1.call-update) | async-done | bytes 2097168 | tf_op jit(solution)/shard_map/all_gather | solution.py:36
  54.8 3.9 %copy.63 = bf16[256,32,128]{0,1,2:T(8,128)(2,1)S(1)} copy(bf16[256,32,128]{2,1,0:T(8,128)(2,1)} %all-gather.3.cloned.1.call-done) | data formatting | bytes 4194304 | tf_op jit(solution)/shard_map/all_gather | solution.py:36
  58.8 4.5 %convolution_bitcast_fusion = f32[256,64,128]{0,1,2:T(8,128)} fusion(bf16[64,32,128]{0,1,2:T(8,128)(2,1)S(1)} %copy.62, bf16[256,32,128]{0,1,2:T(8,128)(2,1)S(1)} %copy.63), kind=kOutput, calls=%fused_computation | convolution fusion | flops 134217728 | bytes 11010048 | tf_op jit(solution)/shard_map/jkh,ikh->jih/dot_general | solution.py:39
  63.3 8.9 %copy.64 = f32[256,64,128]{2,1,0:T(8,128)} copy(f32[256,64,128]{0,1,2:T(8,128)} %convolution_bitcast_fusion) | data formatting | bytes 16777216 | tf_op jit(solution)/shard_map/jkh,ikh->jih/transpose | solution.py:39
  73.6 88.3 %reduce-scatter.3.cloned.1.call-done = f32[32,64,128]{2,1,0:T(8,128)} async-done(((f32[256,64,128]{2,1,0:T(8,128)}), f32[32,64,128]{2,1,0:T(8,128)}) %reduce-scatter.3.cloned.1.call-update) | async-done | bytes 1048592 | tf_op jit(solution)/shard_map/reduce_scatter | solution.py:38
  161.9 1.6 bitcast_reduce_fusion
  163.5 1.9 multiply_reduce_fusion.2
  165.4 1.9 multiply_convert_fusion.2
  170.8 2.6 copy.70
  173.4 1.7 copy.71
  175.1 78.8 %all-gather.5.cloned.1.call-done = bf16[64,256,128]{0,1,2:T(8,128)(2,1)} async-done(((bf16[64,32,128]{0,1,2:T(8,128)(2,1)}), bf16[64,256,128]{0,1,2:T(8,128)(2,1)}) %all-gather.5.cloned.1.call-update) | async-done | bytes 4194320 | tf_op jit(solution)/shard_map/all_gather | solution.py:47
  253.9 8.2 %convolution_bitcast_fusion.1 = f32[256,32,128]{0,1,2:T(8,128)} fusion(bf16[64,32,128]{0,1,2:T(8,128)(2,1)S(1)} %copy.71, bf16[64,256,128]{0,1,2:T(8,128)(2,1)} %all-gather.5.cloned.1.call-done), kind=kOutput, calls=%fused_computation.9 | convolution fusion | flops 134217728 | bytes 8912896 | tf_op jit(solution)/shard_map/kih,kjh->ijh/dot_general | solution.py:50
  262.2 6.0 %copy.72 = f32[256,32,128]{2,1,0:T(8,128)} copy(f32[256,32,128]{0,1,2:T(8,128)} %convolution_bitcast_fusion.1) | data formatting | bytes 8388608 | tf_op jit(solution)/shard_map/kih,kjh->ijh/transpose | solution.py:50
  268.1 0.8 copy-done.7
  269.4 50.1 %reduce-scatter.5.cloned.1.call-done = f32[64,32,128]{2,1,0:T(8,128)} async-done(((f32[256,32,128]{2,1,0:T(8,128)}), f32[64,32,128]{2,1,0:T(8,128)}) %reduce-scatter.5.cloned.1.call-update) | async-done | bytes 1048592 | tf_op jit(solution)/shard_map/reduce_scatter | solution.py:49
  319.5 1.6 reduce_sum.78
  321.3 1.9 multiply_reduce_fusion
  323.3 2.9 fusion.6
  (52 shorter events, 7.7 us)
Async XLA Ops:
  6.5 48.3 %all-gather.3.cloned.1.call-start = ((), (), s32[]{:S(2)}) async-start(), calls=%async_computation.2 | async-start | bytes 2621440 | tf_op jit(solution)/shard_map/all_gather | solution.py:36
  12.9 0.8 copy-start.1
  16.7 145.3 %reduce-scatter.3.cloned.1.call-start = ((), (), s32[]{:S(2)}) async-start(), calls=%async_computation.3 | async-start | bytes 9437184 | tf_op jit(solution)/shard_map/reduce_scatter | solution.py:38
  72.1 0.7 copy-start.5
  72.1 1.1 copy-start.2
  72.1 1.1 copy-start.6
  72.2 181.8 %all-gather.5.cloned.1.call-start = ((), (), s32[]{:S(2)}) async-start(), calls=%async_computation.4 | async-start | bytes 9437184 | tf_op jit(solution)/shard_map/all_gather | solution.py:47
  73.2 94.1 %copy-start = (f32[64,32,128]{2,1,0:T(8,128)S(1)}, f32[64,32,128]{2,1,0:T(8,128)}, u32[]{:S(2)}) copy-start(f32[64,32,128]{2,1,0:T(8,128)} %param.6) | copy-start | bytes 3145732
  73.2 94.1 %copy-start.4 = (bf16[2,128,128]{2,1,0:T(8,128)(2,1)S(1)}, bf16[2,128,128]{2,1,0:T(8,128)(2,1)}, u32[]{:S(2)}) copy-start(bf16[2,128,128]{2,1,0:T(8,128)(2,1)} %param.11) | copy-start | bytes 196612
  165.4 4.1 %copy-start.3 = (bf16[2,128,512]{2,1,0:T(8,128)(2,1)S(1)}, bf16[2,128,512]{2,1,0:T(8,128)(2,1)}, u32[]{:S(2)}) copy-start(bf16[2,128,512]{2,1,0:T(8,128)(2,1)} %param.8) | copy-start | bytes 786436
  173.4 146.1 %reduce-scatter.5.cloned.1.call-start = ((), (), s32[]{:S(2)}) async-start(), calls=%async_computation.5 | async-start | bytes 5242880 | tf_op jit(solution)/shard_map/reduce_scatter | solution.py:49
  268.1 0.8 copy-start.7
Sparse Core Ops, SparseCore 0:
  16.8 38.0 all-gather.2
  72.3 89.5 reduce-scatter.2
  173.5 80.3 all-gather.4
  268.3 51.2 reduce-scatter.4
where the time goes:
time: 334 us; the launch traced here: 333 us
  waiting for transfers between devices  254 us (76%)
  local copies, waits for them, and re-layouts  28.8 us (9%)
  matrix products  19.4 us (6%)
  other arithmetic  17.2 us (5%)
  between operations  13.3 us (4%)
    reduce_scatter x1, waiting for transfers between devices, body(): lax.psum_scatter(jnp.einsum('jkh,ikh->jih', piece, left, preferred_elemen...  88.3 us
    all_gather x1, waiting for transfers between devices, body(): left_all = lax.all_gather(left, 'col', axis=1, tiled=True)  78.8 us
    reduce_scatter x1, waiting for transfers between devices, body(): lax.psum_scatter(jnp.einsum('kih,kjh->ijh', piece, right, preferred_eleme...  50.1 us
    all_gather x1, waiting for transfers between devices, body(): right_all = lax.all_gather(right, 'row', axis=0, tiled=True)  36.4 us
    transpose x1, local copies, waits for them, and re-layouts, body(): jnp.einsum('jkh,ikh->jih', piece, left, preferred_element_type=jnp.float32)  8.86 us
    dot_general x1, matrix products, body(): jnp.einsum('kih,kjh->ijh', piece, right, preferred_element_type=jnp.float32)  8.23 us
  transfers between devices with their start and end apart: 4, of which 4 were waited for; matrix products, arithmetic and copies ran while one was open for 1% of the time, Pallas kernels for 0%

commit v1 on v0

v1 whole, which is shorter than its diff:
```python
import functools

import jax
import jax.numpy as jnp
from jax import lax
from jax.experimental import pallas as pl
from jax.experimental.pallas import tpu as pltpu
from jax.sharding import PartitionSpec as P

LANES = 128
BF16 = jnp.bfloat16
F32 = jnp.float32
VMEM_LIMIT = 48 * 1024 * 1024


def sigmoid(x):
    return 0.5 * jnp.tanh(0.5 * x) + 0.5


def norm_rows(x, gain):
    center = x - jnp.mean(x, axis=-1, keepdims=True)
    spread = jnp.mean(center * center, axis=-1, keepdims=True)
    return (center * lax.rsqrt(spread + 1e-05) * gain).astype(BF16)


def load_chunk(ref, s, first, second):
    split = LANES // first
    n1 = second // split
    return jnp.concatenate(
        [ref[pl.ds(l * n1 + s, first, stride=second), :] for l in range(split)], axis=0
    )


def store_chunk(ref, s, first, second, value):
    split = LANES // first
    n1 = second // split
    for l in range(split):
        ref[pl.ds(l * n1 + s, first, stride=second), :] = value[l * first : (l + 1) * first]


def emit_branches(normed, s, n1, w_t, planes):
    hidden = w_t.shape[0] // 4
    proj = lax.dot_general(w_t, normed, (((1,), (1,)), ((), ())), preferred_element_type=F32)
    left = sigmoid(proj[:hidden]) * proj[hidden : 2 * hidden]
    right = sigmoid(proj[2 * hidden : 3 * hidden]) * proj[3 * hidden :]
    for t in range(normed.shape[0] // LANES):
        cols = slice(t * LANES, (t + 1) * LANES)
        planes[pl.ds(s + t, hidden, stride=n1), :] = left[:, cols]
        planes[pl.ds(hidden * n1 + s + t, hidden, stride=n1), :] = right[:, cols]


def pack_branches(planes, send_ref):
    ndev, _, rows, _ = send_ref.shape
    for side in range(2):
        part = planes[side * ndev * rows : (side + 1) * ndev * rows, :].astype(BF16)
        send_ref[:, side] = part.reshape(ndev, rows, LANES)


def project_kernel(u, first, second, pair_ref, gain_ref, w_ref, send_ref, planes):
    n1 = second * first // LANES
    w_t = w_ref[u].T
    gain = gain_ref[u : u + 1, :]
    for s in range(0, n1, 2):
        x = jnp.concatenate([load_chunk(pair_ref, s + t, first, second) for t in range(2)], axis=0)
        emit_branches(norm_rows(x, gain), s, n1, w_t, planes)
    pack_branches(planes, send_ref)


def gate_kernel(u, first, second, ordered, pair_ref, gain_ref, w_ref, gate_ref):
    n1 = second * first // LANES
    gain = gain_ref[u : u + 1, :]
    w = w_ref[u]
    for s in range(0, n1, 2):
        if ordered:
            x = pair_ref[s * LANES : (s + 2) * LANES, :]
        else:
            x = jnp.concatenate([load_chunk(pair_ref, s + t, first, second) for t in range(2)], axis=0)
        gate_ref[s * LANES : (s + 2) * LANES, :] = sigmoid(
            jnp.dot(norm_rows(x, gain), w, preferred_element_type=F32)
        )


def triangle_kernel(contract, rows, cols, first, recv_ref, out_ref, left, right):
    ndev, _, depth, n1, _ = recv_ref.shape
    split = LANES // first
    for h in range(depth):
        for side, dense in ((0, left), (1, right)):
            for c in range(cols):
                for l in range(split):
                    at = (c * split + l) * n1
                    dense[at : at + n1, :] = jnp.concatenate(
                        [
                            recv_ref[r * cols + c, side, h, :, l * first : (l + 1) * first]
                            for r in range(rows)
                        ],
                        axis=1,
                    )
        summed = lax.dot_general(
            right[...], left[...], (((contract,), (contract,)), ((), ())), preferred_element_type=F32
        ).astype(BF16)
        for r in range(rows):
            for c in range(cols):
                out_ref[r * cols + c, h] = jnp.concatenate(
                    [
                        summed[(c * split + l) * n1 : (c * split + l + 1) * n1, r * first : (r + 1) * first]
                        for l in range(split)
                    ],
                    axis=1,
                )


def norm_planes(summed_ref, normal):
    hidden, n1, _ = summed_ref.shape
    x = summed_ref[...].astype(F32)
    center = x - jnp.mean(x, axis=0, keepdims=True)
    spread = jnp.mean(center * center, axis=0, keepdims=True)
    normal[...] = (center * lax.rsqrt(spread + 1e-05)).reshape(hidden * n1, LANES)


def output_chunk(normal, s, n1, gain_cols, w):
    hidden = w.shape[0]
    mixed = jnp.concatenate(
        [(normal[pl.ds(s + t, hidden, stride=n1), :] * gain_cols).astype(BF16) for t in range(2)], axis=1
    )
    return lax.dot_general(mixed, w, (((0,), (0,)), ((), ())), preferred_element_type=F32)


def middle_kernel(
    first, second, pair_ref, summed_ref, gate_ref, out_gain_ref, w_out_ref, gain_ref, w_ref,
    first_ref, send_ref, normal, planes,
):
    n1 = second * first // LANES
    hidden = w_out_ref.shape[1]
    norm_planes(summed_ref, normal)
    gain_cols = jnp.broadcast_to(out_gain_ref[0:1, :], (LANES, hidden)).T
    w_t = w_ref[1].T
    gain = gain_ref[1:2, :]
    for s in range(0, n1, 2):
        out = output_chunk(normal, s, n1, gain_cols, w_out_ref[0])
        z = jnp.concatenate([load_chunk(pair_ref, s + t, first, second) for t in range(2)], axis=0)
        at = slice(s * LANES, (s + 2) * LANES)
        z = z + gate_ref[at, :] * out
        first_ref[at, :] = z
        emit_branches(norm_rows(z, gain), s, n1, w_t, planes)
    pack_branches(planes, send_ref)


def last_kernel(
    first, second, pair_ref, summed_ref, gate_ref, out_gain_ref, w_out_ref, updated_ref, normal
):
    n1 = second * first // LANES
    hidden = w_out_ref.shape[1]
    norm_planes(summed_ref, normal)
    gain_cols = jnp.broadcast_to(out_gain_ref[1:2, :], (LANES, hidden)).T
    for s in range(0, n1, 2):
        out = output_chunk(normal, s, n1, gain_cols, w_out_ref[1])
        at = slice(s * LANES, (s + 2) * LANES)
        z = pair_ref[at, :] + gate_ref[at, :] * out
        for t in range(2):
            store_chunk(updated_ref, s + t, first, second, z[t * LANES : (t + 1) * LANES])


def call(kernel, outs, scratch, flops, *args):
    moved = sum(a.size * a.dtype.itemsize for a in args) + sum(o.size * o.dtype.itemsize for o in outs)
    return pl.pallas_call(
        kernel,
        out_shape=outs if len(outs) > 1 else outs[0],
        in_specs=[pl.BlockSpec(memory_space=pltpu.VMEM)] * len(args),
        out_specs=[pl.BlockSpec(memory_space=pltpu.VMEM)] * len(outs)
        if len(outs) > 1
        else pl.BlockSpec(memory_space=pltpu.VMEM),
        scratch_shapes=scratch,
        compiler_params=pltpu.CompilerParams(vmem_limit_bytes=VMEM_LIMIT),
        cost_estimate=pl.CostEstimate(flops=flops, bytes_accessed=moved, transcendentals=0),
    )(*args)


def body(rows, cols, pair, norm_in_gain, w_proj, w_gate, norm_out_gain, w_out):
    first, second, chans = pair.shape
    hidden = w_out.shape[1]
    ndev = rows * cols
    depth = hidden // ndev
    count = first * second
    n1 = count // LANES
    total = rows * first
    axes = ("row", "col")
    flat = pair.reshape(count, chans)

    send_shape = jax.ShapeDtypeStruct((ndev, 2, depth * n1, LANES), BF16)
    planes = pltpu.VMEM((2 * hidden * n1, LANES), F32)
    normal = pltpu.VMEM((hidden * n1, LANES), F32)
    flat_shape = jax.ShapeDtypeStruct((count, chans), F32)
    proj_flops = 2 * count * chans * 4 * hidden
    gate_flops = 2 * count * chans * chans

    def exchange(block):
        return lax.all_to_all(block, axes, 0, 0, tiled=True)

    def triangle(recv, contract):
        out = call(
            functools.partial(triangle_kernel, contract, rows, cols, first),
            [jax.ShapeDtypeStruct((ndev, depth, n1, LANES), BF16)],
            [pltpu.VMEM((cols * second, total), BF16)] * 2,
            2 * depth * total**3,
            recv.reshape(ndev, 2, depth, n1, LANES),
        )
        return exchange(out).reshape(hidden, n1, LANES)

    send = call(
        functools.partial(project_kernel, 0, first, second),
        [send_shape], [planes], proj_flops, flat, norm_in_gain, w_proj,
    )
    recv = exchange(send)
    gate = call(
        functools.partial(gate_kernel, 0, first, second, False),
        [flat_shape], [], gate_flops, flat, norm_in_gain, w_gate,
    )
    summed = triangle(recv, 0)
    middle, send = call(
        functools.partial(middle_kernel, first, second),
        [flat_shape, send_shape], [normal, planes], proj_flops + gate_flops,
        flat, summed, gate, norm_out_gain, w_out, norm_in_gain, w_proj,
    )
    recv = exchange(send)
    gate = call(
        functools.partial(gate_kernel, 1, first, second, True),
        [flat_shape], [], gate_flops, middle, norm_in_gain, w_gate,
    )
    summed = triangle(recv, 1)
    updated = call(
        functools.partial(last_kernel, first, second),
        [flat_shape], [normal], gate_flops,
        middle, summed, gate, norm_out_gain, w_out,
    )
    return updated.reshape(pair.shape)


def solution(mesh):
    placed = (P("row", "col", None), P(), P(), P(), P(), P())
    return jax.shard_map(
        functools.partial(body, mesh.shape["row"], mesh.shape["col"]),
        mesh=mesh,
        in_specs=placed,
        out_specs=P("row", "col", None),
        check_vma=False,
    )
```

time: 334 us -> 119 us (0.36)
  waiting for transfers between devices: 254 us -> 30.5 us
  blocking collectives: 0 us -> 64.2 us
  local copies, waits for them, and re-layouts: 28.8 us -> 4.71 us
  matrix products: 19.4 us -> 0 us
  other arithmetic: 17.2 us -> 0 us
  Pallas kernels: 0 us -> 13.3 us
  between operations: 13.3 us -> 0.1 us
  starting transfers between devices: 0.31 us -> 5.34 us
    reduce_scatter x2 -> x0, waiting for transfers between devices: 138 us -> none  [the longest x1 88.3 us: body(): lax.psum_scatter(jnp.einsum('jkh,ikh->jih', piece, left, preferred_elemen...]
    all_gather x2 -> x0, waiting for transfers between devices: 115 us -> none  [the longest x1 78.8 us: body(): left_all = lax.all_gather(left, 'col', axis=1, tiled=True)]
    all_to_all x0 -> x2, blocking collectives: none -> 64.2 us  [exchange(): return lax.all_to_all(block, axes, 0, 0, tiled=True)]
    all_to_all x0 -> x2, waiting for transfers between devices: none -> 30.5 us  [exchange(): return lax.all_to_all(block, axes, 0, 0, tiled=True)]
    dot_general x8 -> x0, matrix products: 19.4 us -> none  [the longest x1 8.23 us: body(): jnp.einsum('kih,kjh->ijh', piece, right, preferred_element_type=jnp.float32)]
    transpose x2 -> x0, local copies, waits for them, and re-layouts: 14.8 us -> none  [the longest x1 8.86 us: body(): jnp.einsum('jkh,ikh->jih', piece, left, preferred_element_type=jnp.float32)]
    pallas_call x0 -> x7, Pallas kernels: none -> 13.3 us  [call(): pl.pallas_call(kernel, out_shape=outs if len(outs) > 1 else outs[0], in_s...]
    reduce_sum x7 -> x0, other arithmetic: 10.9 us -> none  [the longest x4 6.25 us: layer_norm(): spread = jnp.mean(center * center, axis=-1, keepdims=True)]
  transfers between devices with their start and end apart: 4 -> 2, of which waited for: 4 -> 2; matrix products, arithmetic and copies ran while one was open for 1% -> 0% of each run, Pallas kernels for 0% -> 2%
where the time goes in v1:
time: 119 us; the launch traced here: 118 us
  blocking collectives  64.2 us (54%)
  waiting for transfers between devices  30.5 us (26%)
  Pallas kernels  13.3 us (11%)
  starting transfers between devices  5.34 us (4%)
  local copies, waits for them, and re-layouts  4.71 us (4%)
    all_to_all x2, blocking collectives, exchange(): return lax.all_to_all(block, axes, 0, 0, tiled=True)  64.2 us
    all_to_all x2, waiting for transfers between devices, exchange(): return lax.all_to_all(block, axes, 0, 0, tiled=True)  30.5 us
    pallas_call x7, Pallas kernels, call(): pl.pallas_call(kernel, out_shape=outs if len(outs) > 1 else outs[0], in_s...  13.3 us
    all_to_all x2, starting transfers between devices, exchange(): return lax.all_to_all(block, axes, 0, 0, tiled=True)  5.34 us
    unnamed x20, local copies, waits for them, and re-layouts  4.71 us
  transfers between devices with their start and end apart: 2, of which 2 were waited for; matrix products, arithmetic and copies ran while one was open for 0% of the time, Pallas kernels for 2%

profile of v1, /device:TPU:0, one launch (start us, length us, event | category | flops | bytes accessed | tf_op | source)
XLA Modules:
  0.0 118.2 jit_solution(10359753241427177628)
XLA Ops:
  0.0 0.7 copy-done.8
  0.7 1.2 %copy-done = f32[64,32,128]{2,1,0:T(8,128)S(1)} copy-done((f32[64,32,128]{2,1,0:T(8,128)S(1)}, f32[64,32,128]{2,1,0:T(8,128)}, u32[]{:S(2)}) %copy-start) | copy-done | bytes 1048600
  1.9 0.9 copy-done.4
  2.9 2.0 %shard_map.64 = bf16[32,2,64,128]{3,2,1,0:T(8,128)(2,1)S(1)} custom-call(f32[2048,128]{1,0:T(8,128)S(1)} %bitcast.6, f32[2,128]{1,0:T(2,128)S(1)} %copy-done.8, bf16[2,128,512]{2,1,0:T(8,128)(2,1)S(1)} %copy-done.4), custom_call_target="tpu_custom_call" | custom-call | flops 268435456 | bytes 2360320 | tf_op jit(solution)/shard_map/pallas_call | solution.py:165
  4.8 34.7 %all_to_all.20 = bf16[32,2,64,128]{3,2,1,0:T(8,128)(2,1)S(1)} all-to-all(bf16[32,2,64,128]{3,2,1,0:T(8,128)(2,1)S(1)} %shard_map.64), channel_id=1, replica_groups=mesh['row'=4,'col'=8] {'row','col'}, dimensions={0} | all-to-all | bytes 2097152 | tf_op jit(solution)/shard_map/all_to_all | solution.py:197
  39.5 1.8 %shard_map.65 = bf16[32,4,16,128]{3,2,1,0:T(8,128)(2,1)} custom-call(bf16[32,2,4,16,128]{4,3,2,1,0:T(8,128)(2,1)S(1)} %bitcast.9), custom_call_target="tpu_custom_call" | custom-call | flops 134217728 | bytes 1572864 | tf_op jit(solution)/shard_map/pallas_call | solution.py:165
  41.3 2.7 %all-to-all-start.1 = ((bf16[32,4,16,128]{3,2,1,0:T(8,128)(2,1)}), bf16[32,4,16,128]{3,2,1,0:T(8,128)(2,1)S(1)}, u32[]{:S(2)}, u32[]{:S(2)}) async-start(bf16[32,4,16,128]{3,2,1,0:T(8,128)(2,1)} %shard_map.65), calls=%async_computation.1 | async-start | bytes 1048576 | tf_op jit(solution)/shard_map/all_to_all | solution.py:197
  44.1 0.0 copy-done.1
  44.1 0.0 copy-done.7
  44.1 0.0 copy-start.5
  44.1 0.0 copy-start.6
  44.1 1.2 %shard_map.66.gate_ref = f32[2048,128]{1,0:T(8,128)S(1)} custom-call(f32[2048,128]{1,0:T(8,128)S(1)} %bitcast.7, f32[2,128]{1,0:T(2,128)S(1)} %copy-done.8, bf16[2,128,128]{2,1,0:T(8,128)(2,1)S(1)} %copy-done.7), custom_call_target="tpu_custom_call" | custom-call | flops 67108864 | bytes 2163712 | tf_op jit(solution)/shard_map/pallas_call | solution.py:165
  45.3 0.0 copy-start.9
  45.3 15.1 %all-to-all-done.1 = bf16[32,4,16,128]{3,2,1,0:T(8,128)(2,1)S(1)} async-done(((bf16[32,4,16,128]{3,2,1,0:T(8,128)(2,1)}), bf16[32,4,16,128]{3,2,1,0:T(8,128)(2,1)S(1)}, u32[]{:S(2)}, u32[]{:S(2)}) %all-to-all-start.1) | async-done | bytes 524320 | tf_op jit(solution)/shard_map/all_to_all | solution.py:197
  60.4 0.8 copy-done.2
  61.2 0.0 copy-done.6
  61.2 1.0 copy-done.3
  62.3 3.5 %shard_map.67 = (f32[2048,128]{1,0:T(8,128)S(1)}, bf16[32,2,64,128]{3,2,1,0:T(8,128)(2,1)S(1)}) custom-call(f32[2048,128]{1,0:T(8,128)S(1)} %bitcast.8, bf16[128,16,128]{2,1,0:T(8,128)(2,1)S(1)} %bitcast.11, f32[2048,128]{1,0:T(8,128)S(1)} %shard_map.66.gate_ref, f32[2,128]{1,0:T(2,128)S(1)} %copy-done.9, bf16[2,128,128]{2,1,0:T(8,128)(2,1)S(1)} %copy-done.6, ...), custom_call_target="tpu_custom_call" | custom-call | flops 335544320 | bytes 5048320 | tf_op jit(solution)/shard_map/pallas_call | solution.py:165
  65.7 29.5 %all_to_all.21 = bf16[32,2,64,128]{3,2,1,0:T(8,128)(2,1)S(1)} all-to-all(bf16[32,2,64,128]{3,2,1,0:T(8,128)(2,1)S(1)} %get-tuple-element.8), channel_id=1, replica_groups=mesh['row'=4,'col'=8] {'row','col'}, dimensions={0} | all-to-all | bytes 2097152 | tf_op jit(solution)/shard_map/all_to_all | solution.py:197
  95.3 1.4 %shard_map.68 = bf16[32,4,16,128]{3,2,1,0:T(8,128)(2,1)} custom-call(bf16[32,2,4,16,128]{4,3,2,1,0:T(8,128)(2,1)S(1)} %bitcast.10), custom_call_target="tpu_custom_call" | custom-call | flops 134217728 | bytes 1572864 | tf_op jit(solution)/shard_map/pallas_call | solution.py:165
  96.6 2.6 %all-to-all-start.3 = ((bf16[32,4,16,128]{3,2,1,0:T(8,128)(2,1)}), bf16[32,4,16,128]{3,2,1,0:T(8,128)(2,1)S(1)}, u32[]{:S(2)}, u32[]{:S(2)}) async-start(bf16[32,4,16,128]{3,2,1,0:T(8,128)(2,1)} %shard_map.68), calls=%async_computation.3 | async-start | bytes 1048576 | tf_op jit(solution)/shard_map/all_to_all | solution.py:197
  99.2 0.9 shard_map.69.gate_ref
  100.2 15.4 %all-to-all-done.3 = bf16[32,4,16,128]{3,2,1,0:T(8,128)(2,1)S(1)} async-done(((bf16[32,4,16,128]{3,2,1,0:T(8,128)(2,1)}), bf16[32,4,16,128]{3,2,1,0:T(8,128)(2,1)S(1)}, u32[]{:S(2)}, u32[]{:S(2)}) %all-to-all-start.3) | async-done | bytes 524320 | tf_op jit(solution)/shard_map/all_to_all | solution.py:197
  115.6 2.6 %shard_map.70 = f32[2048,128]{1,0:T(8,128)} custom-call(f32[2048,128]{1,0:T(8,128)S(1)} %get-tuple-element.7.pair_ref, bf16[128,16,128]{2,1,0:T(8,128)(2,1)S(1)} %bitcast.12, f32[2048,128]{1,0:T(8,128)S(1)} %shard_map.69.gate_ref, f32[2,128]{1,0:T(2,128)S(1)} %copy-done.9, bf16[2,128,128]{2,1,0:T(8,128)(2,1)S(1)} %copy-done.6), custom_call_target="tpu_custom_call" | custom-call | flops 67108864 | bytes 3736576 | tf_op jit(solution)/shard_map/pallas_call | solution.py:165
  (9 shorter events, 0.0 us)
Async XLA Ops:
  0.0 0.7 copy-start.8
  0.7 1.2 %copy-start = (f32[64,32,128]{2,1,0:T(8,128)S(1)}, f32[64,32,128]{2,1,0:T(8,128)}, u32[]{:S(2)}) copy-start(f32[64,32,128]{2,1,0:T(8,128)} %param.6) | copy-start | bytes 3145732
  1.9 0.9 copy-start.4
  39.5 4.6 %copy-start.1 = (f32[64,32,128]{2,1,0:T(8,128)S(1)}, f32[64,32,128]{2,1,0:T(8,128)}, u32[]{:S(2)}) copy-start(f32[64,32,128]{2,1,0:T(8,128)} %param.6) | copy-start | bytes 3145732
  41.3 2.8 %copy-start.7 = (bf16[2,128,128]{2,1,0:T(8,128)(2,1)S(1)}, bf16[2,128,128]{2,1,0:T(8,128)(2,1)}, u32[]{:S(2)}) copy-start(bf16[2,128,128]{2,1,0:T(8,128)(2,1)} %w_ref.7) | copy-start | bytes 196612
  41.3 19.1 %all-to-all-start.1 = ((bf16[32,4,16,128]{3,2,1,0:T(8,128)(2,1)}), bf16[32,4,16,128]{3,2,1,0:T(8,128)(2,1)S(1)}, u32[]{:S(2)}, u32[]{:S(2)}) async-start(bf16[32,4,16,128]{3,2,1,0:T(8,128)(2,1)} %shard_map.65), calls=%async_computation.1 | async-start | bytes 1048576 | tf_op jit(solution)/shard_map/all_to_all | solution.py:197
  44.1 17.1 %copy-start.5 = (bf16[2,128,512]{2,1,0:T(8,128)(2,1)S(1)}, bf16[2,128,512]{2,1,0:T(8,128)(2,1)}, u32[]{:S(2)}) copy-start(bf16[2,128,512]{2,1,0:T(8,128)(2,1)} %w_ref.6) | copy-start | bytes 786436
  44.1 17.1 %copy-start.6 = (bf16[2,128,128]{2,1,0:T(8,128)(2,1)S(1)}, bf16[2,128,128]{2,1,0:T(8,128)(2,1)}, u32[]{:S(2)}) copy-start(bf16[2,128,128]{2,1,0:T(8,128)(2,1)} %w_out_ref.3) | copy-start | bytes 196612
  45.3 15.9 %copy-start.9 = (f32[2,128]{1,0:T(2,128)S(1)}, f32[2,128]{1,0:T(2,128)}, u32[]{:S(2)}) copy-start(f32[2,128]{1,0:T(2,128)} %out_gain_ref.3) | copy-start | bytes 3076
  60.4 0.8 copy-start.2
  61.2 1.0 copy-start.3
  96.6 19.0 %all-to-all-start.3 = ((bf16[32,4,16,128]{3,2,1,0:T(8,128)(2,1)}), bf16[32,4,16,128]{3,2,1,0:T(8,128)(2,1)S(1)}, u32[]{:S(2)}, u32[]{:S(2)}) async-start(bf16[32,4,16,128]{3,2,1,0:T(8,128)(2,1)} %shard_map.68), calls=%async_computation.3 | async-start | bytes 1048576 | tf_op jit(solution)/shard_map/all_to_all | solution.py:197

commit v2 on v1

--- a/solution.py
+++ b/solution.py
@@ -10,7 +10,9 @@
 LANES = 128
 BF16 = jnp.bfloat16
 F32 = jnp.float32
-VMEM_LIMIT = 48 * 1024 * 1024
+VMEM_LIMIT = 16 * 1024 * 1024
+FULL_LIMIT = 63 * 1024 * 1024
+PIECES = 2
 
 
 def sigmoid(x):
@@ -56,14 +58,63 @@
         send_ref[:, side] = part.reshape(ndev, rows, LANES)
 
 
-def project_kernel(u, first, second, pair_ref, gain_ref, w_ref, send_ref, planes):
-    n1 = second * first // LANES
-    w_t = w_ref[u].T
+def parts_of(hbm, vmem, sems):
+    first, second, _ = hbm.shape
+    n1 = second * first // LANES
+    split = second // n1
+    return [
+        [
+            (hbm.at[:, pl.ds(l * n1 + g * 8, 8), :], vmem.at[:, pl.ds(l * n1 + g * 8, 8), :], sems.at[g * split + l])
+            for l in range(split)
+        ]
+        for g in range(n1 // 8)
+    ]
+
+
+def project_kernel(
+    u, pair_hbm, gain_hbm, w_hbm, send_hbm, pair_ref, gain_ref, w_ref, normed, planes, send_ref, sems, in_sems, out_sems
+):
+    first, second, chans = pair_hbm.shape
+    ndev, _, rows, _ = send_ref.shape
+    n1 = second * first // LANES
+    flat = pair_ref.reshape(first * second, chans)
+    small = [
+        pltpu.make_async_copy(gain_hbm, gain_ref, sems.at[0]),
+        pltpu.make_async_copy(w_hbm.at[u], w_ref, sems.at[1]),
+    ]
+    parts = [[pltpu.make_async_copy(*c) for c in part] for part in parts_of(pair_hbm, pair_ref, in_sems)]
+    for copy in parts[0] + small + [c for part in parts[1:] for c in part]:
+        copy.start()
+    for copy in small:
+        copy.wait()
+    w_t = w_ref[...].T
+    hidden = w_t.shape[0] // 4
     gain = gain_ref[u : u + 1, :]
-    for s in range(0, n1, 2):
-        x = jnp.concatenate([load_chunk(pair_ref, s + t, first, second) for t in range(2)], axis=0)
-        emit_branches(norm_rows(x, gain), s, n1, w_t, planes)
-    pack_branches(planes, send_ref)
+    pieces = out_sems.shape[0]
+    height, owners = hidden // pieces, ndev // pieces
+    sent = []
+    for piece in range(pieces):
+        w_piece = jnp.concatenate(
+            [w_t[k * hidden + piece * height : k * hidden + (piece + 1) * height] for k in range(4)], axis=0
+        )
+        for s in range(0, n1, 2):
+            at = slice(s * LANES, (s + 2) * LANES)
+            if piece == 0:
+                if s % 8 == 0:
+                    for copy in parts[s // 8]:
+                        copy.wait()
+                x = jnp.concatenate([load_chunk(flat, s + t, first, second) for t in range(2)], axis=0)
+                y = norm_rows(x, gain)
+                normed[at, :] = y
+            else:
+                y = normed[at, :]
+            emit_branches(y, s, n1, w_piece, planes.at[piece])
+        own = pl.ds(piece * owners, owners)
+        pack_branches(planes.at[piece], send_ref.at[own])
+        sent.append(pltpu.make_async_copy(send_ref.at[own], send_hbm.at[own], out_sems.at[piece]))
+        sent[-1].start()
+    for copy in sent:
+        copy.wait()
 
 
 def gate_kernel(u, first, second, ordered, pair_ref, gain_ref, w_ref, gate_ref):
@@ -146,10 +197,16 @@
 
 
 def last_kernel(
-    first, second, pair_ref, summed_ref, gate_ref, out_gain_ref, w_out_ref, updated_ref, normal
+    pair_ref, summed_ref, gate_ref, out_gain_ref, w_out_ref, updated_hbm, normal, updated_ref, sems
 ):
+    first, second, chans = updated_hbm.shape
     n1 = second * first // LANES
     hidden = w_out_ref.shape[1]
+    flat = updated_ref.reshape(first * second, chans)
+    parts = [
+        [pltpu.make_async_copy(vmem, hbm, sem) for hbm, vmem, sem in part]
+        for part in parts_of(updated_hbm, updated_ref, sems)
+    ]
     norm_planes(summed_ref, normal)
     gain_cols = jnp.broadcast_to(out_gain_ref[1:2, :], (LANES, hidden)).T
     for s in range(0, n1, 2):
@@ -157,20 +214,26 @@
         at = slice(s * LANES, (s + 2) * LANES)
         z = pair_ref[at, :] + gate_ref[at, :] * out
         for t in range(2):
-            store_chunk(updated_ref, s + t, first, second, z[t * LANES : (t + 1) * LANES])
-
-
-def call(kernel, outs, scratch, flops, *args):
+            store_chunk(flat, s + t, first, second, z[t * LANES : (t + 1) * LANES])
+        if s % 8 == 6:
+            for copy in parts[s // 8]:
+                copy.start()
+    for part in parts:
+        for copy in part:
+            copy.wait()
+
+
+def call(kernel, outs, scratch, flops, *args, ins=pltpu.VMEM, spaces=None, limit=VMEM_LIMIT):
     moved = sum(a.size * a.dtype.itemsize for a in args) + sum(o.size * o.dtype.itemsize for o in outs)
+    out_specs = [pl.BlockSpec(memory_space=space) for space in spaces or [pltpu.VMEM] * len(outs)]
+    several = len(outs) > 1
     return pl.pallas_call(
         kernel,
-        out_shape=outs if len(outs) > 1 else outs[0],
-        in_specs=[pl.BlockSpec(memory_space=pltpu.VMEM)] * len(args),
-        out_specs=[pl.BlockSpec(memory_space=pltpu.VMEM)] * len(outs)
-        if len(outs) > 1
-        else pl.BlockSpec(memory_space=pltpu.VMEM),
+        out_shape=outs if several else outs[0],
+        in_specs=[pl.BlockSpec(memory_space=ins)] * len(args),
+        out_specs=out_specs if several else out_specs[0],
         scratch_shapes=scratch,
-        compiler_params=pltpu.CompilerParams(vmem_limit_bytes=VMEM_LIMIT),
+        compiler_params=pltpu.CompilerParams(vmem_limit_bytes=limit),
         cost_estimate=pl.CostEstimate(flops=flops, bytes_accessed=moved, transcendentals=0),
     )(*args)
 
@@ -206,19 +269,35 @@
         )
         return exchange(out).reshape(hidden, n1, LANES)
 
+    slabs = pltpu.SemaphoreType.DMA((second // 8,))
+    staged = [
+        pltpu.VMEM(pair.shape, F32),
+        pltpu.VMEM(norm_in_gain.shape, F32),
+        pltpu.VMEM(w_proj.shape[1:], BF16),
+        pltpu.VMEM((count, chans), BF16),
+        pltpu.VMEM((PIECES, 2 * hidden * n1 // PIECES, LANES), F32),
+        pltpu.VMEM(send_shape.shape, BF16),
+        pltpu.SemaphoreType.DMA((2,)),
+        slabs,
+        pltpu.SemaphoreType.DMA((PIECES,)),
+    ]
     send = call(
-        functools.partial(project_kernel, 0, first, second),
-        [send_shape], [planes], proj_flops, flat, norm_in_gain, w_proj,
+        functools.partial(project_kernel, 0),
+        [send_shape], staged, proj_flops, pair, norm_in_gain, w_proj,
+        ins=pltpu.HBM, spaces=[pltpu.HBM], limit=FULL_LIMIT,
     )
     recv = exchange(send)
     gate = call(
         functools.partial(gate_kernel, 0, first, second, False),
         [flat_shape], [], gate_flops, flat, norm_in_gain, w_gate,
     )
+    recv, gate = lax.optimization_barrier((recv, gate))
     summed = triangle(recv, 0)
     middle, send = call(
         functools.partial(middle_kernel, first, second),
-        [flat_shape, send_shape], [normal, planes], proj_flops + gate_flops,
+        [flat_shape, send_shape],
+        [normal, planes],
+        proj_flops + gate_flops,
         flat, summed, gate, norm_out_gain, w_out, norm_in_gain, w_proj,
     )
     recv = exchange(send)
@@ -226,13 +305,13 @@
         functools.partial(gate_kernel, 1, first, second, True),
         [flat_shape], [], gate_flops, middle, norm_in_gain, w_gate,
     )
+    recv, gate = lax.optimization_barrier((recv, gate))
     summed = triangle(recv, 1)
-    updated = call(
-        functools.partial(last_kernel, first, second),
-        [flat_shape], [normal], gate_flops,
-        middle, summed, gate, norm_out_gain, w_out,
-    )
-    return updated.reshape(pair.shape)
+    return call(
+        last_kernel,
+        [jax.ShapeDtypeStruct(pair.shape, F32)], [normal, pltpu.VMEM(pair.shape, F32), slabs], gate_flops,
+        middle, summed, gate, norm_out_gain, w_out, spaces=[pltpu.HBM],
+    )
 
 
 def solution(mesh):

time: 119 us -> 116 us (0.975)
  blocking collectives: 64.2 us -> 36.7 us
  waiting for transfers between devices: 30.5 us -> 52.3 us
  starting transfers between devices: 5.34 us -> 9.95 us
  local copies, waits for them, and re-layouts: 4.71 us -> 2.32 us
    all_to_all x2, blocking collectives: 64.2 us -> 36.7 us  [exchange(): return lax.all_to_all(block, axes, 0, 0, tiled=True)]
    all_to_all x2, waiting for transfers between devices: 30.5 us -> 52.3 us  [exchange(): return lax.all_to_all(block, axes, 0, 0, tiled=True)]
    all_to_all x2, starting transfers between devices: 5.34 us -> 9.95 us  [exchange(): return lax.all_to_all(block, axes, 0, 0, tiled=True)]
    unnamed x20 -> x14, local copies, waits for them, and re-layouts: 4.71 us -> 2.32 us
where the time goes in v2:
time: 116 us; the launch traced here: 115 us
  waiting for transfers between devices  52.3 us (45%)
  blocking collectives  36.7 us (32%)
  Pallas kernels  14 us (12%)
  starting transfers between devices  9.95 us (9%)
  local copies, waits for them, and re-layouts  2.32 us (2%)
    all_to_all x2, waiting for transfers between devices, exchange(): return lax.all_to_all(block, axes, 0, 0, tiled=True)  52.3 us
    all_to_all x2, blocking collectives, exchange(): return lax.all_to_all(block, axes, 0, 0, tiled=True)  36.7 us
    pallas_call x7, Pallas kernels, call(): pl.pallas_call(kernel, out_shape=outs if several else outs[0], in_specs=[...  14 us
    all_to_all x2, starting transfers between devices, exchange(): return lax.all_to_all(block, axes, 0, 0, tiled=True)  9.95 us
  transfers between devices with their start and end apart: 2, of which 2 were waited for; matrix products, arithmetic and copies ran while one was open for 0% of the time, Pallas kernels for 2%

profile of v2, /device:TPU:0, one launch (start us, length us, event | category | flops | bytes accessed | tf_op | source)
XLA Modules:
  0.0 115.4 jit_solution(3832110664317393033)
XLA Ops:
  0.0 4.2 %shard_map.64 = bf16[32,2,64,128]{3,2,1,0:T(8,128)(2,1)} custom-call(f32[64,32,128]{2,1,0:T(8,128)} %pair_hbm.1, f32[2,128]{1,0:T(2,128)} %gain_ref.5, bf16[2,128,512]{2,1,0:T(8,128)(2,1)} %w_ref.4), custom_call_target="tpu_custom_call" | custom-call | flops 268435456 | bytes 2360320 | tf_op jit(solution)/shard_map/pallas_call | solution.py:230
  4.3 0.0 copy-start
  4.3 0.0 copy-start.4
  4.3 7.3 %all-to-all-start = ((bf16[32,2,64,128]{3,2,1,0:T(8,128)(2,1)}), bf16[32,2,64,128]{3,2,1,0:T(8,128)(2,1)S(1)}, u32[]{:S(2)}, u32[]{:S(2)}) async-start(bf16[32,2,64,128]{3,2,1,0:T(8,128)(2,1)} %shard_map.64), calls=%async_computation | async-start | bytes 2097152 | tf_op jit(solution)/shard_map/all_to_all | solution.py:260
  11.6 0.0 copy-start.5
  11.6 0.0 copy-done
  11.6 0.7 copy-done.5
  12.3 1.2 %shard_map.65.gate_ref = f32[2048,128]{1,0:T(8,128)S(1)} custom-call(f32[2048,128]{1,0:T(8,128)S(1)} %bitcast.5, f32[2,128]{1,0:T(2,128)S(1)} %copy-done.5, bf16[2,128,128]{2,1,0:T(8,128)(2,1)S(1)} %copy-done.4), custom_call_target="tpu_custom_call" | custom-call | flops 67108864 | bytes 2163712 | tf_op jit(solution)/shard_map/pallas_call | solution.py:230
  13.5 25.7 %all-to-all-done = bf16[32,2,64,128]{3,2,1,0:T(8,128)(2,1)S(1)} async-done(((bf16[32,2,64,128]{3,2,1,0:T(8,128)(2,1)}), bf16[32,2,64,128]{3,2,1,0:T(8,128)(2,1)S(1)}, u32[]{:S(2)}, u32[]{:S(2)}) %all-to-all-start) | async-done | bytes 1048608 | tf_op jit(solution)/shard_map/all_to_all | solution.py:260
  39.2 1.0 shard_map.66
  40.2 0.0 copy-start.1
  40.2 0.0 copy-start.3
  40.2 18.4 %all_to_all.20 = bf16[32,4,16,128]{3,2,1,0:T(8,128)(2,1)S(1)} all-to-all(bf16[32,4,16,128]{3,2,1,0:T(8,128)(2,1)S(1)} %shard_map.66), channel_id=1, replica_groups=mesh['row'=4,'col'=8] {'row','col'}, dimensions={0} | all-to-all | bytes 1048576 | tf_op jit(solution)/shard_map/all_to_all | solution.py:260
  58.6 0.0 copy-done.1
  58.6 0.7 copy-done.6
  59.3 3.5 %shard_map.67 = (f32[2048,128]{1,0:T(8,128)S(1)}, bf16[32,2,64,128]{3,2,1,0:T(8,128)(2,1)S(1)}) custom-call(f32[2048,128]{1,0:T(8,128)S(1)} %bitcast.6, bf16[128,16,128]{2,1,0:T(8,128)(2,1)S(1)} %bitcast.9, f32[2048,128]{1,0:T(8,128)S(1)} %shard_map.65.gate_ref, f32[2,128]{1,0:T(2,128)S(1)} %copy-done.6, bf16[2,128,128]{2,1,0:T(8,128)(2,1)S(1)} %copy-done.3, ...), custom_call_target="tpu_custom_call" | custom-call | flops 335544320 | bytes 5048320 | tf_op jit(solution)/shard_map/pallas_call | solution.py:230
  62.8 0.0 copy-start.2
  62.8 1.0 copy-done.2
  63.8 2.6 %all-to-all-start.2 = ((bf16[32,2,64,128]{3,2,1,0:T(8,128)(2,1)}), bf16[32,2,64,128]{3,2,1,0:T(8,128)(2,1)S(1)}, u32[]{:S(2)}, u32[]{:S(2)}) async-start(bf16[32,2,64,128]{3,2,1,0:T(8,128)(2,1)} %copy-done.2), calls=%async_computation.2 | async-start | bytes 2097152 | tf_op jit(solution)/shard_map/all_to_all | solution.py:260
  66.4 0.9 shard_map.68.gate_ref
  67.3 26.6 %all-to-all-done.2 = bf16[32,2,64,128]{3,2,1,0:T(8,128)(2,1)S(1)} async-done(((bf16[32,2,64,128]{3,2,1,0:T(8,128)(2,1)}), bf16[32,2,64,128]{3,2,1,0:T(8,128)(2,1)S(1)}, u32[]{:S(2)}, u32[]{:S(2)}) %all-to-all-start.2) | async-done | bytes 1048608 | tf_op jit(solution)/shard_map/all_to_all | solution.py:260
  94.0 0.6 shard_map.69
  94.6 18.3 %all_to_all.21 = bf16[32,4,16,128]{3,2,1,0:T(8,128)(2,1)S(1)} all-to-all(bf16[32,4,16,128]{3,2,1,0:T(8,128)(2,1)S(1)} %shard_map.69), channel_id=1, replica_groups=mesh['row'=4,'col'=8] {'row','col'}, dimensions={0} | all-to-all | bytes 1048576 | tf_op jit(solution)/shard_map/all_to_all | solution.py:260
  112.9 2.5 %shard_map.70 = f32[64,32,128]{2,1,0:T(8,128)} custom-call(f32[2048,128]{1,0:T(8,128)S(1)} %get-tuple-element.13.pair_ref, bf16[128,16,128]{2,1,0:T(8,128)(2,1)S(1)} %bitcast.10, f32[2048,128]{1,0:T(8,128)S(1)} %shard_map.68.gate_ref, f32[2,128]{1,0:T(2,128)S(1)} %copy-done.6, bf16[2,128,128]{2,1,0:T(8,128)(2,1)S(1)} %copy-done.3), custom_call_target="tpu_custom_call" | custom-call | flops 67108864 | bytes 3736576 | tf_op jit(solution)/shard_map/pallas_call | solution.py:230
  (3 shorter events, 0.0 us)
Async XLA Ops:
  4.3 7.4 %copy-start = (f32[64,32,128]{2,1,0:T(8,128)S(1)}, f32[64,32,128]{2,1,0:T(8,128)}, u32[]{:S(2)}) copy-start(f32[64,32,128]{2,1,0:T(8,128)} %pair_hbm.1) | copy-start | bytes 3145732
  4.3 7.3 %copy-start.4 = (bf16[2,128,128]{2,1,0:T(8,128)(2,1)S(1)}, bf16[2,128,128]{2,1,0:T(8,128)(2,1)}, u32[]{:S(2)}) copy-start(bf16[2,128,128]{2,1,0:T(8,128)(2,1)} %w_ref.5) | copy-start | bytes 196612
  4.3 34.9 %all-to-all-start = ((bf16[32,2,64,128]{3,2,1,0:T(8,128)(2,1)}), bf16[32,2,64,128]{3,2,1,0:T(8,128)(2,1)S(1)}, u32[]{:S(2)}, u32[]{:S(2)}) async-start(bf16[32,2,64,128]{3,2,1,0:T(8,128)(2,1)} %shard_map.64), calls=%async_computation | async-start | bytes 2097152 | tf_op jit(solution)/shard_map/all_to_all | solution.py:260
  11.6 0.7 copy-start.5
  40.2 18.4 %copy-start.1 = (bf16[2,128,512]{2,1,0:T(8,128)(2,1)S(1)}, bf16[2,128,512]{2,1,0:T(8,128)(2,1)}, u32[]{:S(2)}) copy-start(bf16[2,128,512]{2,1,0:T(8,128)(2,1)} %w_ref.4) | copy-start | bytes 786436
  40.2 18.4 %copy-start.3 = (bf16[2,128,128]{2,1,0:T(8,128)(2,1)S(1)}, bf16[2,128,128]{2,1,0:T(8,128)(2,1)}, u32[]{:S(2)}) copy-start(bf16[2,128,128]{2,1,0:T(8,128)(2,1)} %w_out_ref.3) | copy-start | bytes 196612
  58.6 0.7 copy-start.6
  62.8 1.0 copy-start.2
  63.8 30.2 %all-to-all-start.2 = ((bf16[32,2,64,128]{3,2,1,0:T(8,128)(2,1)}), bf16[32,2,64,128]{3,2,1,0:T(8,128)(2,1)S(1)}, u32[]{:S(2)}, u32[]{:S(2)}) async-start(bf16[32,2,64,128]{3,2,1,0:T(8,128)(2,1)} %copy-done.2), calls=%async_computation.2 | async-start | bytes 2097152 | tf_op jit(solution)/shard_map/all_to_all | solution.py:260

commit v3 on v1

v3 whole, which is shorter than its diff:
```python
import functools

import jax
import jax.numpy as jnp
from jax import lax
from jax.experimental import pallas as pl
from jax.experimental.pallas import tpu as pltpu
from jax.sharding import PartitionSpec as P

LANES = 128
BF16 = jnp.bfloat16
F32 = jnp.float32
VMEM_LIMIT = 16 * 1024 * 1024
FULL_LIMIT = 63 * 1024 * 1024


def sigmoid(x):
    return 0.5 * jnp.tanh(0.5 * x) + 0.5


def norm_rows(x, gain):
    center = x - jnp.mean(x, axis=-1, keepdims=True)
    spread = jnp.mean(center * center, axis=-1, keepdims=True)
    return (center * lax.rsqrt(spread + 1e-05) * gain).astype(BF16)


def block_rows(first, second):
    split = LANES // first
    n1 = second // split
    return [l * n1 + s for s in range(n1) for l in range(split)]


def load_block(padded, first, second):
    rows = block_rows(first, second)
    return jnp.concatenate([padded[pl.ds(row, first, stride=second + 1), :] for row in rows], axis=0)


def block_copies(hbm, padded, sems):
    first, second, _ = hbm.shape
    return [(hbm.at[f], padded.at[pl.ds(f * (second + 1), second), :], sems.at[f]) for f in range(first)]


def emit_branches(normed, w_t, planes, send_ref, done=None):
    ndev, _, rows, _ = send_ref.shape
    hidden = w_t.shape[0] // 4
    depth = hidden // ndev
    n1 = rows // depth
    pad = n1 + 1
    proj = lax.dot_general(w_t, normed, (((1,), (1,)), ((), ())), preferred_element_type=F32)
    for side in range(2):
        at = 2 * side * hidden
        value = sigmoid(proj[at : at + hidden]) * proj[at + hidden : at + 2 * hidden]
        for s in range(n1):
            planes[pl.ds(side * hidden * pad + s, hidden, stride=pad), :] = value[:, s * LANES : (s + 1) * LANES]
    for device in range(ndev):
        for side in range(2):
            for h in range(depth):
                at = (side * hidden + device * depth + h) * pad
                send_ref[device, side, h * n1 : (h + 1) * n1, :] = planes[at : at + n1, :].astype(BF16)
        if done is not None:
            done(device)


def project_kernel(
    u, pair_hbm, gain_hbm, w_hbm, send_hbm, padded, gain_ref, w_ref, planes, send_ref, in_sems, out_sems
):
    first, second, _ = pair_hbm.shape
    ndev = send_ref.shape[0]
    copies = [pltpu.make_async_copy(*c) for c in block_copies(pair_hbm, padded, in_sems)]
    copies.append(pltpu.make_async_copy(gain_hbm, gain_ref, in_sems.at[first]))
    copies.append(pltpu.make_async_copy(w_hbm.at[u], w_ref, in_sems.at[first + 1]))
    for copy in copies:
        copy.start()
    for copy in copies:
        copy.wait()
    half = ndev // 2
    sent = []

    def send(device):
        if (device + 1) % half == 0:
            own = pl.ds(device + 1 - half, half)
            copy = pltpu.make_async_copy(send_ref.at[own], send_hbm.at[own], out_sems.at[len(sent)])
            copy.start()
            sent.append(copy)

    normed = norm_rows(load_block(padded, first, second), gain_ref[u : u + 1, :])
    emit_branches(normed, w_ref[...].T, planes, send_ref, send)
    for copy in sent:
        copy.wait()


def prepare_kernel(
    pair_ref, gain_ref, w_gate_ref, w_ref, out_gain_ref,
    ordered_ref, gate_ref, w_t_ref, gain_cols_ref, padded,
):
    first, second, _ = pair_ref.shape
    for f in range(first):
        padded[f * (second + 1) : f * (second + 1) + second, :] = pair_ref[f]
    x = load_block(padded, first, second)
    ordered_ref[...] = x
    normed = norm_rows(x, gain_ref[0:1, :])
    gate_ref[...] = sigmoid(jnp.dot(normed, w_gate_ref[0], preferred_element_type=F32))
    w_t_ref[...] = w_ref[1].T
    for u in range(2):
        wide = (LANES, out_gain_ref.shape[1])
        gain_cols_ref[u] = jnp.broadcast_to(out_gain_ref[u : u + 1, :], wide).T


def triangle_kernel(contract, rows, cols, first, recv_ref, out_ref, left, right):
    ndev, _, depth, n1, _ = recv_ref.shape
    split = LANES // first
    for h in range(depth):
        for side, dense in ((0, left), (1, right)):
            for c in range(cols):
                for l in range(split):
                    at = (c * split + l) * n1
                    dense[at : at + n1, :] = jnp.concatenate(
                        [
                            recv_ref[r * cols + c, side, h, :, l * first : (l + 1) * first]
                            for r in range(rows)
                        ],
                        axis=1,
                    )
        summed = lax.dot_general(
            right[...], left[...], (((contract,), (contract,)), ((), ())), preferred_element_type=F32
        ).astype(BF16)
        for r in range(rows):
            for c in range(cols):
                out_ref[r * cols + c, h] = jnp.concatenate(
                    [
                        summed[(c * split + l) * n1 : (c * split + l + 1) * n1, r * first : (r + 1) * first]
                        for l in range(split)
                    ],
                    axis=1,
                )


def output(summed_ref, gain_cols, w, normal):
    hidden, n1, _ = summed_ref.shape
    pad = n1 + 1
    x = summed_ref[...].astype(F32)
    center = x - jnp.mean(x, axis=0, keepdims=True)
    spread = jnp.mean(center * center, axis=0, keepdims=True)
    scaled = center * lax.rsqrt(spread + 1e-05)
    for h in range(hidden):
        normal[h * pad : h * pad + n1, :] = scaled[h]
    mixed = jnp.concatenate(
        [(normal[pl.ds(s, hidden, stride=pad), :] * gain_cols).astype(BF16) for s in range(n1)], axis=1
    )
    return lax.dot_general(mixed, w, (((0,), (0,)), ((), ())), preferred_element_type=F32)


def middle_kernel(
    ordered_ref, summed_ref, gate_ref, gain_cols_ref, w_out_ref, gain_ref, w_t_ref, w_gate_ref,
    first_ref, gate_out_ref, send_ref, normal, planes,
):
    z = ordered_ref[...] + gate_ref[...] * output(summed_ref, gain_cols_ref[0], w_out_ref[0], normal)
    first_ref[...] = z
    normed = norm_rows(z, gain_ref[1:2, :])
    emit_branches(normed, w_t_ref[...], planes, send_ref)
    gate_out_ref[...] = sigmoid(jnp.dot(normed, w_gate_ref[1], preferred_element_type=F32))


def last_kernel(
    first_ref, summed_ref, gate_ref, gain_cols_ref, w_out_ref, updated_hbm, normal, padded, sems
):
    first, second, _ = updated_hbm.shape
    z = first_ref[...] + gate_ref[...] * output(summed_ref, gain_cols_ref[1], w_out_ref[1], normal)
    for i, row in enumerate(block_rows(first, second)):
        padded[pl.ds(row, first, stride=second + 1), :] = z[i * first : (i + 1) * first]
    copies = [
        pltpu.make_async_copy(vmem, hbm, sem) for hbm, vmem, sem in block_copies(updated_hbm, padded, sems)
    ]
    for copy in copies:
        copy.start()
    for copy in copies:
        copy.wait()


def call(kernel, outs, scratch, flops, *args, ins=pltpu.VMEM, spaces=None, limit=VMEM_LIMIT):
    moved = sum(a.size * a.dtype.itemsize for a in args) + sum(o.size * o.dtype.itemsize for o in outs)
    out_specs = [pl.BlockSpec(memory_space=space) for space in spaces or [pltpu.VMEM] * len(outs)]
    several = len(outs) > 1
    return pl.pallas_call(
        kernel,
        out_shape=outs if several else outs[0],
        in_specs=[pl.BlockSpec(memory_space=ins)] * len(args),
        out_specs=out_specs if several else out_specs[0],
        scratch_shapes=scratch,
        compiler_params=pltpu.CompilerParams(vmem_limit_bytes=limit),
        cost_estimate=pl.CostEstimate(flops=flops, bytes_accessed=moved, transcendentals=0),
    )(*args)


def body(rows, cols, pair, norm_in_gain, w_proj, w_gate, norm_out_gain, w_out):
    first, second, chans = pair.shape
    hidden = w_out.shape[1]
    ndev = rows * cols
    depth = hidden // ndev
    count = first * second
    n1 = count // LANES
    total = rows * first
    axes = ("row", "col")

    send_shape = jax.ShapeDtypeStruct((ndev, 2, depth * n1, LANES), BF16)
    flat_shape = jax.ShapeDtypeStruct((count, chans), F32)
    planes = pltpu.VMEM((2 * hidden * (n1 + 1), LANES), F32)
    normal = pltpu.VMEM((hidden * (n1 + 1), LANES), F32)
    padded = pltpu.VMEM((first * (second + 1), chans), F32)
    proj_flops = 2 * count * chans * 4 * hidden
    gate_flops = 2 * count * chans * chans

    def exchange(block):
        return lax.all_to_all(block, axes, 0, 0, tiled=True)

    def triangle(recv, contract):
        out = call(
            functools.partial(triangle_kernel, contract, rows, cols, first),
            [jax.ShapeDtypeStruct((ndev, depth, n1, LANES), BF16)],
            [pltpu.VMEM((cols * second, total), BF16)] * 2,
            2 * depth * total**3,
            recv.reshape(ndev, 2, depth, n1, LANES),
        )
        return exchange(out).reshape(hidden, n1, LANES)

    send = call(
        functools.partial(project_kernel, 0),
        [send_shape],
        [
            padded,
            pltpu.VMEM(norm_in_gain.shape, F32),
            pltpu.VMEM(w_proj.shape[1:], BF16),
            planes,
            pltpu.VMEM(send_shape.shape, BF16),
            pltpu.SemaphoreType.DMA((first + 2,)),
            pltpu.SemaphoreType.DMA((2,)),
        ],
        proj_flops, pair, norm_in_gain, w_proj,
        ins=pltpu.HBM, spaces=[pltpu.HBM], limit=FULL_LIMIT,
    )
    recv = exchange(send)
    prepared = call(
        prepare_kernel,
        [
            flat_shape,
            flat_shape,
            jax.ShapeDtypeStruct((4 * hidden, chans), BF16),
            jax.ShapeDtypeStruct((2, hidden, LANES), F32),
        ],
        [padded], gate_flops,
        pair, norm_in_gain, w_gate, w_proj, norm_out_gain,
    )
    recv, (ordered, gate, w_t, gain_cols) = lax.optimization_barrier((recv, prepared))
    summed = triangle(recv, 0)
    middle, gate, send = call(
        middle_kernel,
        [flat_shape, flat_shape, send_shape], [normal, planes], proj_flops + 2 * gate_flops,
        ordered, summed, gate, gain_cols, w_out, norm_in_gain, w_t, w_gate,
    )
    summed = triangle(exchange(send), 1)
    return call(
        last_kernel,
        [jax.ShapeDtypeStruct(pair.shape, F32)], [normal, padded, pltpu.SemaphoreType.DMA((first,))], gate_flops,
        middle, summed, gate, gain_cols, w_out, spaces=[pltpu.HBM],
    )


def solution(mesh):
    placed = (P("row", "col", None), P(), P(), P(), P(), P())
    return jax.shard_map(
        functools.partial(body, mesh.shape["row"], mesh.shape["col"]),
        mesh=mesh,
        in_specs=placed,
        out_specs=P("row", "col", None),
        check_vma=False,
    )
```

time: 119 us -> 112 us (0.941)
  waiting for transfers between devices: 30.5 us -> 24.2 us
  Pallas kernels: 13.3 us -> 10.8 us
  blocking collectives: 64.2 us -> 66.4 us
  local copies, waits for them, and re-layouts: 4.71 us -> 2.51 us
  starting transfers between devices: 5.34 us -> 7.3 us
    all_to_all x2 -> x1, waiting for transfers between devices: 30.5 us -> 24.2 us  [exchange(): return lax.all_to_all(block, axes, 0, 0, tiled=True)]
    pallas_call x7 -> x6, Pallas kernels: 13.3 us -> 10.8 us  [call(): pl.pallas_call(kernel, out_shape=outs if several else outs[0], in_specs=[...]
    unnamed x20 -> x22, local copies, waits for them, and re-layouts: 4.71 us -> 2.51 us
    all_to_all x2 -> x3, blocking collectives: 64.2 us -> 66.4 us  [exchange(): return lax.all_to_all(block, axes, 0, 0, tiled=True)]
    all_to_all x2 -> x1, starting transfers between devices: 5.34 us -> 7.3 us  [exchange(): return lax.all_to_all(block, axes, 0, 0, tiled=True)]
  transfers between devices with their start and end apart: 2 -> 1, of which waited for: 2 -> 1; matrix products, arithmetic and copies ran while one was open for 0% -> 0% of each run, Pallas kernels for 2% -> 1%
where the time goes in v3:
time: 112 us; the launch traced here: 111 us
  blocking collectives  66.4 us (59%)
  waiting for transfers between devices  24.2 us (22%)
  Pallas kernels  10.8 us (10%)
  starting transfers between devices  7.3 us (7%)
  local copies, waits for them, and re-layouts  2.51 us (2%)
    all_to_all x3, blocking collectives, exchange(): return lax.all_to_all(block, axes, 0, 0, tiled=True)  66.4 us
    all_to_all x1, waiting for transfers between devices, exchange(): return lax.all_to_all(block, axes, 0, 0, tiled=True)  24.2 us
    pallas_call x6, Pallas kernels, call(): pl.pallas_call(kernel, out_shape=outs if several else outs[0], in_specs=[...  10.8 us
    all_to_all x1, starting transfers between devices, exchange(): return lax.all_to_all(block, axes, 0, 0, tiled=True)  7.3 us
    unnamed x22, local copies, waits for them, and re-layouts  2.51 us
  transfers between devices with their start and end apart: 1, of which 1 were waited for; matrix products, arithmetic and copies ran while one was open for 0% of the time, Pallas kernels for 1%

profile of v3, /device:TPU:0, one launch (start us, length us, event | category | flops | bytes accessed | tf_op | source)
XLA Modules:
  0.0 111.3 jit_solution(16295414335123553521)
XLA Ops:
  0.0 4.1 %shard_map.64 = bf16[32,2,64,128]{3,2,1,0:T(8,128)(2,1)} custom-call(f32[64,32,128]{2,1,0:T(8,128)} %pair_ref.1, f32[2,128]{1,0:T(2,128)} %gain_ref.3, bf16[2,128,512]{2,1,0:T(8,128)(2,1)} %w_ref.1), custom_call_target="tpu_custom_call" | custom-call | flops 268435456 | bytes 2360320 | tf_op jit(solution)/shard_map/pallas_call | solution.py:184
  4.1 0.0 copy-start
  4.1 0.0 copy-start.3
  4.2 0.0 copy-start.9
  4.2 0.0 copy-start.10
  4.2 7.3 %all-to-all-start = ((bf16[32,2,64,128]{3,2,1,0:T(8,128)(2,1)}), bf16[32,2,64,128]{3,2,1,0:T(8,128)(2,1)S(1)}, u32[]{:S(2)}, u32[]{:S(2)}) async-start(bf16[32,2,64,128]{3,2,1,0:T(8,128)(2,1)} %shard_map.64), calls=%async_computation | async-start | bytes 2097152 | tf_op jit(solution)/shard_map/all_to_all | solution.py:214
  11.5 0.0 copy-done
  11.5 0.0 copy-done.3
  11.5 0.0 copy-done.9
  11.5 0.0 copy-start.5
  11.5 0.8 copy-done.5
  12.4 0.9 shard_map.65
  13.3 1.0 copy-done.1
  14.3 0.6 copy-done.7
  14.9 24.2 %all-to-all-done = bf16[32,2,64,128]{3,2,1,0:T(8,128)(2,1)S(1)} async-done(((bf16[32,2,64,128]{3,2,1,0:T(8,128)(2,1)}), bf16[32,2,64,128]{3,2,1,0:T(8,128)(2,1)S(1)}, u32[]{:S(2)}, u32[]{:S(2)}) %all-to-all-start) | async-done | bytes 1048608 | tf_op jit(solution)/shard_map/all_to_all | solution.py:214
  39.1 1.0 shard_map.66
  40.1 0.0 copy-start.4
  40.1 0.0 copy-start.6
  40.1 18.4 %all_to_all.20 = bf16[32,4,16,128]{3,2,1,0:T(8,128)(2,1)S(1)} all-to-all(bf16[32,4,16,128]{3,2,1,0:T(8,128)(2,1)S(1)} %shard_map.66), channel_id=1, replica_groups=mesh['row'=4,'col'=8] {'row','col'}, dimensions={0} | all-to-all | bytes 1048576 | tf_op jit(solution)/shard_map/all_to_all | solution.py:214
  58.5 1.9 %shard_map.67 = (f32[2048,128]{1,0:T(8,128)S(1)}, f32[2048,128]{1,0:T(8,128)S(1)}, bf16[32,2,64,128]{3,2,1,0:T(8,128)(2,1)S(1)}) custom-call(f32[2048,128]{1,0:T(8,128)S(1)} %get-tuple-element.21.ordered_ref, bf16[128,16,128]{2,1,0:T(8,128)(2,1)S(1)} %bitcast.6, f32[2048,128]{1,0:T(8,128)S(1)} %copy-done.2, ...), custom_call_target="tpu_custom_call" | custom-call | flops 402653184 | bytes 6161408 | tf_op jit(solution)/shard_map/pallas_call | solution.py:184
  60.5 29.6 %all_to_all.21 = bf16[32,2,64,128]{3,2,1,0:T(8,128)(2,1)S(1)} all-to-all(bf16[32,2,64,128]{3,2,1,0:T(8,128)(2,1)S(1)} %get-tuple-element.27), channel_id=1, replica_groups=mesh['row'=4,'col'=8] {'row','col'}, dimensions={0} | all-to-all | bytes 2097152 | tf_op jit(solution)/shard_map/all_to_all | solution.py:214
  90.1 0.6 shard_map.68
  90.7 18.4 %all_to_all.22 = bf16[32,4,16,128]{3,2,1,0:T(8,128)(2,1)S(1)} all-to-all(bf16[32,4,16,128]{3,2,1,0:T(8,128)(2,1)S(1)} %shard_map.68), channel_id=1, replica_groups=mesh['row'=4,'col'=8] {'row','col'}, dimensions={0} | all-to-all | bytes 1048576 | tf_op jit(solution)/shard_map/all_to_all | solution.py:214
  109.0 2.2 %shard_map.69 = f32[64,32,128]{2,1,0:T(8,128)} custom-call(f32[2048,128]{1,0:T(8,128)S(1)} %get-tuple-element.26.first_ref, bf16[128,16,128]{2,1,0:T(8,128)(2,1)S(1)} %bitcast.7, f32[2048,128]{1,0:T(8,128)S(1)} %get-tuple-element.28.gate_ref, f32[2,128,128]{2,1,0:T(8,128)S(1)} %get-tuple-element.24.gain_cols_ref, bf16[2,128,128]{2,1,0:T(8,128)(2,1)S(1)} %copy-done.4), custom_call_target="tpu_custom_call" | custom-call | flops 67108864 | bytes 3866624 | tf_op jit(solution)/shard_map/pallas_call | solution.py:184
  (9 shorter events, 0.0 us)
Async XLA Ops:
  4.1 7.4 %copy-start = (f32[64,32,128]{2,1,0:T(8,128)S(1)}, f32[64,32,128]{2,1,0:T(8,128)}, u32[]{:S(2)}) copy-start(f32[64,32,128]{2,1,0:T(8,128)} %pair_ref.1) | copy-start | bytes 3145732
  4.1 7.4 %copy-start.3 = (bf16[2,128,512]{2,1,0:T(8,128)(2,1)S(1)}, bf16[2,128,512]{2,1,0:T(8,128)(2,1)}, u32[]{:S(2)}) copy-start(bf16[2,128,512]{2,1,0:T(8,128)(2,1)} %w_ref.1) | copy-start | bytes 786436
  4.2 7.4 %copy-start.9 = (f32[2,128]{1,0:T(2,128)S(1)}, f32[2,128]{1,0:T(2,128)}, u32[]{:S(2)}) copy-start(f32[2,128]{1,0:T(2,128)} %gain_ref.3) | copy-start | bytes 3076
  4.2 7.4 %copy-start.10 = (f32[2,128]{1,0:T(2,128)S(1)}, f32[2,128]{1,0:T(2,128)}, u32[]{:S(2)}) copy-start(f32[2,128]{1,0:T(2,128)} %out_gain_ref.1) | copy-start | bytes 3076
  4.2 34.9 %all-to-all-start = ((bf16[32,2,64,128]{3,2,1,0:T(8,128)(2,1)}), bf16[32,2,64,128]{3,2,1,0:T(8,128)(2,1)S(1)}, u32[]{:S(2)}, u32[]{:S(2)}) async-start(bf16[32,2,64,128]{3,2,1,0:T(8,128)(2,1)} %shard_map.64), calls=%async_computation | async-start | bytes 2097152 | tf_op jit(solution)/shard_map/all_to_all | solution.py:214
  11.5 0.8 copy-start.5
  13.3 1.0 copy-start.1
  14.3 0.7 copy-start.7
  39.1 19.4 %copy-start.2 = (f32[2048,128]{1,0:T(8,128)S(1)}, f32[2048,128]{1,0:T(8,128)}, u32[]{:S(2)}) copy-start(f32[2048,128]{1,0:T(8,128)} %copy-done.1) | copy-start | bytes 3145732
  40.1 18.4 %copy-start.4 = (bf16[2,128,128]{2,1,0:T(8,128)(2,1)S(1)}, bf16[2,128,128]{2,1,0:T(8,128)(2,1)}, u32[]{:S(2)}) copy-start(bf16[2,128,128]{2,1,0:T(8,128)(2,1)} %w_out_ref.3) | copy-start | bytes 196612
  40.1 18.4 %copy-start.6 = (bf16[2,128,128]{2,1,0:T(8,128)(2,1)S(1)}, bf16[2,128,128]{2,1,0:T(8,128)(2,1)}, u32[]{:S(2)}) copy-start(bf16[2,128,128]{2,1,0:T(8,128)(2,1)} %w_gate_ref.3) | copy-start | bytes 196612
  40.1 18.4 %copy-start.8 = (bf16[512,128]{1,0:T(8,128)(2,1)S(1)}, bf16[512,128]{1,0:T(8,128)(2,1)}, u32[]{:S(2)}) copy-start(bf16[512,128]{1,0:T(8,128)(2,1)} %copy-done.7) | copy-start | bytes 393220

commit v4 on v3

--- a/solution.py
+++ b/solution.py
@@ -35,9 +35,15 @@
     return jnp.concatenate([padded[pl.ds(row, first, stride=second + 1), :] for row in rows], axis=0)
 
 
-def block_copies(hbm, padded, sems):
+def block_copies(hbm, padded, sem):
     first, second, _ = hbm.shape
-    return [(hbm.at[f], padded.at[pl.ds(f * (second + 1), second), :], sems.at[f]) for f in range(first)]
+    return [(hbm.at[f], padded.at[pl.ds(f * (second + 1), second), :], sem) for f in range(first)]
+
+
+def wait_block(hbm, padded, sem):
+    first, second, chans = hbm.shape
+    whole = padded.at[pl.ds(0, first * second), :]
+    pltpu.make_async_copy(whole, whole, sem).wait()
 
 
 def emit_branches(normed, w_t, planes, send_ref, done=None):
@@ -66,13 +72,16 @@
 ):
     first, second, _ = pair_hbm.shape
     ndev = send_ref.shape[0]
-    copies = [pltpu.make_async_copy(*c) for c in block_copies(pair_hbm, padded, in_sems)]
-    copies.append(pltpu.make_async_copy(gain_hbm, gain_ref, in_sems.at[first]))
-    copies.append(pltpu.make_async_copy(w_hbm.at[u], w_ref, in_sems.at[first + 1]))
-    for copy in copies:
+    copies = [pltpu.make_async_copy(*c) for c in block_copies(pair_hbm, padded, in_sems.at[0])]
+    small = [
+        pltpu.make_async_copy(gain_hbm, gain_ref, in_sems.at[1]),
+        pltpu.make_async_copy(w_hbm.at[u], w_ref, in_sems.at[2]),
+    ]
+    for copy in small + copies:
         copy.start()
-    for copy in copies:
+    for copy in small:
         copy.wait()
+    wait_block(pair_hbm, padded, in_sems.at[0])
     half = ndev // 2
     sent = []
 
@@ -169,12 +178,11 @@
     for i, row in enumerate(block_rows(first, second)):
         padded[pl.ds(row, first, stride=second + 1), :] = z[i * first : (i + 1) * first]
     copies = [
-        pltpu.make_async_copy(vmem, hbm, sem) for hbm, vmem, sem in block_copies(updated_hbm, padded, sems)
+        pltpu.make_async_copy(vmem, hbm, sem) for hbm, vmem, sem in block_copies(updated_hbm, padded, sems.at[0])
     ]
     for copy in copies:
         copy.start()
-    for copy in copies:
-        copy.wait()
+    wait_block(updated_hbm, padded, sems.at[0])
 
 
 def call(kernel, outs, scratch, flops, *args, ins=pltpu.VMEM, spaces=None, limit=VMEM_LIMIT):
@@ -232,7 +240,7 @@
             pltpu.VMEM(w_proj.shape[1:], BF16),
             planes,
             pltpu.VMEM(send_shape.shape, BF16),
-            pltpu.SemaphoreType.DMA((first + 2,)),
+            pltpu.SemaphoreType.DMA((3,)),
             pltpu.SemaphoreType.DMA((2,)),
         ],
         proj_flops, pair, norm_in_gain, w_proj,
@@ -260,7 +268,7 @@
     summed = triangle(exchange(send), 1)
     return call(
         last_kernel,
-        [jax.ShapeDtypeStruct(pair.shape, F32)], [normal, padded, pltpu.SemaphoreType.DMA((first,))], gate_flops,
+        [jax.ShapeDtypeStruct(pair.shape, F32)], [normal, padded, pltpu.SemaphoreType.DMA((1,))], gate_flops,
         middle, summed, gate, gain_cols, w_out, spaces=[pltpu.HBM],
     )
 

time: 112 us -> 110 us (0.982)
  Pallas kernels: 10.8 us -> 9.55 us
    pallas_call x6, Pallas kernels: 10.8 us -> 9.55 us  [call(): pl.pallas_call(kernel, out_shape=outs if several else outs[0], in_specs=[...]
where the time goes in v4:
time: 110 us
  blocking collectives  66.4 us (60%)
  waiting for transfers between devices  24.2 us (22%)
  Pallas kernels  9.55 us (9%)
  starting transfers between devices  7.29 us (7%)
  local copies, waits for them, and re-layouts  2.51 us (2%)
    all_to_all x3, blocking collectives, exchange(): return lax.all_to_all(block, axes, 0, 0, tiled=True)  66.4 us
    all_to_all x1, waiting for transfers between devices, exchange(): return lax.all_to_all(block, axes, 0, 0, tiled=True)  24.2 us
    pallas_call x6, Pallas kernels, call(): pl.pallas_call(kernel, out_shape=outs if several else outs[0], in_specs=[...  9.55 us
    all_to_all x1, starting transfers between devices, exchange(): return lax.all_to_all(block, axes, 0, 0, tiled=True)  7.29 us
    unnamed x22, local copies, waits for them, and re-layouts  2.51 us
  transfers between devices with their start and end apart: 1, of which 1 were waited for; matrix products, arithmetic and copies ran while one was open for 0% of the time, Pallas kernels for 1%

profile of v4, /device:TPU:0, one launch (start us, length us, event | category | flops | bytes accessed | tf_op | source)
XLA Modules:
  0.0 110.1 jit_solution(6872730001689887638)
XLA Ops:
  0.0 3.5 %shard_map.64 = bf16[32,2,64,128]{3,2,1,0:T(8,128)(2,1)} custom-call(f32[64,32,128]{2,1,0:T(8,128)} %pair_ref.1, f32[2,128]{1,0:T(2,128)} %gain_ref.3, bf16[2,128,512]{2,1,0:T(8,128)(2,1)} %w_ref.1), custom_call_target="tpu_custom_call" | custom-call | flops 268435456 | bytes 2360320 | tf_op jit(solution)/shard_map/pallas_call | solution.py:192
  3.5 0.0 copy-start
  3.5 0.0 copy-start.3
  3.5 0.0 copy-start.9
  3.5 0.0 copy-start.10
  3.5 7.3 %all-to-all-start = ((bf16[32,2,64,128]{3,2,1,0:T(8,128)(2,1)}), bf16[32,2,64,128]{3,2,1,0:T(8,128)(2,1)S(1)}, u32[]{:S(2)}, u32[]{:S(2)}) async-start(bf16[32,2,64,128]{3,2,1,0:T(8,128)(2,1)} %shard_map.64), calls=%async_computation | async-start | bytes 2097152 | tf_op jit(solution)/shard_map/all_to_all | solution.py:222
  10.8 0.0 copy-done
  10.8 0.0 copy-done.3
  10.8 0.0 copy-start.5
  10.9 0.8 copy-done.5
  11.7 0.9 shard_map.65
  12.6 1.0 copy-done.1
  13.6 0.6 copy-done.7
  14.2 24.2 %all-to-all-done = bf16[32,2,64,128]{3,2,1,0:T(8,128)(2,1)S(1)} async-done(((bf16[32,2,64,128]{3,2,1,0:T(8,128)(2,1)}), bf16[32,2,64,128]{3,2,1,0:T(8,128)(2,1)S(1)}, u32[]{:S(2)}, u32[]{:S(2)}) %all-to-all-start) | async-done | bytes 1048608 | tf_op jit(solution)/shard_map/all_to_all | solution.py:222
  38.4 1.0 shard_map.66
  39.4 0.0 copy-start.4
  39.4 0.0 copy-start.6
  39.4 18.4 %all_to_all.20 = bf16[32,4,16,128]{3,2,1,0:T(8,128)(2,1)S(1)} all-to-all(bf16[32,4,16,128]{3,2,1,0:T(8,128)(2,1)S(1)} %shard_map.66), channel_id=1, replica_groups=mesh['row'=4,'col'=8] {'row','col'}, dimensions={0} | all-to-all | bytes 1048576 | tf_op jit(solution)/shard_map/all_to_all | solution.py:222
  57.8 0.0 copy-done.8
  57.8 1.9 %shard_map.67 = (f32[2048,128]{1,0:T(8,128)S(1)}, f32[2048,128]{1,0:T(8,128)S(1)}, bf16[32,2,64,128]{3,2,1,0:T(8,128)(2,1)S(1)}) custom-call(f32[2048,128]{1,0:T(8,128)S(1)} %get-tuple-element.21.ordered_ref, bf16[128,16,128]{2,1,0:T(8,128)(2,1)S(1)} %bitcast.6, f32[2048,128]{1,0:T(8,128)S(1)} %copy-done.2, ...), custom_call_target="tpu_custom_call" | custom-call | flops 402653184 | bytes 6161408 | tf_op jit(solution)/shard_map/pallas_call | solution.py:192
  59.8 29.6 %all_to_all.21 = bf16[32,2,64,128]{3,2,1,0:T(8,128)(2,1)S(1)} all-to-all(bf16[32,2,64,128]{3,2,1,0:T(8,128)(2,1)S(1)} %get-tuple-element.27), channel_id=1, replica_groups=mesh['row'=4,'col'=8] {'row','col'}, dimensions={0} | all-to-all | bytes 2097152 | tf_op jit(solution)/shard_map/all_to_all | solution.py:222
  89.4 0.6 shard_map.68
  90.0 18.4 %all_to_all.22 = bf16[32,4,16,128]{3,2,1,0:T(8,128)(2,1)S(1)} all-to-all(bf16[32,4,16,128]{3,2,1,0:T(8,128)(2,1)S(1)} %shard_map.68), channel_id=1, replica_groups=mesh['row'=4,'col'=8] {'row','col'}, dimensions={0} | all-to-all | bytes 1048576 | tf_op jit(solution)/shard_map/all_to_all | solution.py:222
  108.4 1.7 %shard_map.69 = f32[64,32,128]{2,1,0:T(8,128)} custom-call(f32[2048,128]{1,0:T(8,128)S(1)} %get-tuple-element.26.first_ref, bf16[128,16,128]{2,1,0:T(8,128)(2,1)S(1)} %bitcast.7, f32[2048,128]{1,0:T(8,128)S(1)} %get-tuple-element.28.gate_ref, f32[2,128,128]{2,1,0:T(8,128)S(1)} %get-tuple-element.24.gain_cols_ref, bf16[2,128,128]{2,1,0:T(8,128)(2,1)S(1)} %copy-done.4), custom_call_target="tpu_custom_call" | custom-call | flops 67108864 | bytes 3866624 | tf_op jit(solution)/shard_map/pallas_call | solution.py:192
  (9 shorter events, 0.0 us)
Async XLA Ops:
  3.5 7.3 %copy-start = (f32[64,32,128]{2,1,0:T(8,128)S(1)}, f32[64,32,128]{2,1,0:T(8,128)}, u32[]{:S(2)}) copy-start(f32[64,32,128]{2,1,0:T(8,128)} %pair_ref.1) | copy-start | bytes 3145732
  3.5 7.3 %copy-start.3 = (bf16[2,128,512]{2,1,0:T(8,128)(2,1)S(1)}, bf16[2,128,512]{2,1,0:T(8,128)(2,1)}, u32[]{:S(2)}) copy-start(bf16[2,128,512]{2,1,0:T(8,128)(2,1)} %w_ref.1) | copy-start | bytes 786436
  3.5 7.3 %copy-start.9 = (f32[2,128]{1,0:T(2,128)S(1)}, f32[2,128]{1,0:T(2,128)}, u32[]{:S(2)}) copy-start(f32[2,128]{1,0:T(2,128)} %gain_ref.3) | copy-start | bytes 3076
  3.5 7.3 %copy-start.10 = (f32[2,128]{1,0:T(2,128)S(1)}, f32[2,128]{1,0:T(2,128)}, u32[]{:S(2)}) copy-start(f32[2,128]{1,0:T(2,128)} %out_gain_ref.1) | copy-start | bytes 3076
  3.5 34.9 %all-to-all-start = ((bf16[32,2,64,128]{3,2,1,0:T(8,128)(2,1)}), bf16[32,2,64,128]{3,2,1,0:T(8,128)(2,1)S(1)}, u32[]{:S(2)}, u32[]{:S(2)}) async-start(bf16[32,2,64,128]{3,2,1,0:T(8,128)(2,1)} %shard_map.64), calls=%async_computation | async-start | bytes 2097152 | tf_op jit(solution)/shard_map/all_to_all | solution.py:222
  10.8 0.8 copy-start.5
  12.6 1.0 copy-start.1
  13.6 0.7 copy-start.7
  38.4 19.4 %copy-start.2 = (f32[2048,128]{1,0:T(8,128)S(1)}, f32[2048,128]{1,0:T(8,128)}, u32[]{:S(2)}) copy-start(f32[2048,128]{1,0:T(8,128)} %copy-done.1) | copy-start | bytes 3145732
  39.4 18.4 %copy-start.4 = (bf16[2,128,128]{2,1,0:T(8,128)(2,1)S(1)}, bf16[2,128,128]{2,1,0:T(8,128)(2,1)}, u32[]{:S(2)}) copy-start(bf16[2,128,128]{2,1,0:T(8,128)(2,1)} %w_out_ref.3) | copy-start | bytes 196612
  39.4 18.4 %copy-start.6 = (bf16[2,128,128]{2,1,0:T(8,128)(2,1)S(1)}, bf16[2,128,128]{2,1,0:T(8,128)(2,1)}, u32[]{:S(2)}) copy-start(bf16[2,128,128]{2,1,0:T(8,128)(2,1)} %w_gate_ref.3) | copy-start | bytes 196612
  39.4 18.4 %copy-start.8 = (bf16[512,128]{1,0:T(8,128)(2,1)S(1)}, bf16[512,128]{1,0:T(8,128)(2,1)}, u32[]{:S(2)}) copy-start(bf16[512,128]{1,0:T(8,128)(2,1)} %copy-done.7) | copy-start | bytes 393220

commit v5 on v4

v5 whole, which is shorter than its diff:
```python
import functools

import jax
import jax.numpy as jnp
from jax import lax
from jax.experimental import pallas as pl
from jax.experimental.pallas import tpu as pltpu
from jax.sharding import PartitionSpec as P

LANES = 128
BF16 = jnp.bfloat16
F32 = jnp.float32
VMEM_LIMIT = 16 * 1024 * 1024


def sigmoid(x):
    return 0.5 * jnp.tanh(0.5 * x) + 0.5


def norm_rows(x, gain):
    center = x - jnp.mean(x, axis=-1, keepdims=True)
    spread = jnp.mean(center * center, axis=-1, keepdims=True)
    return (center * lax.rsqrt(spread + 1e-05) * gain).astype(BF16)


def block_rows(first, second):
    split = LANES // first
    n1 = second // split
    return [l * n1 + s for s in range(n1) for l in range(split)]


def load_block(padded, first, second):
    rows = block_rows(first, second)
    return jnp.concatenate([padded[pl.ds(row, first, stride=second + 1), :] for row in rows], axis=0)


def block_copies(hbm, padded, sem):
    first, second, _ = hbm.shape
    return [(hbm.at[f], padded.at[pl.ds(f * (second + 1), second), :], sem) for f in range(first)]


def wait_block(hbm, padded, sem):
    first, second, chans = hbm.shape
    whole = padded.at[pl.ds(0, first * second), :]
    pltpu.make_async_copy(whole, whole, sem).wait()


def branch_planes(normed, w_t, n1, planes):
    hidden = w_t.shape[0] // 4
    pad = n1 + 1
    proj = lax.dot_general(w_t, normed, (((1,), (1,)), ((), ())), preferred_element_type=F32)
    for side in range(2):
        at = 2 * side * hidden
        value = sigmoid(proj[at : at + hidden]) * proj[at + hidden : at + 2 * hidden]
        for s in range(n1):
            planes[pl.ds(side * hidden * pad + s, hidden, stride=pad), :] = value[:, s * LANES : (s + 1) * LANES]


def plane(planes, n1, channel):
    at = channel * (n1 + 1)
    return planes[at : at + n1, :].astype(BF16)


def project_kernel(
    u, pair_hbm, gain_hbm, w_hbm, send_hbm, padded, gain_ref, w_ref, planes, send_ref, in_sems, out_sems
):
    first, second, _ = pair_hbm.shape
    ndev = send_ref.shape[0]
    copies = [pltpu.make_async_copy(*c) for c in block_copies(pair_hbm, padded, in_sems.at[0])]
    small = [
        pltpu.make_async_copy(gain_hbm, gain_ref, in_sems.at[1]),
        pltpu.make_async_copy(w_hbm.at[u], w_ref, in_sems.at[2]),
    ]
    for copy in small + copies:
        copy.start()
    for copy in small:
        copy.wait()
    wait_block(pair_hbm, padded, in_sems.at[0])
    depth, n1 = send_ref.shape[2:4]
    hidden = ndev * depth
    normed = norm_rows(load_block(padded, first, second), gain_ref[u : u + 1, :])
    branch_planes(normed, w_ref[...].T, n1, planes)
    sent = []
    for part in range(2):
        own = range(part * ndev // 2, (part + 1) * ndev // 2)
        for device in own:
            for side in range(2):
                for h in range(depth):
                    send_ref[device, side, h] = plane(planes, n1, side * hidden + device * depth + h)
        at = pl.ds(own[0], len(own))
        sent.append(pltpu.make_async_copy(send_ref.at[at], send_hbm.at[at], out_sems.at[part]))
        sent[-1].start()
    for copy in sent:
        copy.wait()


def move(copies):
    for copy in copies:
        copy.start()
    for copy in copies:
        copy.wait()


def prepare_kernel(
    pair_hbm, gain_ref, w_gate_ref, w_ref, out_gain_ref,
    ordered_hbm, gate_hbm, w_t_ref, gain_cols_ref, padded, ordered_ref, gate_ref, sems,
):
    first, second, _ = pair_hbm.shape
    for copy in block_copies(pair_hbm, padded, sems.at[0]):
        pltpu.make_async_copy(*copy).start()
    w_t_ref[...] = w_ref[1].T
    for u in range(2):
        wide = (LANES, out_gain_ref.shape[1])
        gain_cols_ref[u] = jnp.broadcast_to(out_gain_ref[u : u + 1, :], wide).T
    wait_block(pair_hbm, padded, sems.at[0])
    x = load_block(padded, first, second)
    ordered_ref[...] = x
    normed = norm_rows(x, gain_ref[0:1, :])
    gate_ref[...] = sigmoid(jnp.dot(normed, w_gate_ref[0], preferred_element_type=F32))
    move([
        pltpu.make_async_copy(ordered_ref, ordered_hbm, sems.at[1]),
        pltpu.make_async_copy(gate_ref, gate_hbm, sems.at[2]),
    ])


def gate_kernel(first_hbm, gain_ref, w_gate_ref, gate_hbm, first_ref, gate_ref, sems):
    move([pltpu.make_async_copy(first_hbm, first_ref, sems.at[0])])
    normed = norm_rows(first_ref[...], gain_ref[1:2, :])
    gate_ref[...] = sigmoid(jnp.dot(normed, w_gate_ref[1], preferred_element_type=F32))
    move([pltpu.make_async_copy(gate_ref, gate_hbm, sems.at[1])])


def outgoing_kernel(cols, first, recv_ref, out_ref, left, right):
    ndev, _, depth, n1, _ = recv_ref.shape
    split = LANES // first
    rows = ndev // cols
    for h in range(depth):
        for side, dense in ((0, left), (1, right)):
            for c in range(cols):
                for l in range(split):
                    at = (c * split + l) * n1
                    dense[at : at + n1, :] = jnp.concatenate(
                        [
                            recv_ref[r * cols + c, side, h, :, l * first : (l + 1) * first]
                            for r in range(rows)
                        ],
                        axis=1,
                    )
        summed = lax.dot_general(
            right[...], left[...], (((0,), (0,)), ((), ())), preferred_element_type=F32
        ).astype(BF16)
        scatter_product(summed, rows, cols, first, h, out_ref)


def scatter_product(summed, rows, cols, first, h, out_ref):
    split = LANES // first
    n1 = out_ref.shape[2]
    for r in range(rows):
        for c in range(cols):
            out_ref[r * cols + c, h] = jnp.concatenate(
                [
                    summed[(c * split + l) * n1 : (c * split + l + 1) * n1, r * first : (r + 1) * first]
                    for l in range(split)
                ],
                axis=1,
            )


def incoming_kernel(cols, first, recv_ref, *refs):
    *part_refs, out_ref, left, right, b_ref = refs
    ndev, depth, n1, _ = recv_ref.shape
    split = LANES // first
    rows = ndev // cols
    for r in range(rows):
        b_ref[0, r] = part_refs[r][...]
    for apart, part_ref in enumerate(part_refs[rows:], 1):
        b_ref[apart] = part_ref[...]
    my_row, my_rest = lax.axis_index("row"), lax.axis_index("rest")
    for h in range(depth):
        for c in range(cols):
            for l in range(split):
                at = (c * split + l) * n1
                left[at : at + n1, :] = jnp.concatenate(
                    [recv_ref[r * cols + c, h, :, l * first : (l + 1) * first] for r in range(rows)], axis=1
                )
        for c in range(cols // 2):
            apart = jnp.bitwise_xor(my_rest, c)
            for l in range(split):
                at = (c * split + l) * n1
                right[at : at + n1, :] = jnp.concatenate(
                    [
                        b_ref[apart // 2, jnp.bitwise_xor(my_row, r), apart % 2, h, :, l * first : (l + 1) * first]
                        for r in range(rows)
                    ],
                    axis=1,
                )
        summed = lax.dot_general(
            right[...], left[...], (((1,), (1,)), ((), ())), preferred_element_type=F32
        ).astype(BF16)
        scatter_product(summed, rows, cols // 2, first, h, out_ref)


def output(summed_ref, gain_cols, w, normal):
    hidden, n1, _ = summed_ref.shape
    pad = n1 + 1
    x = summed_ref[...].astype(F32)
    center = x - jnp.mean(x, axis=0, keepdims=True)
    spread = jnp.mean(center * center, axis=0, keepdims=True)
    scaled = center * lax.rsqrt(spread + 1e-05)
    for h in range(hidden):
        normal[h * pad : h * pad + n1, :] = scaled[h]
    mixed = jnp.concatenate(
        [(normal[pl.ds(s, hidden, stride=pad), :] * gain_cols).astype(BF16) for s in range(n1)], axis=1
    )
    return lax.dot_general(mixed, w, (((0,), (0,)), ((), ())), preferred_element_type=F32)


def middle_kernel(
    ordered_ref, summed_ref, gate_ref, gain_cols_ref, w_out_ref, gain_ref, w_t_ref,
    first_hbm, send_hbm, keep_hbm, swap_hbm, normal, planes, first_ref, send_ref, b_ref, sems,
):
    rows, halves, rest, depth, n1, _ = send_ref.shape
    hidden = rows * rest * depth
    copies = []

    def leave(vmem, hbm):
        copies.append(pltpu.make_async_copy(vmem, hbm, sems.at[len(copies)]))
        copies[-1].start()

    z = ordered_ref[...] + gate_ref[...] * output(summed_ref, gain_cols_ref[0], w_out_ref[0], normal)
    first_ref[...] = z
    leave(first_ref, first_hbm)
    branch_planes(norm_rows(z, gain_ref[1:2, :]), w_t_ref[...], n1, planes)
    my_row, my_rest = lax.axis_index("row"), lax.axis_index("rest")
    for r in range(rows):
        for c in range(rest):
            apart = jnp.bitwise_xor(my_rest, c)
            at = (r * rest + c) * depth
            for h in range(depth):
                b_ref[apart % 2, jnp.bitwise_xor(my_row, r), apart // 2, h] = plane(planes, n1, hidden + at + h)
    leave(b_ref.at[1], swap_hbm)
    leave(b_ref.at[0], keep_hbm)
    for r in range(rows):
        for c in range(rest):
            at = (r * rest + c) * depth
            for h in range(depth):
                value = plane(planes, n1, at + h)
                for half in range(halves):
                    send_ref[r, half, c, h] = value
        if r % (rows // 2) == rows // 2 - 1:
            own = pl.ds(r + 1 - rows // 2, rows // 2)
            leave(send_ref.at[own], send_hbm.at[own])
    for copy in copies:
        copy.wait()


def last_kernel(
    first_ref, summed_ref, gate_ref, gain_cols_ref, w_out_ref, updated_hbm, normal, padded, sems
):
    first, second, _ = updated_hbm.shape
    z = first_ref[...] + gate_ref[...] * output(summed_ref, gain_cols_ref[1], w_out_ref[1], normal)
    for i, row in enumerate(block_rows(first, second)):
        padded[pl.ds(row, first, stride=second + 1), :] = z[i * first : (i + 1) * first]
    copies = [
        pltpu.make_async_copy(vmem, hbm, sem) for hbm, vmem, sem in block_copies(updated_hbm, padded, sems.at[0])
    ]
    for copy in copies:
        copy.start()
    wait_block(updated_hbm, padded, sems.at[0])


def call(kernel, outs, scratch, flops, *args, pinned=None, spaces=None):
    moved = sum(a.size * a.dtype.itemsize for a in args) + sum(o.size * o.dtype.itemsize for o in outs)
    pinned = pinned or [None] * len(args)
    spaces = spaces or [None] * len(outs)
    args = [a if space is None else pltpu.with_memory_space_constraint(a, space) for a, space in zip(args, pinned)]
    outs = [o if space is None else space(o.shape, o.dtype) for o, space in zip(outs, spaces)]
    in_specs = [pl.BlockSpec(memory_space=space or pltpu.VMEM) for space in pinned]
    out_specs = [pl.BlockSpec(memory_space=space or pltpu.VMEM) for space in spaces]
    several = len(outs) > 1
    return pl.pallas_call(
        kernel,
        out_shape=outs if several else outs[0],
        in_specs=in_specs,
        out_specs=out_specs if several else out_specs[0],
        scratch_shapes=scratch,
        compiler_params=pltpu.CompilerParams(vmem_limit_bytes=VMEM_LIMIT),
        cost_estimate=pl.CostEstimate(flops=flops, bytes_accessed=moved, transcendentals=0),
    )(*args)


def spread(keep, swap):
    rows, highs = keep.shape[:2]
    rest = 2 * highs

    def swapped(x, axis, size, apart):
        return lax.ppermute(x, axis, [(d, d ^ apart) for d in range(size)]) if apart else x

    b = jnp.stack([keep, swapped(swap, "rest", rest, 1)], axis=2)
    far = [
        swapped(jnp.stack([swapped(b[r, c], "row", rows, r) for r in range(rows)]), "rest", rest, 2 * c)
        for c in range(1, highs)
    ]
    return [swapped(b[r, 0], "row", rows, r) for r in range(rows)] + far


def body(rows, cols, pair, norm_in_gain, w_proj, w_gate, norm_out_gain, w_out):
    first, second, chans = pair.shape
    hidden = w_out.shape[1]
    ndev = rows * cols
    rest = cols // 2
    depth, half_depth = hidden // ndev, 2 * hidden // ndev
    count = first * second
    n1 = count // LANES
    total = rows * first

    flat_shape = jax.ShapeDtypeStruct((count, chans), F32)
    planes = pltpu.VMEM((2 * hidden * (n1 + 1), LANES), F32)
    normal = pltpu.VMEM((hidden * (n1 + 1), LANES), F32)
    padded = pltpu.VMEM((first * (second + 1), chans), F32)
    proj_flops = 2 * count * chans * 4 * hidden
    gate_flops = 2 * count * chans * chans
    tri_flops = 2 * depth * total**3

    def shaped(*shape):
        return jax.ShapeDtypeStruct(shape + (n1, LANES), BF16)

    send = call(
        functools.partial(project_kernel, 0),
        [shaped(ndev, 2, depth)],
        [
            padded,
            pltpu.VMEM(norm_in_gain.shape, F32),
            pltpu.VMEM(w_proj.shape[1:], BF16),
            planes,
            pltpu.VMEM((ndev, 2, depth, n1, LANES), BF16),
            pltpu.SemaphoreType.DMA((3,)),
            pltpu.SemaphoreType.DMA((2,)),
        ],
        proj_flops, pair, norm_in_gain, w_proj,
        pinned=[pltpu.HBM] * 3, spaces=[pltpu.HBM],
    )
    recv = lax.all_to_all(send, ("row", "half", "rest"), 0, 0, tiled=True)
    prepared = call(
        prepare_kernel,
        [
            flat_shape,
            flat_shape,
            jax.ShapeDtypeStruct((4 * hidden, chans), BF16),
            jax.ShapeDtypeStruct((2, hidden, LANES), F32),
        ],
        [padded, pltpu.VMEM(flat_shape.shape, F32), pltpu.VMEM(flat_shape.shape, F32), pltpu.SemaphoreType.DMA((3,))],
        gate_flops,
        pair, norm_in_gain, w_gate, w_proj, norm_out_gain,
        pinned=[pltpu.HBM] + [None] * 4, spaces=[pltpu.HBM, pltpu.HBM, None, None],
    )
    recv, (ordered, gate, w_t, gain_cols) = lax.optimization_barrier((recv, prepared))
    product = call(
        functools.partial(outgoing_kernel, cols, first),
        [shaped(ndev, depth)], [pltpu.VMEM((cols * second, total), BF16)] * 2, tri_flops, recv,
    )
    summed = lax.all_to_all(product, ("row", "half", "rest"), 0, 0, tiled=True)
    send_shape, b_shape = shaped(rows, 2, rest, half_depth), shaped(rows, rest // 2, half_depth)
    middle, send, keep, swap = call(
        middle_kernel,
        [flat_shape, send_shape, b_shape, b_shape],
        [
            normal,
            planes,
            pltpu.VMEM(flat_shape.shape, F32),
            pltpu.VMEM(send_shape.shape, BF16),
            pltpu.VMEM((2,) + b_shape.shape, BF16),
            pltpu.SemaphoreType.DMA((5,)),
        ],
        proj_flops + gate_flops,
        ordered, summed.reshape(hidden, n1, LANES), gate, gain_cols, w_out, norm_in_gain, w_t,
        spaces=[pltpu.HBM] * 4,
    )
    recv = lax.all_to_all(
        send.reshape(ndev, half_depth, n1, LANES), ("row", "half", "rest"), 0, 0, tiled=True
    )
    gate = call(
        gate_kernel, [flat_shape],
        [pltpu.VMEM(flat_shape.shape, F32), pltpu.VMEM(flat_shape.shape, F32), pltpu.SemaphoreType.DMA((2,))],
        gate_flops, middle, norm_in_gain, w_gate,
        pinned=[pltpu.HBM, None, None], spaces=[pltpu.HBM],
    )
    recv, gate = lax.optimization_barrier((recv, gate))
    product = call(
        functools.partial(incoming_kernel, cols, first),
        [shaped(rows * rest, half_depth)],
        [
            pltpu.VMEM((cols * second, total), BF16),
            pltpu.VMEM((rest * second, total), BF16),
            pltpu.VMEM((rest // 2, rows, 2, half_depth, n1, LANES), BF16),
        ],
        tri_flops, recv, *spread(keep, swap),
    )
    summed = lax.all_to_all(product, ("row", "rest"), 0, 0, tiled=True)
    return call(
        last_kernel,
        [jax.ShapeDtypeStruct(pair.shape, F32)], [normal, padded, pltpu.SemaphoreType.DMA((1,))], gate_flops,
        middle, summed.reshape(hidden, n1, LANES), gate, gain_cols, w_out, spaces=[pltpu.HBM],
    )


def solution(mesh):
    rows, cols = mesh.shape["row"], mesh.shape["col"]
    halved = jax.sharding.Mesh(mesh.devices.reshape(rows, 2, cols // 2), ("row", "half", "rest"))
    block = P("row", ("half", "rest"), None)
    return jax.shard_map(
        functools.partial(body, rows, cols),
        mesh=halved,
        in_specs=(block, P(), P(), P(), P(), P()),
        out_specs=block,
        check_vma=False,
    )
```

time: 110 us -> 108 us (0.982)
  blocking collectives: 66.4 us -> 31.7 us
  waiting for transfers between devices: 24.2 us -> 40.7 us
  starting transfers between devices: 7.29 us -> 18.2 us
  Pallas kernels: 9.55 us -> 16.4 us
  local copies, waits for them, and re-layouts: 2.51 us -> 0.06 us
    all_to_all x3 -> x2, blocking collectives: 66.4 us -> 31.7 us  [the longest x1 18.4 us: body(): summed = lax.all_to_all(product, ('row', 'half', 'rest'), 0, 0, tiled=True)]
    ppermute x0 -> x8, waiting for transfers between devices: none -> 10 us  [swapped(): lax.ppermute(x, axis, [(d, d ^ apart) for d in range(size)])]
    ppermute x0 -> x8, starting transfers between devices: none -> 8.17 us  [swapped(): lax.ppermute(x, axis, [(d, d ^ apart) for d in range(size)])]
    pallas_call x6 -> x7, Pallas kernels: 9.55 us -> 16.4 us  [call(): pl.pallas_call(kernel, out_shape=outs if several else outs[0], in_specs=i...]
    all_to_all x1 -> x2, waiting for transfers between devices: 24.2 us -> 30.6 us  [the longest x1 24.4 us: body(): recv = lax.all_to_all(send, ('row', 'half', 'rest'), 0, 0, tiled=True)]
    all_to_all x1 -> x2, starting transfers between devices: 7.29 us -> 10.1 us  [the longest x1 7.29 us: body(): recv = lax.all_to_all(send, ('row', 'half', 'rest'), 0, 0, tiled=True)]
    unnamed x22, local copies, waits for them, and re-layouts: 2.51 us -> 0.06 us
  transfers between devices with their start and end apart: 1 -> 10, of which waited for: 1 -> 5; matrix products, arithmetic and copies ran while one was open for 0% -> 0% of each run, Pallas kernels for 1% -> 6%
where the time goes in v5:
time: 108 us; the launch traced here: 107 us
  waiting for transfers between devices  40.7 us (38%)
  blocking collectives  31.7 us (29%)
  starting transfers between devices  18.2 us (17%)
  Pallas kernels  16.4 us (15%)
    all_to_all x1, waiting for transfers between devices, body(): recv = lax.all_to_all(send, ('row', 'half', 'rest'), 0, 0, tiled=True)  24.4 us
    all_to_all x1, blocking collectives, body(): summed = lax.all_to_all(product, ('row', 'half', 'rest'), 0, 0, tiled=True)  18.4 us
    pallas_call x7, Pallas kernels, call(): pl.pallas_call(kernel, out_shape=outs if several else outs[0], in_specs=i...  16.4 us
    all_to_all x1, blocking collectives, body(): summed = lax.all_to_all(product, ('row', 'rest'), 0, 0, tiled=True)  13.3 us
    ppermute x8, waiting for transfers between devices, swapped(): lax.ppermute(x, axis, [(d, d ^ apart) for d in range(size)])  10 us
    ppermute x8, starting transfers between devices, swapped(): lax.ppermute(x, axis, [(d, d ^ apart) for d in range(size)])  8.17 us
    all_to_all x1, starting transfers between devices, body(): recv = lax.all_to_all(send, ('row', 'half', 'rest'), 0, 0, tiled=True)  7.29 us
    all_to_all x1, waiting for transfers between devices, body(): lax.all_to_all(send.reshape(ndev, half_depth, n1, LANES), ('row', 'half',...  6.29 us
  transfers between devices with their start and end apart: 10, of which 5 were waited for; matrix products, arithmetic and copies ran while one was open for 0% of the time, Pallas kernels for 6%

profile of v5, /device:TPU:0, one launch (start us, length us, event | category | flops | bytes accessed | tf_op | source)
XLA Modules:
  0.0 107.3 jit_solution(12820935763586434070)
XLA Ops:
  0.0 3.5 %shard_map.64 = bf16[32,2,4,16,128]{4,3,2,1,0:T(8,128)(2,1)} custom-call(f32[64,32,128]{2,1,0:T(8,128)} %pair_hbm.3, f32[2,128]{1,0:T(2,128)} %gain_ref.5, bf16[2,128,512]{2,1,0:T(8,128)(2,1)} %w_ref.1), custom_call_target="tpu_custom_call" | custom-call | flops 268435456 | bytes 2360320 | tf_op jit(solution)/shard_map/pallas_call | solution.py:281
  3.5 7.3 %all-to-all-start = ((bf16[32,2,4,16,128]{4,3,2,1,0:T(8,128)(2,1)}), bf16[32,2,4,16,128]{4,3,2,1,0:T(8,128)(2,1)S(1)}, u32[]{:S(2)}, u32[]{:S(2)}) async-start(bf16[32,2,4,16,128]{4,3,2,1,0:T(8,128)(2,1)} %shard_map.64), calls=%async_computation | async-start | bytes 2097152 | tf_op jit(solution)/shard_map/all_to_all | solution.py:343
  10.8 3.2 %shard_map.65 = (f32[2048,128]{1,0:T(8,128)}, f32[2048,128]{1,0:T(8,128)}, bf16[512,128]{1,0:T(8,128)(2,1)S(1)}, f32[2,128,128]{2,1,0:T(8,128)S(1)}) custom-call(f32[64,32,128]{2,1,0:T(8,128)} %pair_hbm.3, f32[2,128]{1,0:T(2,128)S(1)} %copy-done.7, bf16[2,128,128]{2,1,0:T(8,128)(2,1)S(1)} %copy-done.6, bf16[2,128,512]{2,1,0:T(8,128)(2,1)S(1)} %copy-done.4, ...), custom_call_target="tpu_custom_call" | custom-call | flops 67108864 | bytes 3737600 | tf_op jit(solution)/shard_map/pallas_call | solution.py:281
  14.0 24.4 %all-to-all-done.recv_ref = bf16[32,2,4,16,128]{4,3,2,1,0:T(8,128)(2,1)S(1)} async-done(((bf16[32,2,4,16,128]{4,3,2,1,0:T(8,128)(2,1)}), bf16[32,2,4,16,128]{4,3,2,1,0:T(8,128)(2,1)S(1)}, u32[]{:S(2)}, u32[]{:S(2)}) %all-to-all-start) | async-done | bytes 1048608 | tf_op jit(solution)/shard_map/all_to_all | solution.py:343
  38.4 1.0 shard_map.66
  39.4 18.4 %all_to_all.20 = bf16[32,4,16,128]{3,2,1,0:T(8,128)(2,1)S(1)} all-to-all(bf16[32,4,16,128]{3,2,1,0:T(8,128)(2,1)S(1)} %shard_map.66), channel_id=1, replica_groups=mesh['row'=4,'half'=2,'rest'=4] {'row','half','rest'}, dimensions={0} | all-to-all | bytes 1048576 | tf_op jit(solution)/shard_map/all_to_all | solution.py:362
  57.8 3.2 %shard_map.67 = (f32[2048,128]{1,0:T(8,128)}, bf16[4,2,4,8,16,128]{5,4,3,2,1,0:T(8,128)(2,1)}, bf16[4,2,8,16,128]{4,3,2,1,0:T(8,128)(2,1)}, bf16[4,2,8,16,128]{4,3,2,1,0:T(8,128)(2,1)}) custom-call(f32[2048,128]{1,0:T(8,128)S(1)} %copy-done.2, bf16[128,16,128]{2,1,0:T(8,128)(2,1)S(1)} %bitcast.24, f32[2048,128]{1,0:T(8,128)S(1)} %copy-done.3, ...), custom_call_target="tpu_custom_call" | custom-call | flops 335544320 | bytes 5571584 | tf_op jit(solution)/shard_map/pallas_call | solution.py:281
  61.1 2.8 %all-to-all-start.2 = ((bf16[32,8,16,128]{3,2,1,0:T(8,128)(2,1)}), bf16[32,8,16,128]{3,2,1,0:T(8,128)(2,1)S(1)}, u32[]{:S(2)}, u32[]{:S(2)}) async-start(bf16[32,8,16,128]{3,2,1,0:T(8,128)(2,1)} %bitcast.26), calls=%async_computation.2 | async-start | bytes 2097152 | tf_op jit(solution)/shard_map/all_to_all | solution.py:379
  63.9 0.2 collective-permute-start
  64.1 1.4 %collective-permute-done = bf16[4,2,8,16,128]{4,3,2,1,0:T(8,128)(2,1)S(1)} collective-permute-done((bf16[4,2,8,16,128]{4,3,2,1,0:T(8,128)(2,1)S(1)}, bf16[4,2,8,16,128]{4,3,2,1,0:T(8,128)(2,1)S(1)}, u32[]{:S(2)}, u32[]{:S(2)}) %collective-permute-start) | collective-permute-done | bytes 262176 | tf_op jit(solution)/shard_map/ppermute | solution.py:297
  65.6 1.7 %collective-permute-start.4 = (bf16[2,8,16,128]{3,2,1,0:T(8,128)(2,1)S(1)}, bf16[2,8,16,128]{3,2,1,0:T(8,128)(2,1)S(1)}, u32[]{:S(2)}, u32[]{:S(2)}) collective-permute-start(bf16[2,8,16,128]{3,2,1,0:T(8,128)(2,1)S(1)} %get-tuple-element.40), channel_id=1, source_target_pairs={{0,8},{8,0},{16,24},{24,16},{1,9},{9,1},{17,25},{25,17},{2,10},{10... | collective-permute-start | bytes 196616 | tf_op jit(solution)/shard_map/ppermute | solution.py:297
  67.3 1.5 %collective-permute-start.6 = (bf16[2,8,16,128]{3,2,1,0:T(8,128)(2,1)S(1)}, bf16[2,8,16,128]{3,2,1,0:T(8,128)(2,1)S(1)}, u32[]{:S(2)}, u32[]{:S(2)}) collective-permute-start(bf16[2,8,16,128]{3,2,1,0:T(8,128)(2,1)S(1)} %get-tuple-element.41), channel_id=1, source_target_pairs={{0,24},{8,16},{16,8},{24,0},{1,25},{9,17},{17,9},{25,1},{2,26},{10... | collective-permute-start | bytes 196616 | tf_op jit(solution)/shard_map/ppermute | solution.py:297
  68.7 0.4 collective-permute-start.5
  69.1 5.4 %collective-permute-done.4 = bf16[2,8,16,128]{3,2,1,0:T(8,128)(2,1)S(1)} collective-permute-done((bf16[2,8,16,128]{3,2,1,0:T(8,128)(2,1)S(1)}, bf16[2,8,16,128]{3,2,1,0:T(8,128)(2,1)S(1)}, u32[]{:S(2)}, u32[]{:S(2)}) %collective-permute-start.4) | collective-permute-done | bytes 65568 | tf_op jit(solution)/shard_map/ppermute | solution.py:297
  74.5 3.2 %collective-permute-done.6 = bf16[2,8,16,128]{3,2,1,0:T(8,128)(2,1)S(1)} collective-permute-done((bf16[2,8,16,128]{3,2,1,0:T(8,128)(2,1)S(1)}, bf16[2,8,16,128]{3,2,1,0:T(8,128)(2,1)S(1)}, u32[]{:S(2)}, u32[]{:S(2)}) %collective-permute-start.6) | collective-permute-done | bytes 65568 | tf_op jit(solution)/shard_map/ppermute | solution.py:297
  77.8 1.0 collective-permute-start.7
  78.7 0.2 collective-permute-start.1
  78.9 0.6 collective-permute-start.2
  79.5 2.7 %collective-permute-start.3 = (bf16[2,8,16,128]{3,2,1,0:T(8,128)(2,1)S(1)}, bf16[2,8,16,128]{3,2,1,0:T(8,128)(2,1)S(1)}, u32[]{:S(2)}, u32[]{:S(2)}) collective-permute-start(bf16[2,8,16,128]{3,2,1,0:T(8,128)(2,1)S(1)} %get-tuple-element.39), channel_id=1, source_target_pairs={{0,24},{8,16},{16,8},{24,0},{1,25},{9,17},{17,9},{25,1},{2,26},{10... | collective-permute-start | bytes 196616 | tf_op jit(solution)/shard_map/ppermute | solution.py:297
  82.2 3.0 %shard_map.68.gate_ref = f32[2048,128]{1,0:T(8,128)} custom-call(f32[2048,128]{1,0:T(8,128)} %get-tuple-element.29.first_hbm.first_ref, f32[2,128]{1,0:T(2,128)S(1)} %copy-done.7, bf16[2,128,128]{2,1,0:T(8,128)(2,1)S(1)} %copy-done.6), custom_call_target="tpu_custom_call" | custom-call | flops 67108864 | bytes 2163712 | tf_op jit(solution)/shard_map/pallas_call | solution.py:281
  85.2 6.3 %all-to-all-done.2.recv_ref = bf16[32,8,16,128]{3,2,1,0:T(8,128)(2,1)S(1)} async-done(((bf16[32,8,16,128]{3,2,1,0:T(8,128)(2,1)}), bf16[32,8,16,128]{3,2,1,0:T(8,128)(2,1)S(1)}, u32[]{:S(2)}, u32[]{:S(2)}) %all-to-all-start.2) | async-done | bytes 1048608 | tf_op jit(solution)/shard_map/all_to_all | solution.py:379
  91.5 0.8 shard_map.69
  92.3 13.3 %all_to_all.21 = bf16[16,8,16,128]{3,2,1,0:T(8,128)(2,1)S(1)} all-to-all(bf16[16,8,16,128]{3,2,1,0:T(8,128)(2,1)S(1)} %shard_map.69), channel_id=1, replica_groups=mesh['row'=4,'half'=2,'rest'=4] {'row','rest'}, dimensions={0} | all-to-all | bytes 1048576 | tf_op jit(solution)/shard_map/all_to_all | solution.py:399
  105.6 1.7 %shard_map.70 = f32[64,32,128]{2,1,0:T(8,128)} custom-call(f32[2048,128]{1,0:T(8,128)S(1)} %copy-done, bf16[128,16,128]{2,1,0:T(8,128)(2,1)S(1)} %bitcast.25, f32[2048,128]{1,0:T(8,128)S(1)} %copy-done.1, f32[2,128,128]{2,1,0:T(8,128)S(1)} %get-tuple-element.27.gain_cols_ref, bf16[2,128,128]{2,1,0:T(8,128)(2,1)S(1)} %copy-done.5), custom_call_target="tpu_custom_call" | custom-call | flops 67108864 | bytes 3866624 | tf_op jit(solution)/shard_map/pallas_call | solution.py:281
  (29 shorter events, 0.2 us)
Async XLA Ops:
  3.5 7.3 %copy-start.4 = (bf16[2,128,512]{2,1,0:T(8,128)(2,1)S(1)}, bf16[2,128,512]{2,1,0:T(8,128)(2,1)}, u32[]{:S(2)}) copy-start(bf16[2,128,512]{2,1,0:T(8,128)(2,1)} %w_ref.1) | copy-start | bytes 786436
  3.5 7.3 %copy-start.6 = (bf16[2,128,128]{2,1,0:T(8,128)(2,1)S(1)}, bf16[2,128,128]{2,1,0:T(8,128)(2,1)}, u32[]{:S(2)}) copy-start(bf16[2,128,128]{2,1,0:T(8,128)(2,1)} %w_gate_ref.3) | copy-start | bytes 196612
  3.5 7.3 %copy-start.7 = (f32[2,128]{1,0:T(2,128)S(1)}, f32[2,128]{1,0:T(2,128)}, u32[]{:S(2)}) copy-start(f32[2,128]{1,0:T(2,128)} %gain_ref.5) | copy-start | bytes 3076
  3.5 7.3 %copy-start.8 = (f32[2,128]{1,0:T(2,128)S(1)}, f32[2,128]{1,0:T(2,128)}, u32[]{:S(2)}) copy-start(f32[2,128]{1,0:T(2,128)} %out_gain_ref.1) | copy-start | bytes 3076
  3.5 34.9 %all-to-all-start = ((bf16[32,2,4,16,128]{4,3,2,1,0:T(8,128)(2,1)}), bf16[32,2,4,16,128]{4,3,2,1,0:T(8,128)(2,1)S(1)}, u32[]{:S(2)}, u32[]{:S(2)}) async-start(bf16[32,2,4,16,128]{4,3,2,1,0:T(8,128)(2,1)} %shard_map.64), calls=%async_computation | async-start | bytes 2097152 | tf_op jit(solution)/shard_map/all_to_all | solution.py:343
  38.4 19.4 %copy-start.2 = (f32[2048,128]{1,0:T(8,128)S(1)}, f32[2048,128]{1,0:T(8,128)}, u32[]{:S(2)}) copy-start(f32[2048,128]{1,0:T(8,128)} %get-tuple-element.24.ordered_ref) | copy-start | bytes 3145732
  38.4 19.4 %copy-start.3 = (f32[2048,128]{1,0:T(8,128)S(1)}, f32[2048,128]{1,0:T(8,128)}, u32[]{:S(2)}) copy-start(f32[2048,128]{1,0:T(8,128)} %get-tuple-element.26.gate_ref) | copy-start | bytes 3145732
  39.4 18.4 %copy-start.5 = (bf16[2,128,128]{2,1,0:T(8,128)(2,1)S(1)}, bf16[2,128,128]{2,1,0:T(8,128)(2,1)}, u32[]{:S(2)}) copy-start(bf16[2,128,128]{2,1,0:T(8,128)(2,1)} %w_out_ref.3) | copy-start | bytes 196612
  61.1 2.8 %copy-start.10 = (bf16[4,2,8,16,128]{4,3,2,1,0:T(8,128)(2,1)S(1)}, bf16[4,2,8,16,128]{4,3,2,1,0:T(8,128)(2,1)}, u32[]{:S(2)}) copy-start(bf16[4,2,8,16,128]{4,3,2,1,0:T(8,128)(2,1)} %get-tuple-element.33) | copy-start | bytes 786436
  61.1 4.4 %copy-start.9 = (bf16[4,2,8,16,128]{4,3,2,1,0:T(8,128)(2,1)S(1)}, bf16[4,2,8,16,128]{4,3,2,1,0:T(8,128)(2,1)}, u32[]{:S(2)}) copy-start(bf16[4,2,8,16,128]{4,3,2,1,0:T(8,128)(2,1)} %get-tuple-element.32) | copy-start | bytes 786436
  61.1 30.4 %all-to-all-start.2 = ((bf16[32,8,16,128]{3,2,1,0:T(8,128)(2,1)}), bf16[32,8,16,128]{3,2,1,0:T(8,128)(2,1)S(1)}, u32[]{:S(2)}, u32[]{:S(2)}) async-start(bf16[32,8,16,128]{3,2,1,0:T(8,128)(2,1)} %bitcast.26), calls=%async_computation.2 | async-start | bytes 2097152 | tf_op jit(solution)/shard_map/all_to_all | solution.py:379
  63.9 1.6 %collective-permute-start = (bf16[4,2,8,16,128]{4,3,2,1,0:T(8,128)(2,1)S(1)}, bf16[4,2,8,16,128]{4,3,2,1,0:T(8,128)(2,1)S(1)}, u32[]{:S(2)}, u32[]{:S(2)}) collective-permute-start(bf16[4,2,8,16,128]{4,3,2,1,0:T(8,128)(2,1)S(1)} %copy-done.10), channel_id=1, source_target_pairs={{0,1},{1,0},{2,3},{3,2},{4,5},{5,4},{6,7},{7,6},{8,9},{9,8},{10,11... | collective-permute-start | bytes 786440 | tf_op jit(solution)/shard_map/ppermute | solution.py:297
  65.6 8.9 %collective-permute-start.4 = (bf16[2,8,16,128]{3,2,1,0:T(8,128)(2,1)S(1)}, bf16[2,8,16,128]{3,2,1,0:T(8,128)(2,1)S(1)}, u32[]{:S(2)}, u32[]{:S(2)}) collective-permute-start(bf16[2,8,16,128]{3,2,1,0:T(8,128)(2,1)S(1)} %get-tuple-element.40), channel_id=1, source_target_pairs={{0,8},{8,0},{16,24},{24,16},{1,9},{9,1},{17,25},{25,17},{2,10},{10... | collective-permute-start | bytes 196616 | tf_op jit(solution)/shard_map/ppermute | solution.py:297
  67.3 10.5 %collective-permute-start.6 = (bf16[2,8,16,128]{3,2,1,0:T(8,128)(2,1)S(1)}, bf16[2,8,16,128]{3,2,1,0:T(8,128)(2,1)S(1)}, u32[]{:S(2)}, u32[]{:S(2)}) collective-permute-start(bf16[2,8,16,128]{3,2,1,0:T(8,128)(2,1)S(1)} %get-tuple-element.41), channel_id=1, source_target_pairs={{0,24},{8,16},{16,8},{24,0},{1,25},{9,17},{17,9},{25,1},{2,26},{10... | collective-permute-start | bytes 196616 | tf_op jit(solution)/shard_map/ppermute | solution.py:297
  68.7 9.0 %collective-permute-start.5 = (bf16[2,8,16,128]{3,2,1,0:T(8,128)(2,1)S(1)}, bf16[2,8,16,128]{3,2,1,0:T(8,128)(2,1)S(1)}, u32[]{:S(2)}, u32[]{:S(2)}) collective-permute-start(bf16[2,8,16,128]{3,2,1,0:T(8,128)(2,1)S(1)} %get-tuple-element.42), channel_id=1, source_target_pairs={{0,16},{8,24},{16,0},{24,8},{1,17},{9,25},{17,1},{25,9},{2,18},{10... | collective-permute-start | bytes 196616 | tf_op jit(solution)/shard_map/ppermute | solution.py:297
  77.8 13.7 %collective-permute-start.7 = (bf16[4,2,8,16,128]{4,3,2,1,0:T(8,128)(2,1)S(1)}, bf16[4,2,8,16,128]{4,3,2,1,0:T(8,128)(2,1)S(1)}, u32[]{:S(2)}, u32[]{:S(2)}) collective-permute-start(bf16[4,2,8,16,128]{4,3,2,1,0:T(8,128)(2,1)S(1)} %pad_maximum_fusion), channel_id=1, source_target_pairs={{0,2},{1,3},{2,0},{3,1},{4,6},{5,7},{6,4},{7,5},{8,10},{9,11},{10,... | collective-permute-start | bytes 786440 | tf_op jit(solution)/shard_map/ppermute | solution.py:297
  78.7 12.8 %collective-permute-start.1 = (bf16[2,8,16,128]{3,2,1,0:T(8,128)(2,1)S(1)}, bf16[2,8,16,128]{3,2,1,0:T(8,128)(2,1)S(1)}, u32[]{:S(2)}, u32[]{:S(2)}) collective-permute-start(bf16[2,8,16,128]{3,2,1,0:T(8,128)(2,1)S(1)} %get-tuple-element.37), channel_id=1, source_target_pairs={{0,8},{8,0},{16,24},{24,16},{1,9},{9,1},{17,25},{25,17},{2,10},{10... | collective-permute-start | bytes 196616 | tf_op jit(solution)/shard_map/ppermute | solution.py:297
  78.9 12.6 %collective-permute-start.2 = (bf16[2,8,16,128]{3,2,1,0:T(8,128)(2,1)S(1)}, bf16[2,8,16,128]{3,2,1,0:T(8,128)(2,1)S(1)}, u32[]{:S(2)}, u32[]{:S(2)}) collective-permute-start(bf16[2,8,16,128]{3,2,1,0:T(8,128)(2,1)S(1)} %get-tuple-element.38), channel_id=1, source_target_pairs={{0,16},{8,24},{16,0},{24,8},{1,17},{9,25},{17,1},{25,9},{2,18},{10... | collective-permute-start | bytes 196616 | tf_op jit(solution)/shard_map/ppermute | solution.py:297
  79.5 12.0 %collective-permute-start.3 = (bf16[2,8,16,128]{3,2,1,0:T(8,128)(2,1)S(1)}, bf16[2,8,16,128]{3,2,1,0:T(8,128)(2,1)S(1)}, u32[]{:S(2)}, u32[]{:S(2)}) collective-permute-start(bf16[2,8,16,128]{3,2,1,0:T(8,128)(2,1)S(1)} %get-tuple-element.39), channel_id=1, source_target_pairs={{0,24},{8,16},{16,8},{24,0},{1,25},{9,17},{17,9},{25,1},{2,26},{10... | collective-permute-start | bytes 196616 | tf_op jit(solution)/shard_map/ppermute | solution.py:297
  91.5 14.1 %copy-start.1 = (f32[2048,128]{1,0:T(8,128)S(1)}, f32[2048,128]{1,0:T(8,128)}, u32[]{:S(2)}) copy-start(f32[2048,128]{1,0:T(8,128)} %shard_map.68.gate_ref) | copy-start | bytes 3145732
  92.3 13.3 %copy-start = (f32[2048,128]{1,0:T(8,128)S(1)}, f32[2048,128]{1,0:T(8,128)}, u32[]{:S(2)}) copy-start(f32[2048,128]{1,0:T(8,128)} %get-tuple-element.29.first_hbm.first_ref) | copy-start | bytes 3145732

commit v6 on v5

--- a/solution.py
+++ b/solution.py
@@ -61,26 +61,52 @@
     return planes[at : at + n1, :].astype(BF16)
 
 
-def project_kernel(
-    u, pair_hbm, gain_hbm, w_hbm, send_hbm, padded, gain_ref, w_ref, planes, send_ref, in_sems, out_sems
-):
+def relative_blocks(b_ref, planes, n1, channels):
+    rows, highs = b_ref.shape[1:3]
+    my_row, my_rest = lax.axis_index("row"), lax.axis_index("rest")
+    for r in range(rows):
+        for c in range(2 * highs):
+            apart = jnp.bitwise_xor(my_rest, c)
+            for i, channel in enumerate(channels(r, c)):
+                b_ref[apart % 2, jnp.bitwise_xor(my_row, r), apart // 2, i] = plane(planes, n1, channel)
+
+
+def project_kernel(shared, pair_hbm, gain_hbm, w_hbm, send_hbm, *refs):
+    if shared:
+        keep_hbm, swap_hbm, padded, gain_ref, w_ref, planes, send_ref, b_ref, in_sems, out_sems = refs
+    else:
+        padded, gain_ref, w_ref, planes, send_ref, in_sems, out_sems = refs
     first, second, _ = pair_hbm.shape
-    ndev = send_ref.shape[0]
+    ndev, _, depth, n1, _ = send_ref.shape
+    hidden = ndev * (depth + shared)
     copies = [pltpu.make_async_copy(*c) for c in block_copies(pair_hbm, padded, in_sems.at[0])]
     small = [
         pltpu.make_async_copy(gain_hbm, gain_ref, in_sems.at[1]),
-        pltpu.make_async_copy(w_hbm.at[u], w_ref, in_sems.at[2]),
+        pltpu.make_async_copy(w_hbm.at[0], w_ref, in_sems.at[2]),
     ]
     for copy in small + copies:
         copy.start()
     for copy in small:
         copy.wait()
     wait_block(pair_hbm, padded, in_sems.at[0])
-    depth, n1 = send_ref.shape[2:4]
-    hidden = ndev * depth
-    normed = norm_rows(load_block(padded, first, second), gain_ref[u : u + 1, :])
+    normed = norm_rows(load_block(padded, first, second), gain_ref[0:1, :])
     branch_planes(normed, w_ref[...].T, n1, planes)
     sent = []
+
+    def leave(vmem, hbm):
+        sent.append(pltpu.make_async_copy(vmem, hbm, out_sems.at[len(sent)]))
+        sent[-1].start()
+
+    if shared:
+        rest = 2 * b_ref.shape[2]
+
+        def channels(r, c):
+            at = ndev * depth + (r * rest + c) * 2 * shared
+            return [side * hidden + at + h for side in range(2) for h in range(2 * shared)]
+
+        relative_blocks(b_ref, planes, n1, channels)
+        leave(b_ref.at[1], swap_hbm)
+        leave(b_ref.at[0], keep_hbm)
     for part in range(2):
         own = range(part * ndev // 2, (part + 1) * ndev // 2)
         for device in own:
@@ -88,8 +114,7 @@
                 for h in range(depth):
                     send_ref[device, side, h] = plane(planes, n1, side * hidden + device * depth + h)
         at = pl.ds(own[0], len(own))
-        sent.append(pltpu.make_async_copy(send_ref.at[at], send_hbm.at[at], out_sems.at[part]))
-        sent[-1].start()
+        leave(send_ref.at[at], send_hbm.at[at])
     for copy in sent:
         copy.wait()
 
@@ -130,10 +155,45 @@
     move([pltpu.make_async_copy(gate_ref, gate_hbm, sems.at[1])])
 
 
-def outgoing_kernel(cols, first, recv_ref, out_ref, left, right):
+def stage(part_refs, b_ref):
+    rows = b_ref.shape[1]
+    for r in range(rows):
+        b_ref[0, r] = part_refs[r][...]
+    for apart, part_ref in enumerate(part_refs[rows:], 1):
+        b_ref[apart] = part_ref[...]
+
+
+def dense_half(b_ref, i, first, dense):
+    highs, rows, _, _, n1, _ = b_ref.shape
+    split = LANES // first
+    my_row, my_rest = lax.axis_index("row"), lax.axis_index("rest")
+    for c in range(2 * highs):
+        apart = jnp.bitwise_xor(my_rest, c)
+        for l in range(split):
+            at = (c * split + l) * n1
+            dense[at : at + n1, :] = jnp.concatenate(
+                [
+                    b_ref[apart // 2, jnp.bitwise_xor(my_row, r), apart % 2, i, :, l * first : (l + 1) * first]
+                    for r in range(rows)
+                ],
+                axis=1,
+            )
+
+
+def outgoing_kernel(cols, first, shared, recv_ref, *refs):
+    if shared:
+        *part_refs, out_ref, left, right, half_left, half_right, b_ref = refs
+    else:
+        out_ref, left, right = refs
     ndev, _, depth, n1, _ = recv_ref.shape
     split = LANES // first
     rows = ndev // cols
+
+    def product(left, right):
+        return lax.dot_general(
+            right[...], left[...], (((0,), (0,)), ((), ())), preferred_element_type=F32
+        ).astype(BF16)
+
     for h in range(depth):
         for side, dense in ((0, left), (1, right)):
             for c in range(cols):
@@ -146,10 +206,13 @@
                         ],
                         axis=1,
                     )
-        summed = lax.dot_general(
-            right[...], left[...], (((0,), (0,)), ((), ())), preferred_element_type=F32
-        ).astype(BF16)
-        scatter_product(summed, rows, cols, first, h, out_ref)
+        scatter_product(product(left, right), rows, cols, first, h, out_ref)
+    if shared:
+        stage(part_refs, b_ref)
+        for h in range(2 * shared):
+            dense_half(b_ref, h, first, half_left)
+            dense_half(b_ref, 2 * shared + h, first, half_right)
+            scatter_product(product(half_left, half_right), rows, cols, first, depth + h, out_ref)
 
 
 def scatter_product(summed, rows, cols, first, h, out_ref):
@@ -171,11 +234,7 @@
     ndev, depth, n1, _ = recv_ref.shape
     split = LANES // first
     rows = ndev // cols
-    for r in range(rows):
-        b_ref[0, r] = part_refs[r][...]
-    for apart, part_ref in enumerate(part_refs[rows:], 1):
-        b_ref[apart] = part_ref[...]
-    my_row, my_rest = lax.axis_index("row"), lax.axis_index("rest")
+    stage(part_refs, b_ref)
     for h in range(depth):
         for c in range(cols):
             for l in range(split):
@@ -183,27 +242,16 @@
                 left[at : at + n1, :] = jnp.concatenate(
                     [recv_ref[r * cols + c, h, :, l * first : (l + 1) * first] for r in range(rows)], axis=1
                 )
-        for c in range(cols // 2):
-            apart = jnp.bitwise_xor(my_rest, c)
-            for l in range(split):
-                at = (c * split + l) * n1
-                right[at : at + n1, :] = jnp.concatenate(
-                    [
-                        b_ref[apart // 2, jnp.bitwise_xor(my_row, r), apart % 2, h, :, l * first : (l + 1) * first]
-                        for r in range(rows)
-                    ],
-                    axis=1,
-                )
+        dense_half(b_ref, h, first, right)
         summed = lax.dot_general(
             right[...], left[...], (((1,), (1,)), ((), ())), preferred_element_type=F32
         ).astype(BF16)
         scatter_product(summed, rows, cols // 2, first, h, out_ref)
 
 
-def output(summed_ref, gain_cols, w, normal):
-    hidden, n1, _ = summed_ref.shape
+def output(x, gain_cols, w, normal):
+    hidden, n1, _ = x.shape
     pad = n1 + 1
-    x = summed_ref[...].astype(F32)
     center = x - jnp.mean(x, axis=0, keepdims=True)
     spread = jnp.mean(center * center, axis=0, keepdims=True)
     scaled = center * lax.rsqrt(spread + 1e-05)
@@ -227,17 +275,19 @@
         copies.append(pltpu.make_async_copy(vmem, hbm, sems.at[len(copies)]))
         copies[-1].start()
 
-    z = ordered_ref[...] + gate_ref[...] * output(summed_ref, gain_cols_ref[0], w_out_ref[0], normal)
+    shared = summed_ref.shape[3] - depth // 2
+    own = summed_ref.shape[3] - 2 * shared
+    x = summed_ref[:, :, :, :own].astype(F32).reshape(-1, n1, LANES)
+    if shared:
+        x_shared = summed_ref[:, 0, :, own:].astype(F32) + summed_ref[:, 1, :, own:].astype(F32)
+        x = jnp.concatenate([x, x_shared.reshape(-1, n1, LANES)], axis=0)
+    z = ordered_ref[...] + gate_ref[...] * output(x, gain_cols_ref[0], w_out_ref[0], normal)
     first_ref[...] = z
     leave(first_ref, first_hbm)
     branch_planes(norm_rows(z, gain_ref[1:2, :]), w_t_ref[...], n1, planes)
-    my_row, my_rest = lax.axis_index("row"), lax.axis_index("rest")
-    for r in range(rows):
-        for c in range(rest):
-            apart = jnp.bitwise_xor(my_rest, c)
-            at = (r * rest + c) * depth
-            for h in range(depth):
-                b_ref[apart % 2, jnp.bitwise_xor(my_row, r), apart // 2, h] = plane(planes, n1, hidden + at + h)
+    relative_blocks(
+        b_ref, planes, n1, lambda r, c: [hidden + (r * rest + c) * depth + h for h in range(depth)]
+    )
     leave(b_ref.at[1], swap_hbm)
     leave(b_ref.at[0], keep_hbm)
     for r in range(rows):
@@ -258,7 +308,7 @@
     first_ref, summed_ref, gate_ref, gain_cols_ref, w_out_ref, updated_hbm, normal, padded, sems
 ):
     first, second, _ = updated_hbm.shape
-    z = first_ref[...] + gate_ref[...] * output(summed_ref, gain_cols_ref[1], w_out_ref[1], normal)
+    z = first_ref[...] + gate_ref[...] * output(summed_ref[...].astype(F32), gain_cols_ref[1], w_out_ref[1], normal)
     for i, row in enumerate(block_rows(first, second)):
         padded[pl.ds(row, first, stride=second + 1), :] = z[i * first : (i + 1) * first]
     copies = [
@@ -277,12 +327,11 @@
     outs = [o if space is None else space(o.shape, o.dtype) for o, space in zip(outs, spaces)]
     in_specs = [pl.BlockSpec(memory_space=space or pltpu.VMEM) for space in pinned]
     out_specs = [pl.BlockSpec(memory_space=space or pltpu.VMEM) for space in spaces]
-    several = len(outs) > 1
     return pl.pallas_call(
         kernel,
-        out_shape=outs if several else outs[0],
+        out_shape=outs,
         in_specs=in_specs,
-        out_specs=out_specs if several else out_specs[0],
+        out_specs=out_specs,
         scratch_shapes=scratch,
         compiler_params=pltpu.CompilerParams(vmem_limit_bytes=VMEM_LIMIT),
         cost_estimate=pl.CostEstimate(flops=flops, bytes_accessed=moved, transcendentals=0),
@@ -309,7 +358,8 @@
     hidden = w_out.shape[1]
     ndev = rows * cols
     rest = cols // 2
-    depth, half_depth = hidden // ndev, 2 * hidden // ndev
+    shared = hidden // ndev // 4
+    depth, half_depth = hidden // ndev - shared, 2 * hidden // ndev
     count = first * second
     n1 = count // LANES
     total = rows * first
@@ -320,25 +370,26 @@
     padded = pltpu.VMEM((first * (second + 1), chans), F32)
     proj_flops = 2 * count * chans * 4 * hidden
     gate_flops = 2 * count * chans * chans
-    tri_flops = 2 * depth * total**3
+    tri_flops = 2 * (depth + shared) * total**3
 
     def shaped(*shape):
         return jax.ShapeDtypeStruct(shape + (n1, LANES), BF16)
 
-    send = call(
-        functools.partial(project_kernel, 0),
-        [shaped(ndev, 2, depth)],
+    out_shapes = [shaped(ndev, 2, depth)] + [shaped(rows, rest // 2, 4 * shared)] * (2 if shared else 0)
+    send, *swaps = call(
+        functools.partial(project_kernel, shared),
+        out_shapes,
         [
             padded,
             pltpu.VMEM(norm_in_gain.shape, F32),
             pltpu.VMEM(w_proj.shape[1:], BF16),
             planes,
-            pltpu.VMEM((ndev, 2, depth, n1, LANES), BF16),
-            pltpu.SemaphoreType.DMA((3,)),
-            pltpu.SemaphoreType.DMA((2,)),
-        ],
+            pltpu.VMEM(out_shapes[0].shape, BF16),
+        ]
+        + ([pltpu.VMEM((2,) + out_shapes[1].shape, BF16)] if shared else [])
+        + [pltpu.SemaphoreType.DMA((3,)), pltpu.SemaphoreType.DMA((4,))],
         proj_flops, pair, norm_in_gain, w_proj,
-        pinned=[pltpu.HBM] * 3, spaces=[pltpu.HBM],
+        pinned=[pltpu.HBM] * 3, spaces=[pltpu.HBM] * len(out_shapes),
     )
     recv = lax.all_to_all(send, ("row", "half", "rest"), 0, 0, tiled=True)
     prepared = call(
@@ -355,9 +406,16 @@
         pinned=[pltpu.HBM] + [None] * 4, spaces=[pltpu.HBM, pltpu.HBM, None, None],
     )
     recv, (ordered, gate, w_t, gain_cols) = lax.optimization_barrier((recv, prepared))
-    product = call(
-        functools.partial(outgoing_kernel, cols, first),
-        [shaped(ndev, depth)], [pltpu.VMEM((cols * second, total), BF16)] * 2, tri_flops, recv,
+    half_scratch = [
+        pltpu.VMEM((rest * second, total), BF16),
+        pltpu.VMEM((rest * second, total), BF16),
+        pltpu.VMEM((rest // 2, rows, 2, 4 * shared, n1, LANES), BF16),
+    ]
+    (product,) = call(
+        functools.partial(outgoing_kernel, cols, first, shared),
+        [shaped(ndev, depth + 2 * shared)],
+        [pltpu.VMEM((cols * second, total), BF16)] * 2 + (half_scratch if shared else []),
+        tri_flops, recv, *(spread(*swaps) if shared else []),
     )
     summed = lax.all_to_all(product, ("row", "half", "rest"), 0, 0, tiled=True)
     send_shape, b_shape = shaped(rows, 2, rest, half_depth), shaped(rows, rest // 2, half_depth)
@@ -373,20 +431,20 @@
             pltpu.SemaphoreType.DMA((5,)),
         ],
         proj_flops + gate_flops,
-        ordered, summed.reshape(hidden, n1, LANES), gate, gain_cols, w_out, norm_in_gain, w_t,
+        ordered, summed.reshape(rows, 2, rest, depth + 2 * shared, n1, LANES), gate, gain_cols, w_out, norm_in_gain, w_t,
         spaces=[pltpu.HBM] * 4,
     )
     recv = lax.all_to_all(
         send.reshape(ndev, half_depth, n1, LANES), ("row", "half", "rest"), 0, 0, tiled=True
     )
-    gate = call(
+    (gate,) = call(
         gate_kernel, [flat_shape],
         [pltpu.VMEM(flat_shape.shape, F32), pltpu.VMEM(flat_shape.shape, F32), pltpu.SemaphoreType.DMA((2,))],
         gate_flops, middle, norm_in_gain, w_gate,
         pinned=[pltpu.HBM, None, None], spaces=[pltpu.HBM],
     )
     recv, gate = lax.optimization_barrier((recv, gate))
-    product = call(
+    (product,) = call(
         functools.partial(incoming_kernel, cols, first),
         [shaped(rows * rest, half_depth)],
         [
@@ -397,11 +455,12 @@
         tri_flops, recv, *spread(keep, swap),
     )
     summed = lax.all_to_all(product, ("row", "rest"), 0, 0, tiled=True)
-    return call(
+    (updated,) = call(
         last_kernel,
         [jax.ShapeDtypeStruct(pair.shape, F32)], [normal, padded, pltpu.SemaphoreType.DMA((1,))], gate_flops,
         middle, summed.reshape(hidden, n1, LANES), gate, gain_cols, w_out, spaces=[pltpu.HBM],
     )
+    return updated
 
 
 def solution(mesh):

time: 108 us -> 105 us (0.972)
  waiting for transfers between devices: 40.7 us -> 27 us
  starting transfers between devices: 18.2 us -> 26.3 us
  blocking collectives: 31.7 us -> 34.5 us
    all_to_all x1, waiting for transfers between devices: 24.4 us -> 4.38 us  [body(): recv = lax.all_to_all(send, ('row', 'half', 'rest'), 0, 0, tiled=True)]
    ppermute x8 -> x16, starting transfers between devices: 8.17 us -> 16.2 us  [swapped(): lax.ppermute(x, axis, [(d, d ^ apart) for d in range(size)])]
    ppermute x8 -> x16, waiting for transfers between devices: 10 us -> 16.4 us  [swapped(): lax.ppermute(x, axis, [(d, d ^ apart) for d in range(size)])]
    all_to_all x1, blocking collectives: 18.4 us -> 21.2 us  [body(): summed = lax.all_to_all(product, ('row', 'half', 'rest'), 0, 0, tiled=True)]
  transfers between devices with their start and end apart: 10 -> 18, of which waited for: 5 -> 9; matrix products, arithmetic and copies ran while one was open for 0% -> 0% of each run, Pallas kernels for 6% -> 6%
where the time goes in v6:
time: 105 us
  blocking collectives  34.5 us (33%)
  waiting for transfers between devices  27 us (26%)
  starting transfers between devices  26.3 us (25%)
  Pallas kernels  16.6 us (16%)
    all_to_all x1, blocking collectives, body(): summed = lax.all_to_all(product, ('row', 'half', 'rest'), 0, 0, tiled=True)  21.2 us
    pallas_call x7, Pallas kernels, call(): pl.pallas_call(kernel, out_shape=outs, in_specs=in_specs, out_specs=out_s...  16.6 us
    ppermute x16, waiting for transfers between devices, swapped(): lax.ppermute(x, axis, [(d, d ^ apart) for d in range(size)])  16.4 us
    ppermute x16, starting transfers between devices, swapped(): lax.ppermute(x, axis, [(d, d ^ apart) for d in range(size)])  16.2 us
    all_to_all x1, blocking collectives, body(): summed = lax.all_to_all(product, ('row', 'rest'), 0, 0, tiled=True)  13.3 us
    all_to_all x1, starting transfers between devices, body(): recv = lax.all_to_all(send, ('row', 'half', 'rest'), 0, 0, tiled=True)  7.29 us
    all_to_all x1, waiting for transfers between devices, body(): lax.all_to_all(send.reshape(ndev, half_depth, n1, LANES), ('row', 'half',...  6.29 us
    all_to_all x1, waiting for transfers between devices, body(): recv = lax.all_to_all(send, ('row', 'half', 'rest'), 0, 0, tiled=True)  4.38 us
  transfers between devices with their start and end apart: 18, of which 9 were waited for; matrix products, arithmetic and copies ran while one was open for 0% of the time, Pallas kernels for 6%

profile of v6, /device:TPU:0, one launch (start us, length us, event | category | flops | bytes accessed | tf_op | source)
XLA Modules:
  0.0 104.8 jit_solution(6860893787203863099)
XLA Ops:
  0.0 3.5 %shard_map.64 = (bf16[32,2,3,16,128]{4,3,2,1,0:T(8,128)(2,1)}, bf16[4,2,4,16,128]{4,3,2,1,0:T(8,128)(2,1)}, bf16[4,2,4,16,128]{4,3,2,1,0:T(8,128)(2,1)}) custom-call(f32[64,32,128]{2,1,0:T(8,128)} %pair_hbm.3, f32[2,128]{1,0:T(2,128)} %gain_ref.5, bf16[2,128,512]{2,1,0:T(8,128)(2,1)} %w_ref.1), custom_call_target="tpu_custom_call" | custom-call | flops 268435456 | bytes 2360320 | tf_op jit(solution)/shard_map/pallas_call | solution.py:330
  3.6 7.3 %all-to-all-start = ((bf16[32,2,3,16,128]{4,3,2,1,0:T(8,128)(2,1)}), bf16[32,2,3,16,128]{4,3,2,1,0:T(8,128)(2,1)S(1)}, u32[]{:S(2)}, u32[]{:S(2)}) async-start(bf16[32,2,3,16,128]{4,3,2,1,0:T(8,128)(2,1)} %get-tuple-element.23), calls=%async_computation | async-start | bytes 1572864 | tf_op jit(solution)/shard_map/all_to_all | solution.py:394
  12.3 1.8 %collective-permute-start.4 = (bf16[2,4,16,128]{3,2,1,0:T(8,128)(2,1)S(1)}, bf16[2,4,16,128]{3,2,1,0:T(8,128)(2,1)S(1)}, u32[]{:S(2)}, u32[]{:S(2)}) collective-permute-start(bf16[2,4,16,128]{3,2,1,0:T(8,128)(2,1)S(1)} %get-tuple-element.54), channel_id=1, source_target_pairs={{0,8},{8,0},{16,24},{24,16},{1,9},{9,1},{17,25},{25,17},{2,10},{10... | collective-permute-start | bytes 98312 | tf_op jit(solution)/shard_map/ppermute | solution.py:346
  14.2 1.5 %collective-permute-start.6 = (bf16[2,4,16,128]{3,2,1,0:T(8,128)(2,1)S(1)}, bf16[2,4,16,128]{3,2,1,0:T(8,128)(2,1)S(1)}, u32[]{:S(2)}, u32[]{:S(2)}) collective-permute-start(bf16[2,4,16,128]{3,2,1,0:T(8,128)(2,1)S(1)} %get-tuple-element.55), channel_id=1, source_target_pairs={{0,24},{8,16},{16,8},{24,0},{1,25},{9,17},{17,9},{25,1},{2,26},{10... | collective-permute-start | bytes 98312 | tf_op jit(solution)/shard_map/ppermute | solution.py:346
  15.9 2.4 %collective-permute-done.4 = bf16[2,4,16,128]{3,2,1,0:T(8,128)(2,1)S(1)} collective-permute-done((bf16[2,4,16,128]{3,2,1,0:T(8,128)(2,1)S(1)}, bf16[2,4,16,128]{3,2,1,0:T(8,128)(2,1)S(1)}, u32[]{:S(2)}, u32[]{:S(2)}) %collective-permute-start.4) | collective-permute-done | bytes 32800 | tf_op jit(solution)/shard_map/ppermute | solution.py:346
  18.2 2.5 %collective-permute-done.6 = bf16[2,4,16,128]{3,2,1,0:T(8,128)(2,1)S(1)} collective-permute-done((bf16[2,4,16,128]{3,2,1,0:T(8,128)(2,1)S(1)}, bf16[2,4,16,128]{3,2,1,0:T(8,128)(2,1)S(1)}, u32[]{:S(2)}, u32[]{:S(2)}) %collective-permute-start.6) | collective-permute-done | bytes 32800 | tf_op jit(solution)/shard_map/ppermute | solution.py:346
  21.8 1.4 %collective-permute-start.1 = (bf16[2,4,16,128]{3,2,1,0:T(8,128)(2,1)S(1)}, bf16[2,4,16,128]{3,2,1,0:T(8,128)(2,1)S(1)}, u32[]{:S(2)}, u32[]{:S(2)}) collective-permute-start(bf16[2,4,16,128]{3,2,1,0:T(8,128)(2,1)S(1)} %get-tuple-element.51), channel_id=1, source_target_pairs={{0,8},{8,0},{16,24},{24,16},{1,9},{9,1},{17,25},{25,17},{2,10},{10... | collective-permute-start | bytes 98312 | tf_op jit(solution)/shard_map/ppermute | solution.py:346
  23.7 1.5 %collective-permute-start.3 = (bf16[2,4,16,128]{3,2,1,0:T(8,128)(2,1)S(1)}, bf16[2,4,16,128]{3,2,1,0:T(8,128)(2,1)S(1)}, u32[]{:S(2)}, u32[]{:S(2)}) collective-permute-start(bf16[2,4,16,128]{3,2,1,0:T(8,128)(2,1)S(1)} %get-tuple-element.53), channel_id=1, source_target_pairs={{0,24},{8,16},{16,8},{24,0},{1,25},{9,17},{17,9},{25,1},{2,26},{10... | collective-permute-start | bytes 98312 | tf_op jit(solution)/shard_map/ppermute | solution.py:346
  25.3 3.2 %shard_map.65 = (f32[2048,128]{1,0:T(8,128)}, f32[2048,128]{1,0:T(8,128)}, bf16[512,128]{1,0:T(8,128)(2,1)S(1)}, f32[2,128,128]{2,1,0:T(8,128)S(1)}) custom-call(f32[64,32,128]{2,1,0:T(8,128)} %pair_hbm.3, f32[2,128]{1,0:T(2,128)S(1)} %copy-done.7, bf16[2,128,128]{2,1,0:T(8,128)(2,1)S(1)} %copy-done.6, bf16[2,128,512]{2,1,0:T(8,128)(2,1)S(1)} %copy-done.4, ...), custom_call_target="tpu_custom_call" | custom-call | flops 67108864 | bytes 3737600 | tf_op jit(solution)/shard_map/pallas_call | solution.py:330
  28.4 4.4 %all-to-all-done.recv_ref = bf16[32,2,3,16,128]{4,3,2,1,0:T(8,128)(2,1)S(1)} async-done(((bf16[32,2,3,16,128]{4,3,2,1,0:T(8,128)(2,1)}), bf16[32,2,3,16,128]{4,3,2,1,0:T(8,128)(2,1)S(1)}, u32[]{:S(2)}, u32[]{:S(2)}) %all-to-all-start) | async-done | bytes 786464 | tf_op jit(solution)/shard_map/all_to_all | solution.py:394
  32.9 1.2 %shard_map.66 = bf16[32,5,16,128]{3,2,1,0:T(8,128)(2,1)S(1)} custom-call(bf16[32,2,3,16,128]{4,3,2,1,0:T(8,128)(2,1)S(1)} %all-to-all-done.recv_ref, bf16[2,4,16,128]{3,2,1,0:T(8,128)(2,1)S(1)} %get-tuple-element.50.refs_0_, bf16[2,4,16,128]{3,2,1,0:T(8,128)(2,1)S(1)} %collective-permute-done.1.refs_1_, ...), custom_call_target="tpu_custom_call" | custom-call | flops 134217728 | bytes 1703936 | tf_op jit(solution)/shard_map/pallas_call | solution.py:330
  34.1 21.2 %all_to_all.20 = bf16[32,5,16,128]{3,2,1,0:T(8,128)(2,1)S(1)} all-to-all(bf16[32,5,16,128]{3,2,1,0:T(8,128)(2,1)S(1)} %shard_map.66), channel_id=1, replica_groups=mesh['row'=4,'half'=2,'rest'=4] {'row','half','rest'}, dimensions={0} | all-to-all | bytes 1310720 | tf_op jit(solution)/shard_map/all_to_all | solution.py:420
  55.3 3.3 %shard_map.67 = (f32[2048,128]{1,0:T(8,128)}, bf16[4,2,4,8,16,128]{5,4,3,2,1,0:T(8,128)(2,1)}, bf16[4,2,8,16,128]{4,3,2,1,0:T(8,128)(2,1)}, bf16[4,2,8,16,128]{4,3,2,1,0:T(8,128)(2,1)}) custom-call(f32[2048,128]{1,0:T(8,128)S(1)} %copy-done.2, bf16[4,2,4,5,16,128]{5,4,3,2,1,0:T(8,128)(2,1)S(1)} %bitcast.45, f32[2048,128]{1,0:T(8,128)S(1)} %copy-done.3, ...), custom_call_target="tpu_custom_call" | custom-call | flops 335544320 | bytes 5702656 | tf_op jit(solution)/shard_map/pallas_call | solution.py:330
  58.5 2.8 %all-to-all-start.2 = ((bf16[32,8,16,128]{3,2,1,0:T(8,128)(2,1)}), bf16[32,8,16,128]{3,2,1,0:T(8,128)(2,1)S(1)}, u32[]{:S(2)}, u32[]{:S(2)}) async-start(bf16[32,8,16,128]{3,2,1,0:T(8,128)(2,1)} %bitcast.47), calls=%async_computation.2 | async-start | bytes 2097152 | tf_op jit(solution)/shard_map/all_to_all | solution.py:437
  61.5 1.4 %collective-permute-done.8 = bf16[4,2,8,16,128]{4,3,2,1,0:T(8,128)(2,1)S(1)} collective-permute-done((bf16[4,2,8,16,128]{4,3,2,1,0:T(8,128)(2,1)S(1)}, bf16[4,2,8,16,128]{4,3,2,1,0:T(8,128)(2,1)S(1)}, u32[]{:S(2)}, u32[]{:S(2)}) %collective-permute-start.8) | collective-permute-done | bytes 262176 | tf_op jit(solution)/shard_map/ppermute | solution.py:346
  63.0 1.7 %collective-permute-start.12 = (bf16[2,8,16,128]{3,2,1,0:T(8,128)(2,1)S(1)}, bf16[2,8,16,128]{3,2,1,0:T(8,128)(2,1)S(1)}, u32[]{:S(2)}, u32[]{:S(2)}) collective-permute-start(bf16[2,8,16,128]{3,2,1,0:T(8,128)(2,1)S(1)} %get-tuple-element.46), channel_id=1, source_target_pairs={{0,8},{8,0},{16,24},{24,16},{1,9},{9,1},{17,25},{25,17},{2,10},{10... | collective-permute-start | bytes 196616 | tf_op jit(solution)/shard_map/ppermute | solution.py:346
  64.7 1.5 %collective-permute-start.14 = (bf16[2,8,16,128]{3,2,1,0:T(8,128)(2,1)S(1)}, bf16[2,8,16,128]{3,2,1,0:T(8,128)(2,1)S(1)}, u32[]{:S(2)}, u32[]{:S(2)}) collective-permute-start(bf16[2,8,16,128]{3,2,1,0:T(8,128)(2,1)S(1)} %get-tuple-element.47), channel_id=1, source_target_pairs={{0,24},{8,16},{16,8},{24,0},{1,25},{9,17},{17,9},{25,1},{2,26},{10... | collective-permute-start | bytes 196616 | tf_op jit(solution)/shard_map/ppermute | solution.py:346
  66.6 5.4 %collective-permute-done.12 = bf16[2,8,16,128]{3,2,1,0:T(8,128)(2,1)S(1)} collective-permute-done((bf16[2,8,16,128]{3,2,1,0:T(8,128)(2,1)S(1)}, bf16[2,8,16,128]{3,2,1,0:T(8,128)(2,1)S(1)}, u32[]{:S(2)}, u32[]{:S(2)}) %collective-permute-start.12) | collective-permute-done | bytes 65568 | tf_op jit(solution)/shard_map/ppermute | solution.py:346
  71.9 3.2 %collective-permute-done.14 = bf16[2,8,16,128]{3,2,1,0:T(8,128)(2,1)S(1)} collective-permute-done((bf16[2,8,16,128]{3,2,1,0:T(8,128)(2,1)S(1)}, bf16[2,8,16,128]{3,2,1,0:T(8,128)(2,1)S(1)}, u32[]{:S(2)}, u32[]{:S(2)}) %collective-permute-start.14) | collective-permute-done | bytes 65568 | tf_op jit(solution)/shard_map/ppermute | solution.py:346
  77.0 2.7 %collective-permute-start.11 = (bf16[2,8,16,128]{3,2,1,0:T(8,128)(2,1)S(1)}, bf16[2,8,16,128]{3,2,1,0:T(8,128)(2,1)S(1)}, u32[]{:S(2)}, u32[]{:S(2)}) collective-permute-start(bf16[2,8,16,128]{3,2,1,0:T(8,128)(2,1)S(1)} %get-tuple-element.45), channel_id=1, source_target_pairs={{0,24},{8,16},{16,8},{24,0},{1,25},{9,17},{17,9},{25,1},{2,26},{10... | collective-permute-start | bytes 196616 | tf_op jit(solution)/shard_map/ppermute | solution.py:346
  79.6 3.0 %shard_map.68.gate_ref = f32[2048,128]{1,0:T(8,128)} custom-call(f32[2048,128]{1,0:T(8,128)} %get-tuple-element.35.first_hbm.first_ref, f32[2,128]{1,0:T(2,128)S(1)} %copy-done.7, bf16[2,128,128]{2,1,0:T(8,128)(2,1)S(1)} %copy-done.6), custom_call_target="tpu_custom_call" | custom-call | flops 67108864 | bytes 2163712 | tf_op jit(solution)/shard_map/pallas_call | solution.py:330
  82.6 6.3 %all-to-all-done.2.recv_ref = bf16[32,8,16,128]{3,2,1,0:T(8,128)(2,1)S(1)} async-done(((bf16[32,8,16,128]{3,2,1,0:T(8,128)(2,1)}), bf16[32,8,16,128]{3,2,1,0:T(8,128)(2,1)S(1)}, u32[]{:S(2)}, u32[]{:S(2)}) %all-to-all-start.2) | async-done | bytes 1048608 | tf_op jit(solution)/shard_map/all_to_all | solution.py:437
  89.8 13.3 %all_to_all.21 = bf16[16,8,16,128]{3,2,1,0:T(8,128)(2,1)S(1)} all-to-all(bf16[16,8,16,128]{3,2,1,0:T(8,128)(2,1)S(1)} %shard_map.69), channel_id=1, replica_groups=mesh['row'=4,'half'=2,'rest'=4] {'row','rest'}, dimensions={0} | all-to-all | bytes 1048576 | tf_op jit(solution)/shard_map/all_to_all | solution.py:457
  103.1 1.7 %shard_map.70 = f32[64,32,128]{2,1,0:T(8,128)} custom-call(f32[2048,128]{1,0:T(8,128)S(1)} %copy-done, bf16[128,16,128]{2,1,0:T(8,128)(2,1)S(1)} %bitcast.46, f32[2048,128]{1,0:T(8,128)S(1)} %copy-done.1, f32[2,128,128]{2,1,0:T(8,128)S(1)} %get-tuple-element.33.gain_cols_ref, bf16[2,128,128]{2,1,0:T(8,128)(2,1)S(1)} %copy-done.5), custom_call_target="tpu_custom_call" | custom-call | flops 67108864 | bytes 3866624 | tf_op jit(solution)/shard_map/pallas_call | solution.py:330
  (51 shorter events, 6.6 us)
Async XLA Ops:
  3.6 29.3 %all-to-all-start = ((bf16[32,2,3,16,128]{4,3,2,1,0:T(8,128)(2,1)}), bf16[32,2,3,16,128]{4,3,2,1,0:T(8,128)(2,1)S(1)}, u32[]{:S(2)}, u32[]{:S(2)}) async-start(bf16[32,2,3,16,128]{4,3,2,1,0:T(8,128)(2,1)} %get-tuple-element.23), calls=%async_computation | async-start | bytes 1572864 | tf_op jit(solution)/shard_map/all_to_all | solution.py:394
  10.9 1.4 %collective-permute-start = (bf16[4,2,4,16,128]{4,3,2,1,0:T(8,128)(2,1)S(1)}, bf16[4,2,4,16,128]{4,3,2,1,0:T(8,128)(2,1)S(1)}, u32[]{:S(2)}, u32[]{:S(2)}) collective-permute-start(bf16[4,2,4,16,128]{4,3,2,1,0:T(8,128)(2,1)S(1)} %copy-done.12), channel_id=1, source_target_pairs={{0,1},{1,0},{2,3},{3,2},{4,5},{5,4},{6,7},{7,6},{8,9},{9,8},{10,11... | collective-permute-start | bytes 393224 | tf_op jit(solution)/shard_map/ppermute | solution.py:346
  12.3 13.0 %copy-start.6 = (bf16[2,128,128]{2,1,0:T(8,128)(2,1)S(1)}, bf16[2,128,128]{2,1,0:T(8,128)(2,1)}, u32[]{:S(2)}) copy-start(bf16[2,128,128]{2,1,0:T(8,128)(2,1)} %w_gate_ref.3) | copy-start | bytes 196612
  12.3 5.9 %collective-permute-start.4 = (bf16[2,4,16,128]{3,2,1,0:T(8,128)(2,1)S(1)}, bf16[2,4,16,128]{3,2,1,0:T(8,128)(2,1)S(1)}, u32[]{:S(2)}, u32[]{:S(2)}) collective-permute-start(bf16[2,4,16,128]{3,2,1,0:T(8,128)(2,1)S(1)} %get-tuple-element.54), channel_id=1, source_target_pairs={{0,8},{8,0},{16,24},{24,16},{1,9},{9,1},{17,25},{25,17},{2,10},{10... | collective-permute-start | bytes 98312 | tf_op jit(solution)/shard_map/ppermute | solution.py:346
  14.2 6.5 %collective-permute-start.6 = (bf16[2,4,16,128]{3,2,1,0:T(8,128)(2,1)S(1)}, bf16[2,4,16,128]{3,2,1,0:T(8,128)(2,1)S(1)}, u32[]{:S(2)}, u32[]{:S(2)}) collective-permute-start(bf16[2,4,16,128]{3,2,1,0:T(8,128)(2,1)S(1)} %get-tuple-element.55), channel_id=1, source_target_pairs={{0,24},{8,16},{16,8},{24,0},{1,25},{9,17},{17,9},{25,1},{2,26},{10... | collective-permute-start | bytes 98312 | tf_op jit(solution)/shard_map/ppermute | solution.py:346
  15.6 5.5 %collective-permute-start.5 = (bf16[2,4,16,128]{3,2,1,0:T(8,128)(2,1)S(1)}, bf16[2,4,16,128]{3,2,1,0:T(8,128)(2,1)S(1)}, u32[]{:S(2)}, u32[]{:S(2)}) collective-permute-start(bf16[2,4,16,128]{3,2,1,0:T(8,128)(2,1)S(1)} %get-tuple-element.56), channel_id=1, source_target_pairs={{0,16},{8,24},{16,0},{24,8},{1,17},{9,25},{17,1},{25,9},{2,18},{10... | collective-permute-start | bytes 98312 | tf_op jit(solution)/shard_map/ppermute | solution.py:346
  21.1 11.7 %collective-permute-start.7 = (bf16[4,2,4,16,128]{4,3,2,1,0:T(8,128)(2,1)S(1)}, bf16[4,2,4,16,128]{4,3,2,1,0:T(8,128)(2,1)S(1)}, u32[]{:S(2)}, u32[]{:S(2)}) collective-permute-start(bf16[4,2,4,16,128]{4,3,2,1,0:T(8,128)(2,1)S(1)} %pad_maximum_fusion.1), channel_id=1, source_target_pairs={{0,2},{1,3},{2,0},{3,1},{4,6},{5,7},{6,4},{7,5},{8,10},{9,11},{10,... | collective-permute-start | bytes 393224 | tf_op jit(solution)/shard_map/ppermute | solution.py:346
  21.8 11.0 %collective-permute-start.1 = (bf16[2,4,16,128]{3,2,1,0:T(8,128)(2,1)S(1)}, bf16[2,4,16,128]{3,2,1,0:T(8,128)(2,1)S(1)}, u32[]{:S(2)}, u32[]{:S(2)}) collective-permute-start(bf16[2,4,16,128]{3,2,1,0:T(8,128)(2,1)S(1)} %get-tuple-element.51), channel_id=1, source_target_pairs={{0,8},{8,0},{16,24},{24,16},{1,9},{9,1},{17,25},{25,17},{2,10},{10... | collective-permute-start | bytes 98312 | tf_op jit(solution)/shard_map/ppermute | solution.py:346
  23.2 9.7 %collective-permute-start.2 = (bf16[2,4,16,128]{3,2,1,0:T(8,128)(2,1)S(1)}, bf16[2,4,16,128]{3,2,1,0:T(8,128)(2,1)S(1)}, u32[]{:S(2)}, u32[]{:S(2)}) collective-permute-start(bf16[2,4,16,128]{3,2,1,0:T(8,128)(2,1)S(1)} %get-tuple-element.52), channel_id=1, source_target_pairs={{0,16},{8,24},{16,0},{24,8},{1,17},{9,25},{17,1},{25,9},{2,18},{10... | collective-permute-start | bytes 98312 | tf_op jit(solution)/shard_map/ppermute | solution.py:346
  23.7 9.1 %collective-permute-start.3 = (bf16[2,4,16,128]{3,2,1,0:T(8,128)(2,1)S(1)}, bf16[2,4,16,128]{3,2,1,0:T(8,128)(2,1)S(1)}, u32[]{:S(2)}, u32[]{:S(2)}) collective-permute-start(bf16[2,4,16,128]{3,2,1,0:T(8,128)(2,1)S(1)} %get-tuple-element.53), channel_id=1, source_target_pairs={{0,24},{8,16},{16,8},{24,0},{1,25},{9,17},{17,9},{25,1},{2,26},{10... | collective-permute-start | bytes 98312 | tf_op jit(solution)/shard_map/ppermute | solution.py:346
  32.9 22.4 %copy-start.3 = (f32[2048,128]{1,0:T(8,128)S(1)}, f32[2048,128]{1,0:T(8,128)}, u32[]{:S(2)}) copy-start(f32[2048,128]{1,0:T(8,128)} %get-tuple-element.32.gate_ref) | copy-start | bytes 3145732
  34.0 21.2 %copy-start.2 = (f32[2048,128]{1,0:T(8,128)S(1)}, f32[2048,128]{1,0:T(8,128)}, u32[]{:S(2)}) copy-start(f32[2048,128]{1,0:T(8,128)} %get-tuple-element.28.ordered_ref) | copy-start | bytes 3145732
  34.0 21.2 %copy-start.5 = (bf16[2,128,128]{2,1,0:T(8,128)(2,1)S(1)}, bf16[2,128,128]{2,1,0:T(8,128)(2,1)}, u32[]{:S(2)}) copy-start(bf16[2,128,128]{2,1,0:T(8,128)(2,1)} %w_out_ref.3) | copy-start | bytes 196612
  58.5 30.4 %all-to-all-start.2 = ((bf16[32,8,16,128]{3,2,1,0:T(8,128)(2,1)}), bf16[32,8,16,128]{3,2,1,0:T(8,128)(2,1)S(1)}, u32[]{:S(2)}, u32[]{:S(2)}) async-start(bf16[32,8,16,128]{3,2,1,0:T(8,128)(2,1)} %bitcast.47), calls=%async_computation.2 | async-start | bytes 2097152 | tf_op jit(solution)/shard_map/all_to_all | solution.py:437
  61.3 1.6 %collective-permute-start.8 = (bf16[4,2,8,16,128]{4,3,2,1,0:T(8,128)(2,1)S(1)}, bf16[4,2,8,16,128]{4,3,2,1,0:T(8,128)(2,1)S(1)}, u32[]{:S(2)}, u32[]{:S(2)}) collective-permute-start(bf16[4,2,8,16,128]{4,3,2,1,0:T(8,128)(2,1)S(1)} %copy-done.11), channel_id=1, source_target_pairs={{0,1},{1,0},{2,3},{3,2},{4,5},{5,4},{6,7},{7,6},{8,9},{9,8},{10,11... | collective-permute-start | bytes 786440 | tf_op jit(solution)/shard_map/ppermute | solution.py:346
  63.0 8.9 %collective-permute-start.12 = (bf16[2,8,16,128]{3,2,1,0:T(8,128)(2,1)S(1)}, bf16[2,8,16,128]{3,2,1,0:T(8,128)(2,1)S(1)}, u32[]{:S(2)}, u32[]{:S(2)}) collective-permute-start(bf16[2,8,16,128]{3,2,1,0:T(8,128)(2,1)S(1)} %get-tuple-element.46), channel_id=1, source_target_pairs={{0,8},{8,0},{16,24},{24,16},{1,9},{9,1},{17,25},{25,17},{2,10},{10... | collective-permute-start | bytes 196616 | tf_op jit(solution)/shard_map/ppermute | solution.py:346
  64.7 10.5 %collective-permute-start.14 = (bf16[2,8,16,128]{3,2,1,0:T(8,128)(2,1)S(1)}, bf16[2,8,16,128]{3,2,1,0:T(8,128)(2,1)S(1)}, u32[]{:S(2)}, u32[]{:S(2)}) collective-permute-start(bf16[2,8,16,128]{3,2,1,0:T(8,128)(2,1)S(1)} %get-tuple-element.47), channel_id=1, source_target_pairs={{0,24},{8,16},{16,8},{24,0},{1,25},{9,17},{17,9},{25,1},{2,26},{10... | collective-permute-start | bytes 196616 | tf_op jit(solution)/shard_map/ppermute | solution.py:346
  66.2 9.0 %collective-permute-start.13 = (bf16[2,8,16,128]{3,2,1,0:T(8,128)(2,1)S(1)}, bf16[2,8,16,128]{3,2,1,0:T(8,128)(2,1)S(1)}, u32[]{:S(2)}, u32[]{:S(2)}) collective-permute-start(bf16[2,8,16,128]{3,2,1,0:T(8,128)(2,1)S(1)} %get-tuple-element.48), channel_id=1, source_target_pairs={{0,16},{8,24},{16,0},{24,8},{1,17},{9,25},{17,1},{25,9},{2,18},{10... | collective-permute-start | bytes 196616 | tf_op jit(solution)/shard_map/ppermute | solution.py:346
  75.2 13.7 %collective-permute-start.15 = (bf16[4,2,8,16,128]{4,3,2,1,0:T(8,128)(2,1)S(1)}, bf16[4,2,8,16,128]{4,3,2,1,0:T(8,128)(2,1)S(1)}, u32[]{:S(2)}, u32[]{:S(2)}) collective-permute-start(bf16[4,2,8,16,128]{4,3,2,1,0:T(8,128)(2,1)S(1)} %pad_maximum_fusion), channel_id=1, source_target_pairs={{0,2},{1,3},{2,0},{3,1},{4,6},{5,7},{6,4},{7,5},{8,10},{9,11},{10,... | collective-permute-start | bytes 786440 | tf_op jit(solution)/shard_map/ppermute | solution.py:346
  76.2 12.8 %collective-permute-start.9 = (bf16[2,8,16,128]{3,2,1,0:T(8,128)(2,1)S(1)}, bf16[2,8,16,128]{3,2,1,0:T(8,128)(2,1)S(1)}, u32[]{:S(2)}, u32[]{:S(2)}) collective-permute-start(bf16[2,8,16,128]{3,2,1,0:T(8,128)(2,1)S(1)} %get-tuple-element.43), channel_id=1, source_target_pairs={{0,8},{8,0},{16,24},{24,16},{1,9},{9,1},{17,25},{25,17},{2,10},{10... | collective-permute-start | bytes 196616 | tf_op jit(solution)/shard_map/ppermute | solution.py:346
  76.3 12.6 %collective-permute-start.10 = (bf16[2,8,16,128]{3,2,1,0:T(8,128)(2,1)S(1)}, bf16[2,8,16,128]{3,2,1,0:T(8,128)(2,1)S(1)}, u32[]{:S(2)}, u32[]{:S(2)}) collective-permute-start(bf16[2,8,16,128]{3,2,1,0:T(8,128)(2,1)S(1)} %get-tuple-element.44), channel_id=1, source_target_pairs={{0,16},{8,24},{16,0},{24,8},{1,17},{9,25},{17,1},{25,9},{2,18},{10... | collective-permute-start | bytes 196616 | tf_op jit(solution)/shard_map/ppermute | solution.py:346
  77.0 12.0 %collective-permute-start.11 = (bf16[2,8,16,128]{3,2,1,0:T(8,128)(2,1)S(1)}, bf16[2,8,16,128]{3,2,1,0:T(8,128)(2,1)S(1)}, u32[]{:S(2)}, u32[]{:S(2)}) collective-permute-start(bf16[2,8,16,128]{3,2,1,0:T(8,128)(2,1)S(1)} %get-tuple-element.45), channel_id=1, source_target_pairs={{0,24},{8,16},{16,8},{24,0},{1,25},{9,17},{17,9},{25,1},{2,26},{10... | collective-permute-start | bytes 196616 | tf_op jit(solution)/shard_map/ppermute | solution.py:346
  88.9 14.1 %copy-start.1 = (f32[2048,128]{1,0:T(8,128)S(1)}, f32[2048,128]{1,0:T(8,128)}, u32[]{:S(2)}) copy-start(f32[2048,128]{1,0:T(8,128)} %shard_map.68.gate_ref) | copy-start | bytes 3145732
  89.8 13.3 %copy-start = (f32[2048,128]{1,0:T(8,128)S(1)}, f32[2048,128]{1,0:T(8,128)}, u32[]{:S(2)}) copy-start(f32[2048,128]{1,0:T(8,128)} %get-tuple-element.35.first_hbm.first_ref) | copy-start | bytes 3145732
  (7 other events, 40.5 us)

commit v7 on v6

--- a/solution.py
+++ b/solution.py
@@ -180,20 +180,27 @@
             )
 
 
-def outgoing_kernel(cols, first, shared, recv_ref, *refs):
-    if shared:
-        *part_refs, out_ref, left, right, half_left, half_right, b_ref = refs
-    else:
-        out_ref, left, right = refs
+def transposed_product(left, right):
+    return lax.dot_general(
+        right[...], left[...], (((0,), (0,)), ((), ())), preferred_element_type=F32
+    ).astype(BF16)
+
+
+def outgoing_half_kernel(cols, first, *refs):
+    *part_refs, out_ref, left, right, b_ref = refs
+    rows, depth = out_ref.shape[0] // cols, out_ref.shape[1]
+    stage(part_refs, b_ref)
+    for h in range(depth):
+        dense_half(b_ref, h, first, left)
+        dense_half(b_ref, depth + h, first, right)
+        scatter_product(transposed_product(left, right), rows, cols, first, h, out_ref)
+
+
+def outgoing_kernel(cols, first, recv_ref, *refs):
+    *half_ref, out_ref, left, right = refs
     ndev, _, depth, n1, _ = recv_ref.shape
     split = LANES // first
     rows = ndev // cols
-
-    def product(left, right):
-        return lax.dot_general(
-            right[...], left[...], (((0,), (0,)), ((), ())), preferred_element_type=F32
-        ).astype(BF16)
-
     for h in range(depth):
         for side, dense in ((0, left), (1, right)):
             for c in range(cols):
@@ -206,13 +213,9 @@
                         ],
                         axis=1,
                     )
-        scatter_product(product(left, right), rows, cols, first, h, out_ref)
-    if shared:
-        stage(part_refs, b_ref)
-        for h in range(2 * shared):
-            dense_half(b_ref, h, first, half_left)
-            dense_half(b_ref, 2 * shared + h, first, half_right)
-            scatter_product(product(half_left, half_right), rows, cols, first, depth + h, out_ref)
+        scatter_product(transposed_product(left, right), rows, cols, first, h, out_ref)
+    for ref in half_ref:
+        out_ref[:, depth:] = ref[...]
 
 
 def scatter_product(summed, rows, cols, first, h, out_ref):
@@ -229,12 +232,17 @@
             )
 
 
-def incoming_kernel(cols, first, recv_ref, *refs):
-    *part_refs, out_ref, left, right, b_ref = refs
+def incoming_layout_kernel(first, *refs):
+    *part_refs, dense_ref, b_ref = refs
+    stage(part_refs, b_ref)
+    for h in range(dense_ref.shape[0]):
+        dense_half(b_ref, h, first, dense_ref.at[h])
+
+
+def incoming_kernel(cols, first, recv_ref, dense_ref, out_ref, left):
     ndev, depth, n1, _ = recv_ref.shape
     split = LANES // first
     rows = ndev // cols
-    stage(part_refs, b_ref)
     for h in range(depth):
         for c in range(cols):
             for l in range(split):
@@ -242,9 +250,8 @@
                 left[at : at + n1, :] = jnp.concatenate(
                     [recv_ref[r * cols + c, h, :, l * first : (l + 1) * first] for r in range(rows)], axis=1
                 )
-        dense_half(b_ref, h, first, right)
         summed = lax.dot_general(
-            right[...], left[...], (((1,), (1,)), ((), ())), preferred_element_type=F32
+            dense_ref[h], left[...], (((1,), (1,)), ((), ())), preferred_element_type=F32
         ).astype(BF16)
         scatter_product(summed, rows, cols // 2, first, h, out_ref)
 
@@ -267,7 +274,8 @@
     ordered_ref, summed_ref, gate_ref, gain_cols_ref, w_out_ref, gain_ref, w_t_ref,
     first_hbm, send_hbm, keep_hbm, swap_hbm, normal, planes, first_ref, send_ref, b_ref, sems,
 ):
-    rows, halves, rest, depth, n1, _ = send_ref.shape
+    rows, rest, depth, n1, _ = send_ref.shape
+    halves = send_hbm.shape[1]
     hidden = rows * rest * depth
     copies = []
 
@@ -292,14 +300,12 @@
     leave(b_ref.at[0], keep_hbm)
     for r in range(rows):
         for c in range(rest):
-            at = (r * rest + c) * depth
             for h in range(depth):
-                value = plane(planes, n1, at + h)
-                for half in range(halves):
-                    send_ref[r, half, c, h] = value
+                send_ref[r, c, h] = plane(planes, n1, (r * rest + c) * depth + h)
         if r % (rows // 2) == rows // 2 - 1:
             own = pl.ds(r + 1 - rows // 2, rows // 2)
-            leave(send_ref.at[own], send_hbm.at[own])
+            for half in range(halves):
+                leave(send_ref.at[own], send_hbm.at[own, half])
     for copy in copies:
         copy.wait()
 
@@ -405,17 +411,24 @@
         pair, norm_in_gain, w_gate, w_proj, norm_out_gain,
         pinned=[pltpu.HBM] + [None] * 4, spaces=[pltpu.HBM, pltpu.HBM, None, None],
     )
-    recv, (ordered, gate, w_t, gain_cols) = lax.optimization_barrier((recv, prepared))
-    half_scratch = [
-        pltpu.VMEM((rest * second, total), BF16),
-        pltpu.VMEM((rest * second, total), BF16),
-        pltpu.VMEM((rest // 2, rows, 2, 4 * shared, n1, LANES), BF16),
-    ]
+    halves = []
+    if shared:
+        halves = call(
+            functools.partial(outgoing_half_kernel, cols, first),
+            [shaped(ndev, 2 * shared)],
+            [
+                pltpu.VMEM((rest * second, total), BF16),
+                pltpu.VMEM((rest * second, total), BF16),
+                pltpu.VMEM((rest // 2, rows, 2, 4 * shared, n1, LANES), BF16),
+            ],
+            tri_flops // 4, *spread(*swaps),
+        )
+    recv, halves, (ordered, gate, w_t, gain_cols) = lax.optimization_barrier((recv, halves, prepared))
     (product,) = call(
-        functools.partial(outgoing_kernel, cols, first, shared),
+        functools.partial(outgoing_kernel, cols, first),
         [shaped(ndev, depth + 2 * shared)],
-        [pltpu.VMEM((cols * second, total), BF16)] * 2 + (half_scratch if shared else []),
-        tri_flops, recv, *(spread(*swaps) if shared else []),
+        [pltpu.VMEM((cols * second, total), BF16)] * 2,
+        tri_flops, recv, *halves,
     )
     summed = lax.all_to_all(product, ("row", "half", "rest"), 0, 0, tiled=True)
     send_shape, b_shape = shaped(rows, 2, rest, half_depth), shaped(rows, rest // 2, half_depth)
@@ -426,9 +439,9 @@
             normal,
             planes,
             pltpu.VMEM(flat_shape.shape, F32),
-            pltpu.VMEM(send_shape.shape, BF16),
+            pltpu.VMEM((rows, rest, half_depth, n1, LANES), BF16),
             pltpu.VMEM((2,) + b_shape.shape, BF16),
-            pltpu.SemaphoreType.DMA((5,)),
+            pltpu.SemaphoreType.DMA((7,)),
         ],
         proj_flops + gate_flops,
         ordered, summed.reshape(rows, 2, rest, depth + 2 * shared, n1, LANES), gate, gain_cols, w_out, norm_in_gain, w_t,
@@ -443,16 +456,17 @@
         gate_flops, middle, norm_in_gain, w_gate,
         pinned=[pltpu.HBM, None, None], spaces=[pltpu.HBM],
     )
-    recv, gate = lax.optimization_barrier((recv, gate))
+    dense = call(
+        functools.partial(incoming_layout_kernel, first),
+        [jax.ShapeDtypeStruct((half_depth, rest * second, total), BF16)],
+        [pltpu.VMEM((rest // 2, rows, 2, half_depth, n1, LANES), BF16)],
+        0, *spread(keep, swap),
+    )
+    recv, gate, dense = lax.optimization_barrier((recv, gate, dense))
     (product,) = call(
         functools.partial(incoming_kernel, cols, first),
-        [shaped(rows * rest, half_depth)],
-        [
-            pltpu.VMEM((cols * second, total), BF16),
-            pltpu.VMEM((rest * second, total), BF16),
-            pltpu.VMEM((rest // 2, rows, 2, half_depth, n1, LANES), BF16),
-        ],
-        tri_flops, recv, *spread(keep, swap),
+        [shaped(rows * rest, half_depth)], [pltpu.VMEM((cols * second, total), BF16)],
+        tri_flops, recv, *dense,
     )
     summed = lax.all_to_all(product, ("row", "rest"), 0, 0, tiled=True)
     (updated,) = call(

time: 105 us -> 105 us (level)
    ppermute x16, waiting for transfers between devices: 16.4 us -> 22.8 us  [swapped(): lax.ppermute(x, axis, [(d, d ^ apart) for d in range(size)])]
    all_to_all x1, waiting for transfers between devices: 6.29 us -> 0.42 us  [body(): lax.all_to_all(send.reshape(ndev, half_depth, n1, LANES), ('row', 'half',...]
    all_to_all x1, waiting for transfers between devices: 4.38 us -> 3.05 us  [body(): recv = lax.all_to_all(send, ('row', 'half', 'rest'), 0, 0, tiled=True)]
    pallas_call x7 -> x9, Pallas kernels: 16.6 us -> 16.7 us  [call(): pl.pallas_call(kernel, out_shape=outs, in_specs=in_specs, out_specs=out_s...]
  transfers between devices with their start and end apart: 18 -> 18, of which waited for: 9 -> 12; matrix products, arithmetic and copies ran while one was open for 0% -> 0% of each run, Pallas kernels for 6% -> 7%
where the time goes in v7:
time: 105 us; the launch traced here: 104 us
  blocking collectives  34.5 us (33%)
  starting transfers between devices  26.3 us (25%)
  waiting for transfers between devices  26.3 us (25%)
  Pallas kernels  16.7 us (16%)
    ppermute x16, waiting for transfers between devices, swapped(): lax.ppermute(x, axis, [(d, d ^ apart) for d in range(size)])  22.8 us
    all_to_all x1, blocking collectives, body(): summed = lax.all_to_all(product, ('row', 'half', 'rest'), 0, 0, tiled=True)  21.2 us
    pallas_call x9, Pallas kernels, call(): pl.pallas_call(kernel, out_shape=outs, in_specs=in_specs, out_specs=out_s...  16.7 us
    ppermute x16, starting transfers between devices, swapped(): lax.ppermute(x, axis, [(d, d ^ apart) for d in range(size)])  16.2 us
    all_to_all x1, blocking collectives, body(): summed = lax.all_to_all(product, ('row', 'rest'), 0, 0, tiled=True)  13.3 us
    all_to_all x1, starting transfers between devices, body(): recv = lax.all_to_all(send, ('row', 'half', 'rest'), 0, 0, tiled=True)  7.29 us
    all_to_all x1, waiting for transfers between devices, body(): recv = lax.all_to_all(send, ('row', 'half', 'rest'), 0, 0, tiled=True)  3.05 us
    all_to_all x1, starting transfers between devices, body(): lax.all_to_all(send.reshape(ndev, half_depth, n1, LANES), ('row', 'half',...  2.79 us
  transfers between devices with their start and end apart: 18, of which 12 were waited for; matrix products, arithmetic and copies ran while one was open for 0% of the time, Pallas kernels for 7%

profile of v7, /device:TPU:0, one launch (start us, length us, event | category | flops | bytes accessed | tf_op | source)
XLA Modules:
  0.0 104.1 jit_solution(13102264598597805291)
XLA Ops:
  0.0 3.5 %shard_map.64 = (bf16[32,2,3,16,128]{4,3,2,1,0:T(8,128)(2,1)}, bf16[4,2,4,16,128]{4,3,2,1,0:T(8,128)(2,1)}, bf16[4,2,4,16,128]{4,3,2,1,0:T(8,128)(2,1)}) custom-call(f32[64,32,128]{2,1,0:T(8,128)} %pair_hbm.3, f32[2,128]{1,0:T(2,128)} %gain_ref.5, bf16[2,128,512]{2,1,0:T(8,128)(2,1)} %w_ref.1), custom_call_target="tpu_custom_call" | custom-call | flops 268435456 | bytes 2360320 | tf_op jit(solution)/shard_map/pallas_call | solution.py:336
  3.6 7.3 %all-to-all-start = ((bf16[32,2,3,16,128]{4,3,2,1,0:T(8,128)(2,1)}), bf16[32,2,3,16,128]{4,3,2,1,0:T(8,128)(2,1)S(1)}, u32[]{:S(2)}, u32[]{:S(2)}) async-start(bf16[32,2,3,16,128]{4,3,2,1,0:T(8,128)(2,1)} %get-tuple-element.25), calls=%async_computation | async-start | bytes 1572864 | tf_op jit(solution)/shard_map/all_to_all | solution.py:400
  11.2 1.1 %collective-permute-done = bf16[4,2,4,16,128]{4,3,2,1,0:T(8,128)(2,1)S(1)} collective-permute-done((bf16[4,2,4,16,128]{4,3,2,1,0:T(8,128)(2,1)S(1)}, bf16[4,2,4,16,128]{4,3,2,1,0:T(8,128)(2,1)S(1)}, u32[]{:S(2)}, u32[]{:S(2)}) %collective-permute-start) | collective-permute-done | bytes 131104 | tf_op jit(solution)/shard_map/ppermute | solution.py:352
  12.3 1.8 %collective-permute-start.4 = (bf16[2,4,16,128]{3,2,1,0:T(8,128)(2,1)S(1)}, bf16[2,4,16,128]{3,2,1,0:T(8,128)(2,1)S(1)}, u32[]{:S(2)}, u32[]{:S(2)}) collective-permute-start(bf16[2,4,16,128]{3,2,1,0:T(8,128)(2,1)S(1)} %get-tuple-element.58), channel_id=1, source_target_pairs={{0,8},{8,0},{16,24},{24,16},{1,9},{9,1},{17,25},{25,17},{2,10},{10... | collective-permute-start | bytes 98312 | tf_op jit(solution)/shard_map/ppermute | solution.py:352
  14.2 1.5 %collective-permute-start.6 = (bf16[2,4,16,128]{3,2,1,0:T(8,128)(2,1)S(1)}, bf16[2,4,16,128]{3,2,1,0:T(8,128)(2,1)S(1)}, u32[]{:S(2)}, u32[]{:S(2)}) collective-permute-start(bf16[2,4,16,128]{3,2,1,0:T(8,128)(2,1)S(1)} %get-tuple-element.59), channel_id=1, source_target_pairs={{0,24},{8,16},{16,8},{24,0},{1,25},{9,17},{17,9},{25,1},{2,26},{10... | collective-permute-start | bytes 98312 | tf_op jit(solution)/shard_map/ppermute | solution.py:352
  15.9 2.4 %collective-permute-done.4 = bf16[2,4,16,128]{3,2,1,0:T(8,128)(2,1)S(1)} collective-permute-done((bf16[2,4,16,128]{3,2,1,0:T(8,128)(2,1)S(1)}, bf16[2,4,16,128]{3,2,1,0:T(8,128)(2,1)S(1)}, u32[]{:S(2)}, u32[]{:S(2)}) %collective-permute-start.4) | collective-permute-done | bytes 32800 | tf_op jit(solution)/shard_map/ppermute | solution.py:352
  18.2 2.5 %collective-permute-done.6 = bf16[2,4,16,128]{3,2,1,0:T(8,128)(2,1)S(1)} collective-permute-done((bf16[2,4,16,128]{3,2,1,0:T(8,128)(2,1)S(1)}, bf16[2,4,16,128]{3,2,1,0:T(8,128)(2,1)S(1)}, u32[]{:S(2)}, u32[]{:S(2)}) %collective-permute-start.6) | collective-permute-done | bytes 32800 | tf_op jit(solution)/shard_map/ppermute | solution.py:352
  21.8 1.4 %collective-permute-start.1 = (bf16[2,4,16,128]{3,2,1,0:T(8,128)(2,1)S(1)}, bf16[2,4,16,128]{3,2,1,0:T(8,128)(2,1)S(1)}, u32[]{:S(2)}, u32[]{:S(2)}) collective-permute-start(bf16[2,4,16,128]{3,2,1,0:T(8,128)(2,1)S(1)} %get-tuple-element.55), channel_id=1, source_target_pairs={{0,8},{8,0},{16,24},{24,16},{1,9},{9,1},{17,25},{25,17},{2,10},{10... | collective-permute-start | bytes 98312 | tf_op jit(solution)/shard_map/ppermute | solution.py:352
  23.7 1.5 %collective-permute-start.3 = (bf16[2,4,16,128]{3,2,1,0:T(8,128)(2,1)S(1)}, bf16[2,4,16,128]{3,2,1,0:T(8,128)(2,1)S(1)}, u32[]{:S(2)}, u32[]{:S(2)}) collective-permute-start(bf16[2,4,16,128]{3,2,1,0:T(8,128)(2,1)S(1)} %get-tuple-element.57), channel_id=1, source_target_pairs={{0,24},{8,16},{16,8},{24,0},{1,25},{9,17},{17,9},{25,1},{2,26},{10... | collective-permute-start | bytes 98312 | tf_op jit(solution)/shard_map/ppermute | solution.py:352
  25.3 3.2 %shard_map.66 = (f32[2048,128]{1,0:T(8,128)}, f32[2048,128]{1,0:T(8,128)}, bf16[512,128]{1,0:T(8,128)(2,1)S(1)}, f32[2,128,128]{2,1,0:T(8,128)S(1)}) custom-call(f32[64,32,128]{2,1,0:T(8,128)} %pair_hbm.3, f32[2,128]{1,0:T(2,128)S(1)} %copy-done.7, bf16[2,128,128]{2,1,0:T(8,128)(2,1)S(1)} %copy-done.6, bf16[2,128,512]{2,1,0:T(8,128)(2,1)S(1)} %copy-done.4, ...), custom_call_target="tpu_custom_call" | custom-call | flops 67108864 | bytes 3737600 | tf_op jit(solution)/shard_map/pallas_call | solution.py:336
  29.8 3.0 %all-to-all-done.recv_ref = bf16[32,2,3,16,128]{4,3,2,1,0:T(8,128)(2,1)S(1)} async-done(((bf16[32,2,3,16,128]{4,3,2,1,0:T(8,128)(2,1)}), bf16[32,2,3,16,128]{4,3,2,1,0:T(8,128)(2,1)S(1)}, u32[]{:S(2)}, u32[]{:S(2)}) %all-to-all-start) | async-done | bytes 786464 | tf_op jit(solution)/shard_map/all_to_all | solution.py:400
  33.6 21.2 %all_to_all.20 = bf16[32,5,16,128]{3,2,1,0:T(8,128)(2,1)S(1)} all-to-all(bf16[32,5,16,128]{3,2,1,0:T(8,128)(2,1)S(1)} %shard_map.67), channel_id=1, replica_groups=mesh['row'=4,'half'=2,'rest'=4] {'row','half','rest'}, dimensions={0} | all-to-all | bytes 1310720 | tf_op jit(solution)/shard_map/all_to_all | solution.py:433
  54.8 3.2 %shard_map.68 = (f32[2048,128]{1,0:T(8,128)}, bf16[4,2,4,8,16,128]{5,4,3,2,1,0:T(8,128)(2,1)}, bf16[4,2,8,16,128]{4,3,2,1,0:T(8,128)(2,1)}, bf16[4,2,8,16,128]{4,3,2,1,0:T(8,128)(2,1)}) custom-call(f32[2048,128]{1,0:T(8,128)S(1)} %copy-done.2, bf16[4,2,4,5,16,128]{5,4,3,2,1,0:T(8,128)(2,1)S(1)} %bitcast.45, f32[2048,128]{1,0:T(8,128)S(1)} %copy-done.3, ...), custom_call_target="tpu_custom_call" | custom-call | flops 335544320 | bytes 5702656 | tf_op jit(solution)/shard_map/pallas_call | solution.py:336
  58.1 2.8 %all-to-all-start.2 = ((bf16[32,8,16,128]{3,2,1,0:T(8,128)(2,1)}), bf16[32,8,16,128]{3,2,1,0:T(8,128)(2,1)S(1)}, u32[]{:S(2)}, u32[]{:S(2)}) async-start(bf16[32,8,16,128]{3,2,1,0:T(8,128)(2,1)} %bitcast.47), calls=%async_computation.2 | async-start | bytes 2097152 | tf_op jit(solution)/shard_map/all_to_all | solution.py:450
  61.1 1.4 %collective-permute-done.8 = bf16[4,2,8,16,128]{4,3,2,1,0:T(8,128)(2,1)S(1)} collective-permute-done((bf16[4,2,8,16,128]{4,3,2,1,0:T(8,128)(2,1)S(1)}, bf16[4,2,8,16,128]{4,3,2,1,0:T(8,128)(2,1)S(1)}, u32[]{:S(2)}, u32[]{:S(2)}) %collective-permute-start.8) | collective-permute-done | bytes 262176 | tf_op jit(solution)/shard_map/ppermute | solution.py:352
  62.6 1.7 %collective-permute-start.12 = (bf16[2,8,16,128]{3,2,1,0:T(8,128)(2,1)S(1)}, bf16[2,8,16,128]{3,2,1,0:T(8,128)(2,1)S(1)}, u32[]{:S(2)}, u32[]{:S(2)}) collective-permute-start(bf16[2,8,16,128]{3,2,1,0:T(8,128)(2,1)S(1)} %get-tuple-element.50), channel_id=1, source_target_pairs={{0,8},{8,0},{16,24},{24,16},{1,9},{9,1},{17,25},{25,17},{2,10},{10... | collective-permute-start | bytes 196616 | tf_op jit(solution)/shard_map/ppermute | solution.py:352
  64.3 1.5 %collective-permute-start.14 = (bf16[2,8,16,128]{3,2,1,0:T(8,128)(2,1)S(1)}, bf16[2,8,16,128]{3,2,1,0:T(8,128)(2,1)S(1)}, u32[]{:S(2)}, u32[]{:S(2)}) collective-permute-start(bf16[2,8,16,128]{3,2,1,0:T(8,128)(2,1)S(1)} %get-tuple-element.51), channel_id=1, source_target_pairs={{0,24},{8,16},{16,8},{24,0},{1,25},{9,17},{17,9},{25,1},{2,26},{10... | collective-permute-start | bytes 196616 | tf_op jit(solution)/shard_map/ppermute | solution.py:352
  66.1 5.4 %collective-permute-done.12 = bf16[2,8,16,128]{3,2,1,0:T(8,128)(2,1)S(1)} collective-permute-done((bf16[2,8,16,128]{3,2,1,0:T(8,128)(2,1)S(1)}, bf16[2,8,16,128]{3,2,1,0:T(8,128)(2,1)S(1)}, u32[]{:S(2)}, u32[]{:S(2)}) %collective-permute-start.12) | collective-permute-done | bytes 65568 | tf_op jit(solution)/shard_map/ppermute | solution.py:352
  71.5 3.2 %collective-permute-done.14 = bf16[2,8,16,128]{3,2,1,0:T(8,128)(2,1)S(1)} collective-permute-done((bf16[2,8,16,128]{3,2,1,0:T(8,128)(2,1)S(1)}, bf16[2,8,16,128]{3,2,1,0:T(8,128)(2,1)S(1)}, u32[]{:S(2)}, u32[]{:S(2)}) %collective-permute-start.14) | collective-permute-done | bytes 65568 | tf_op jit(solution)/shard_map/ppermute | solution.py:352
  76.5 2.7 %collective-permute-start.11 = (bf16[2,8,16,128]{3,2,1,0:T(8,128)(2,1)S(1)}, bf16[2,8,16,128]{3,2,1,0:T(8,128)(2,1)S(1)}, u32[]{:S(2)}, u32[]{:S(2)}) collective-permute-start(bf16[2,8,16,128]{3,2,1,0:T(8,128)(2,1)S(1)} %get-tuple-element.49), channel_id=1, source_target_pairs={{0,24},{8,16},{16,8},{24,0},{1,25},{9,17},{17,9},{25,1},{2,26},{10... | collective-permute-start | bytes 196616 | tf_op jit(solution)/shard_map/ppermute | solution.py:352
  79.2 3.0 %shard_map.69.gate_ref = f32[2048,128]{1,0:T(8,128)} custom-call(f32[2048,128]{1,0:T(8,128)} %get-tuple-element.38.first_hbm.first_ref, f32[2,128]{1,0:T(2,128)S(1)} %copy-done.7, bf16[2,128,128]{2,1,0:T(8,128)(2,1)S(1)} %copy-done.6), custom_call_target="tpu_custom_call" | custom-call | flops 67108864 | bytes 2163712 | tf_op jit(solution)/shard_map/pallas_call | solution.py:336
  82.2 5.6 %collective-permute-done.15.refs_4_ = bf16[4,2,8,16,128]{4,3,2,1,0:T(8,128)(2,1)S(1)} collective-permute-done((bf16[4,2,8,16,128]{4,3,2,1,0:T(8,128)(2,1)S(1)}, bf16[4,2,8,16,128]{4,3,2,1,0:T(8,128)(2,1)S(1)}, u32[]{:S(2)}, u32[]{:S(2)}) %collective-permute-start.15) | collective-permute-done | bytes 262176 | tf_op jit(solution)/shard_map/ppermute | solution.py:352
  89.1 13.3 %all_to_all.21 = bf16[16,8,16,128]{3,2,1,0:T(8,128)(2,1)S(1)} all-to-all(bf16[16,8,16,128]{3,2,1,0:T(8,128)(2,1)S(1)} %shard_map.71), channel_id=1, replica_groups=mesh['row'=4,'half'=2,'rest'=4] {'row','rest'}, dimensions={0} | all-to-all | bytes 1048576 | tf_op jit(solution)/shard_map/all_to_all | solution.py:471
  102.4 1.7 %shard_map.72 = f32[64,32,128]{2,1,0:T(8,128)} custom-call(f32[2048,128]{1,0:T(8,128)S(1)} %copy-done, bf16[128,16,128]{2,1,0:T(8,128)(2,1)S(1)} %bitcast.46, f32[2048,128]{1,0:T(8,128)S(1)} %copy-done.1, f32[2,128,128]{2,1,0:T(8,128)S(1)} %get-tuple-element.36.gain_cols_ref, bf16[2,128,128]{2,1,0:T(8,128)(2,1)S(1)} %copy-done.5), custom_call_target="tpu_custom_call" | custom-call | flops 67108864 | bytes 3866624 | tf_op jit(solution)/shard_map/pallas_call | solution.py:336
  (53 shorter events, 8.1 us)
Async XLA Ops:
  3.6 29.3 %all-to-all-start = ((bf16[32,2,3,16,128]{4,3,2,1,0:T(8,128)(2,1)}), bf16[32,2,3,16,128]{4,3,2,1,0:T(8,128)(2,1)S(1)}, u32[]{:S(2)}, u32[]{:S(2)}) async-start(bf16[32,2,3,16,128]{4,3,2,1,0:T(8,128)(2,1)} %get-tuple-element.25), calls=%async_computation | async-start | bytes 1572864 | tf_op jit(solution)/shard_map/all_to_all | solution.py:400
  10.9 1.4 %collective-permute-start = (bf16[4,2,4,16,128]{4,3,2,1,0:T(8,128)(2,1)S(1)}, bf16[4,2,4,16,128]{4,3,2,1,0:T(8,128)(2,1)S(1)}, u32[]{:S(2)}, u32[]{:S(2)}) collective-permute-start(bf16[4,2,4,16,128]{4,3,2,1,0:T(8,128)(2,1)S(1)} %copy-done.12), channel_id=1, source_target_pairs={{0,1},{1,0},{2,3},{3,2},{4,5},{5,4},{6,7},{7,6},{8,9},{9,8},{10,11... | collective-permute-start | bytes 393224 | tf_op jit(solution)/shard_map/ppermute | solution.py:352
  12.3 13.0 %copy-start.6 = (bf16[2,128,128]{2,1,0:T(8,128)(2,1)S(1)}, bf16[2,128,128]{2,1,0:T(8,128)(2,1)}, u32[]{:S(2)}) copy-start(bf16[2,128,128]{2,1,0:T(8,128)(2,1)} %w_gate_ref.3) | copy-start | bytes 196612
  12.3 5.9 %collective-permute-start.4 = (bf16[2,4,16,128]{3,2,1,0:T(8,128)(2,1)S(1)}, bf16[2,4,16,128]{3,2,1,0:T(8,128)(2,1)S(1)}, u32[]{:S(2)}, u32[]{:S(2)}) collective-permute-start(bf16[2,4,16,128]{3,2,1,0:T(8,128)(2,1)S(1)} %get-tuple-element.58), channel_id=1, source_target_pairs={{0,8},{8,0},{16,24},{24,16},{1,9},{9,1},{17,25},{25,17},{2,10},{10... | collective-permute-start | bytes 98312 | tf_op jit(solution)/shard_map/ppermute | solution.py:352
  14.2 6.5 %collective-permute-start.6 = (bf16[2,4,16,128]{3,2,1,0:T(8,128)(2,1)S(1)}, bf16[2,4,16,128]{3,2,1,0:T(8,128)(2,1)S(1)}, u32[]{:S(2)}, u32[]{:S(2)}) collective-permute-start(bf16[2,4,16,128]{3,2,1,0:T(8,128)(2,1)S(1)} %get-tuple-element.59), channel_id=1, source_target_pairs={{0,24},{8,16},{16,8},{24,0},{1,25},{9,17},{17,9},{25,1},{2,26},{10... | collective-permute-start | bytes 98312 | tf_op jit(solution)/shard_map/ppermute | solution.py:352
  15.6 5.5 %collective-permute-start.5 = (bf16[2,4,16,128]{3,2,1,0:T(8,128)(2,1)S(1)}, bf16[2,4,16,128]{3,2,1,0:T(8,128)(2,1)S(1)}, u32[]{:S(2)}, u32[]{:S(2)}) collective-permute-start(bf16[2,4,16,128]{3,2,1,0:T(8,128)(2,1)S(1)} %get-tuple-element.60), channel_id=1, source_target_pairs={{0,16},{8,24},{16,0},{24,8},{1,17},{9,25},{17,1},{25,9},{2,18},{10... | collective-permute-start | bytes 98312 | tf_op jit(solution)/shard_map/ppermute | solution.py:352
  21.1 8.2 %collective-permute-start.7 = (bf16[4,2,4,16,128]{4,3,2,1,0:T(8,128)(2,1)S(1)}, bf16[4,2,4,16,128]{4,3,2,1,0:T(8,128)(2,1)S(1)}, u32[]{:S(2)}, u32[]{:S(2)}) collective-permute-start(bf16[4,2,4,16,128]{4,3,2,1,0:T(8,128)(2,1)S(1)} %pad_maximum_fusion.1), channel_id=1, source_target_pairs={{0,2},{1,3},{2,0},{3,1},{4,6},{5,7},{6,4},{7,5},{8,10},{9,11},{10,... | collective-permute-start | bytes 393224 | tf_op jit(solution)/shard_map/ppermute | solution.py:352
  21.8 6.7 %collective-permute-start.1 = (bf16[2,4,16,128]{3,2,1,0:T(8,128)(2,1)S(1)}, bf16[2,4,16,128]{3,2,1,0:T(8,128)(2,1)S(1)}, u32[]{:S(2)}, u32[]{:S(2)}) collective-permute-start(bf16[2,4,16,128]{3,2,1,0:T(8,128)(2,1)S(1)} %get-tuple-element.55), channel_id=1, source_target_pairs={{0,8},{8,0},{16,24},{24,16},{1,9},{9,1},{17,25},{25,17},{2,10},{10... | collective-permute-start | bytes 98312 | tf_op jit(solution)/shard_map/ppermute | solution.py:352
  23.2 5.3 %collective-permute-start.2 = (bf16[2,4,16,128]{3,2,1,0:T(8,128)(2,1)S(1)}, bf16[2,4,16,128]{3,2,1,0:T(8,128)(2,1)S(1)}, u32[]{:S(2)}, u32[]{:S(2)}) collective-permute-start(bf16[2,4,16,128]{3,2,1,0:T(8,128)(2,1)S(1)} %get-tuple-element.56), channel_id=1, source_target_pairs={{0,16},{8,24},{16,0},{24,8},{1,17},{9,25},{17,1},{25,9},{2,18},{10... | collective-permute-start | bytes 98312 | tf_op jit(solution)/shard_map/ppermute | solution.py:352
  23.7 5.1 %collective-permute-start.3 = (bf16[2,4,16,128]{3,2,1,0:T(8,128)(2,1)S(1)}, bf16[2,4,16,128]{3,2,1,0:T(8,128)(2,1)S(1)}, u32[]{:S(2)}, u32[]{:S(2)}) collective-permute-start(bf16[2,4,16,128]{3,2,1,0:T(8,128)(2,1)S(1)} %get-tuple-element.57), channel_id=1, source_target_pairs={{0,24},{8,16},{16,8},{24,0},{1,25},{9,17},{17,9},{25,1},{2,26},{10... | collective-permute-start | bytes 98312 | tf_op jit(solution)/shard_map/ppermute | solution.py:352
  32.8 22.0 %copy-start.3 = (f32[2048,128]{1,0:T(8,128)S(1)}, f32[2048,128]{1,0:T(8,128)}, u32[]{:S(2)}) copy-start(f32[2048,128]{1,0:T(8,128)} %get-tuple-element.35.gate_ref) | copy-start | bytes 3145732
  33.6 21.2 %copy-start.2 = (f32[2048,128]{1,0:T(8,128)S(1)}, f32[2048,128]{1,0:T(8,128)}, u32[]{:S(2)}) copy-start(f32[2048,128]{1,0:T(8,128)} %get-tuple-element.32.ordered_ref) | copy-start | bytes 3145732
  33.6 21.2 %copy-start.5 = (bf16[2,128,128]{2,1,0:T(8,128)(2,1)S(1)}, bf16[2,128,128]{2,1,0:T(8,128)(2,1)}, u32[]{:S(2)}) copy-start(bf16[2,128,128]{2,1,0:T(8,128)(2,1)} %w_out_ref.3) | copy-start | bytes 196612
  58.1 30.4 %all-to-all-start.2 = ((bf16[32,8,16,128]{3,2,1,0:T(8,128)(2,1)}), bf16[32,8,16,128]{3,2,1,0:T(8,128)(2,1)S(1)}, u32[]{:S(2)}, u32[]{:S(2)}) async-start(bf16[32,8,16,128]{3,2,1,0:T(8,128)(2,1)} %bitcast.47), calls=%async_computation.2 | async-start | bytes 2097152 | tf_op jit(solution)/shard_map/all_to_all | solution.py:450
  60.9 1.6 %collective-permute-start.8 = (bf16[4,2,8,16,128]{4,3,2,1,0:T(8,128)(2,1)S(1)}, bf16[4,2,8,16,128]{4,3,2,1,0:T(8,128)(2,1)S(1)}, u32[]{:S(2)}, u32[]{:S(2)}) collective-permute-start(bf16[4,2,8,16,128]{4,3,2,1,0:T(8,128)(2,1)S(1)} %copy-done.11), channel_id=1, source_target_pairs={{0,1},{1,0},{2,3},{3,2},{4,5},{5,4},{6,7},{7,6},{8,9},{9,8},{10,11... | collective-permute-start | bytes 786440 | tf_op jit(solution)/shard_map/ppermute | solution.py:352
  62.6 8.9 %collective-permute-start.12 = (bf16[2,8,16,128]{3,2,1,0:T(8,128)(2,1)S(1)}, bf16[2,8,16,128]{3,2,1,0:T(8,128)(2,1)S(1)}, u32[]{:S(2)}, u32[]{:S(2)}) collective-permute-start(bf16[2,8,16,128]{3,2,1,0:T(8,128)(2,1)S(1)} %get-tuple-element.50), channel_id=1, source_target_pairs={{0,8},{8,0},{16,24},{24,16},{1,9},{9,1},{17,25},{25,17},{2,10},{10... | collective-permute-start | bytes 196616 | tf_op jit(solution)/shard_map/ppermute | solution.py:352
  64.3 10.5 %collective-permute-start.14 = (bf16[2,8,16,128]{3,2,1,0:T(8,128)(2,1)S(1)}, bf16[2,8,16,128]{3,2,1,0:T(8,128)(2,1)S(1)}, u32[]{:S(2)}, u32[]{:S(2)}) collective-permute-start(bf16[2,8,16,128]{3,2,1,0:T(8,128)(2,1)S(1)} %get-tuple-element.51), channel_id=1, source_target_pairs={{0,24},{8,16},{16,8},{24,0},{1,25},{9,17},{17,9},{25,1},{2,26},{10... | collective-permute-start | bytes 196616 | tf_op jit(solution)/shard_map/ppermute | solution.py:352
  65.7 9.0 %collective-permute-start.13 = (bf16[2,8,16,128]{3,2,1,0:T(8,128)(2,1)S(1)}, bf16[2,8,16,128]{3,2,1,0:T(8,128)(2,1)S(1)}, u32[]{:S(2)}, u32[]{:S(2)}) collective-permute-start(bf16[2,8,16,128]{3,2,1,0:T(8,128)(2,1)S(1)} %get-tuple-element.52), channel_id=1, source_target_pairs={{0,16},{8,24},{16,0},{24,8},{1,17},{9,25},{17,1},{25,9},{2,18},{10... | collective-permute-start | bytes 196616 | tf_op jit(solution)/shard_map/ppermute | solution.py:352
  74.8 13.0 %collective-permute-start.15 = (bf16[4,2,8,16,128]{4,3,2,1,0:T(8,128)(2,1)S(1)}, bf16[4,2,8,16,128]{4,3,2,1,0:T(8,128)(2,1)S(1)}, u32[]{:S(2)}, u32[]{:S(2)}) collective-permute-start(bf16[4,2,8,16,128]{4,3,2,1,0:T(8,128)(2,1)S(1)} %pad_maximum_fusion), channel_id=1, source_target_pairs={{0,2},{1,3},{2,0},{3,1},{4,6},{5,7},{6,4},{7,5},{8,10},{9,11},{10,... | collective-permute-start | bytes 786440 | tf_op jit(solution)/shard_map/ppermute | solution.py:352
  75.7 6.5 %collective-permute-start.9 = (bf16[2,8,16,128]{3,2,1,0:T(8,128)(2,1)S(1)}, bf16[2,8,16,128]{3,2,1,0:T(8,128)(2,1)S(1)}, u32[]{:S(2)}, u32[]{:S(2)}) collective-permute-start(bf16[2,8,16,128]{3,2,1,0:T(8,128)(2,1)S(1)} %get-tuple-element.47), channel_id=1, source_target_pairs={{0,8},{8,0},{16,24},{24,16},{1,9},{9,1},{17,25},{25,17},{2,10},{10... | collective-permute-start | bytes 196616 | tf_op jit(solution)/shard_map/ppermute | solution.py:352
  75.9 6.3 %collective-permute-start.10 = (bf16[2,8,16,128]{3,2,1,0:T(8,128)(2,1)S(1)}, bf16[2,8,16,128]{3,2,1,0:T(8,128)(2,1)S(1)}, u32[]{:S(2)}, u32[]{:S(2)}) collective-permute-start(bf16[2,8,16,128]{3,2,1,0:T(8,128)(2,1)S(1)} %get-tuple-element.48), channel_id=1, source_target_pairs={{0,16},{8,24},{16,0},{24,8},{1,17},{9,25},{17,1},{25,9},{2,18},{10... | collective-permute-start | bytes 196616 | tf_op jit(solution)/shard_map/ppermute | solution.py:352
  76.5 5.7 %collective-permute-start.11 = (bf16[2,8,16,128]{3,2,1,0:T(8,128)(2,1)S(1)}, bf16[2,8,16,128]{3,2,1,0:T(8,128)(2,1)S(1)}, u32[]{:S(2)}, u32[]{:S(2)}) collective-permute-start(bf16[2,8,16,128]{3,2,1,0:T(8,128)(2,1)S(1)} %get-tuple-element.49), channel_id=1, source_target_pairs={{0,24},{8,16},{16,8},{24,0},{1,25},{9,17},{17,9},{25,1},{2,26},{10... | collective-permute-start | bytes 196616 | tf_op jit(solution)/shard_map/ppermute | solution.py:352
  88.5 14.0 %copy-start.1 = (f32[2048,128]{1,0:T(8,128)S(1)}, f32[2048,128]{1,0:T(8,128)}, u32[]{:S(2)}) copy-start(f32[2048,128]{1,0:T(8,128)} %shard_map.69.gate_ref) | copy-start | bytes 3145732
  89.1 13.3 %copy-start = (f32[2048,128]{1,0:T(8,128)S(1)}, f32[2048,128]{1,0:T(8,128)}, u32[]{:S(2)}) copy-start(f32[2048,128]{1,0:T(8,128)} %get-tuple-element.38.first_hbm.first_ref) | copy-start | bytes 3145732
  (7 other events, 40.5 us)

commit v8 on v7

--- a/solution.py
+++ b/solution.py
@@ -61,14 +61,14 @@
     return planes[at : at + n1, :].astype(BF16)
 
 
-def relative_blocks(b_ref, planes, n1, channels):
-    rows, highs = b_ref.shape[1:3]
+def leave_blocks(b_ref, keep_hbm, swap_hbm, sem):
     my_row, my_rest = lax.axis_index("row"), lax.axis_index("rest")
-    for r in range(rows):
-        for c in range(2 * highs):
-            apart = jnp.bitwise_xor(my_rest, c)
-            for i, channel in enumerate(channels(r, c)):
-                b_ref[apart % 2, jnp.bitwise_xor(my_row, r), apart // 2, i] = plane(planes, n1, channel)
+    for core, hbm in ((1, swap_hbm), (0, keep_hbm)):
+        for r in range(hbm.shape[0]):
+            for c in range(hbm.shape[1]):
+                block = b_ref.at[jnp.bitwise_xor(my_row, r), jnp.bitwise_xor(my_rest, 2 * c + core)]
+                pltpu.make_async_copy(block, hbm.at[r, c], sem).start()
+    return pltpu.make_async_copy(b_ref, b_ref, sem)
 
 
 def project_kernel(shared, pair_hbm, gain_hbm, w_hbm, send_hbm, *refs):
@@ -93,20 +93,19 @@
     branch_planes(normed, w_ref[...].T, n1, planes)
     sent = []
 
-    def leave(vmem, hbm):
-        sent.append(pltpu.make_async_copy(vmem, hbm, out_sems.at[len(sent)]))
+    def leave(vmem, hbm, sem):
+        sent.append(pltpu.make_async_copy(vmem, hbm, sem))
         sent[-1].start()
 
     if shared:
-        rest = 2 * b_ref.shape[2]
-
-        def channels(r, c):
-            at = ndev * depth + (r * rest + c) * 2 * shared
-            return [side * hidden + at + h for side in range(2) for h in range(2 * shared)]
-
-        relative_blocks(b_ref, planes, n1, channels)
-        leave(b_ref.at[1], swap_hbm)
-        leave(b_ref.at[0], keep_hbm)
+        rows, rest = b_ref.shape[:2]
+        for r in range(rows):
+            for c in range(rest):
+                at = ndev * depth + (r * rest + c) * 2 * shared
+                for side in range(2):
+                    for h in range(2 * shared):
+                        b_ref[r, c, 2 * shared * side + h] = plane(planes, n1, side * hidden + at + h)
+        sent.append(leave_blocks(b_ref, keep_hbm, swap_hbm, out_sems.at[2]))
     for part in range(2):
         own = range(part * ndev // 2, (part + 1) * ndev // 2)
         for device in own:
@@ -114,7 +113,7 @@
                 for h in range(depth):
                     send_ref[device, side, h] = plane(planes, n1, side * hidden + device * depth + h)
         at = pl.ds(own[0], len(own))
-        leave(send_ref.at[at], send_hbm.at[at])
+        leave(send_ref.at[at], send_hbm.at[at], out_sems.at[part])
     for copy in sent:
         copy.wait()
 
@@ -189,11 +188,12 @@
 def outgoing_half_kernel(cols, first, *refs):
     *part_refs, out_ref, left, right, b_ref = refs
     rows, depth = out_ref.shape[0] // cols, out_ref.shape[1]
+    places = [[slot(cols, r, c) for c in range(cols)] for r in range(rows)]
     stage(part_refs, b_ref)
     for h in range(depth):
         dense_half(b_ref, h, first, left)
         dense_half(b_ref, depth + h, first, right)
-        scatter_product(transposed_product(left, right), rows, cols, first, h, out_ref)
+        scatter_product(transposed_product(left, right), first, h, places, out_ref)
 
 
 def outgoing_kernel(cols, first, recv_ref, *refs):
@@ -201,6 +201,7 @@
     ndev, _, depth, n1, _ = recv_ref.shape
     split = LANES // first
     rows = ndev // cols
+    places = [[slot(cols, r, c) for c in range(cols)] for r in range(rows)]
     for h in range(depth):
         for side, dense in ((0, left), (1, right)):
             for c in range(cols):
@@ -208,22 +209,27 @@
                     at = (c * split + l) * n1
                     dense[at : at + n1, :] = jnp.concatenate(
                         [
-                            recv_ref[r * cols + c, side, h, :, l * first : (l + 1) * first]
+                            recv_ref[places[r][c], side, h, :, l * first : (l + 1) * first]
                             for r in range(rows)
                         ],
                         axis=1,
                     )
-        scatter_product(transposed_product(left, right), rows, cols, first, h, out_ref)
+        scatter_product(transposed_product(left, right), first, h, places, out_ref)
     for ref in half_ref:
         out_ref[:, depth:] = ref[...]
 
 
-def scatter_product(summed, rows, cols, first, h, out_ref):
+def slot(cols, r, c):
+    rest = cols // 2
+    return (r * rest + c % rest) * 2 + c // rest
+
+
+def scatter_product(summed, first, h, places, out_ref):
     split = LANES // first
     n1 = out_ref.shape[2]
-    for r in range(rows):
-        for c in range(cols):
-            out_ref[r * cols + c, h] = jnp.concatenate(
+    for r, row in enumerate(places):
+        for c, place in enumerate(row):
+            out_ref[place, h] = jnp.concatenate(
                 [
                     summed[(c * split + l) * n1 : (c * split + l + 1) * n1, r * first : (r + 1) * first]
                     for l in range(split)
@@ -243,17 +249,18 @@
     ndev, depth, n1, _ = recv_ref.shape
     split = LANES // first
     rows = ndev // cols
+    places = [[c * rows + r for c in range(cols // 2)] for r in range(rows)]
     for h in range(depth):
         for c in range(cols):
             for l in range(split):
                 at = (c * split + l) * n1
                 left[at : at + n1, :] = jnp.concatenate(
-                    [recv_ref[r * cols + c, h, :, l * first : (l + 1) * first] for r in range(rows)], axis=1
+                    [recv_ref[slot(cols, r, c), h, :, l * first : (l + 1) * first] for r in range(rows)], axis=1
                 )
         summed = lax.dot_general(
             dense_ref[h], left[...], (((1,), (1,)), ((), ())), preferred_element_type=F32
         ).astype(BF16)
-        scatter_product(summed, rows, cols // 2, first, h, out_ref)
+        scatter_product(summed, first, h, places, out_ref)
 
 
 def output(x, gain_cols, w, normal):
@@ -275,7 +282,7 @@
     first_hbm, send_hbm, keep_hbm, swap_hbm, normal, planes, first_ref, send_ref, b_ref, sems,
 ):
     rows, rest, depth, n1, _ = send_ref.shape
-    halves = send_hbm.shape[1]
+    halves = send_hbm.shape[2]
     hidden = rows * rest * depth
     copies = []
 
@@ -287,25 +294,25 @@
     own = summed_ref.shape[3] - 2 * shared
     x = summed_ref[:, :, :, :own].astype(F32).reshape(-1, n1, LANES)
     if shared:
-        x_shared = summed_ref[:, 0, :, own:].astype(F32) + summed_ref[:, 1, :, own:].astype(F32)
+        x_shared = summed_ref[:, :, 0, own:].astype(F32) + summed_ref[:, :, 1, own:].astype(F32)
         x = jnp.concatenate([x, x_shared.reshape(-1, n1, LANES)], axis=0)
     z = ordered_ref[...] + gate_ref[...] * output(x, gain_cols_ref[0], w_out_ref[0], normal)
     first_ref[...] = z
     leave(first_ref, first_hbm)
     branch_planes(norm_rows(z, gain_ref[1:2, :]), w_t_ref[...], n1, planes)
-    relative_blocks(
-        b_ref, planes, n1, lambda r, c: [hidden + (r * rest + c) * depth + h for h in range(depth)]
-    )
-    leave(b_ref.at[1], swap_hbm)
-    leave(b_ref.at[0], keep_hbm)
     for r in range(rows):
         for c in range(rest):
             for h in range(depth):
-                send_ref[r, c, h] = plane(planes, n1, (r * rest + c) * depth + h)
+                b_ref[r, c, h] = plane(planes, n1, hidden + (c * rows + r) * depth + h)
+    copies.append(leave_blocks(b_ref, keep_hbm, swap_hbm, sems.at[len(copies)]))
+    for r in range(rows):
+        for c in range(rest):
+            for h in range(depth):
+                send_ref[r, c, h] = plane(planes, n1, (c * rows + r) * depth + h)
         if r % (rows // 2) == rows // 2 - 1:
             own = pl.ds(r + 1 - rows // 2, rows // 2)
             for half in range(halves):
-                leave(send_ref.at[own], send_hbm.at[own, half])
+                leave(send_ref.at[own], send_hbm.at[own, :, half])
     for copy in copies:
         copy.wait()
 
@@ -371,9 +378,9 @@
     total = rows * first
 
     flat_shape = jax.ShapeDtypeStruct((count, chans), F32)
-    planes = pltpu.VMEM((2 * hidden * (n1 + 1), LANES), F32)
-    normal = pltpu.VMEM((hidden * (n1 + 1), LANES), F32)
-    padded = pltpu.VMEM((first * (second + 1), chans), F32)
+    planes = pltpu.VMEM(((2 * hidden + 1) * (n1 + 1), LANES), F32)
+    normal = pltpu.VMEM(((hidden + 1) * (n1 + 1), LANES), F32)
+    padded = pltpu.VMEM(((first + 1) * (second + 1), chans), F32)
     proj_flops = 2 * count * chans * 4 * hidden
     gate_flops = 2 * count * chans * chans
     tri_flops = 2 * (depth + shared) * total**3
@@ -392,12 +399,12 @@
             planes,
             pltpu.VMEM(out_shapes[0].shape, BF16),
         ]
-        + ([pltpu.VMEM((2,) + out_shapes[1].shape, BF16)] if shared else [])
-        + [pltpu.SemaphoreType.DMA((3,)), pltpu.SemaphoreType.DMA((4,))],
+        + ([pltpu.VMEM((rows, rest, 4 * shared, n1, LANES), BF16)] if shared else [])
+        + [pltpu.SemaphoreType.DMA((3,)), pltpu.SemaphoreType.DMA((3,))],
         proj_flops, pair, norm_in_gain, w_proj,
         pinned=[pltpu.HBM] * 3, spaces=[pltpu.HBM] * len(out_shapes),
     )
-    recv = lax.all_to_all(send, ("row", "half", "rest"), 0, 0, tiled=True)
+    recv = lax.all_to_all(send, ("row", "rest", "half"), 0, 0, tiled=True)
     prepared = call(
         prepare_kernel,
         [
@@ -430,8 +437,8 @@
         [pltpu.VMEM((cols * second, total), BF16)] * 2,
         tri_flops, recv, *halves,
     )
-    summed = lax.all_to_all(product, ("row", "half", "rest"), 0, 0, tiled=True)
-    send_shape, b_shape = shaped(rows, 2, rest, half_depth), shaped(rows, rest // 2, half_depth)
+    summed = lax.all_to_all(product, ("row", "rest", "half"), 0, 0, tiled=True)
+    send_shape, b_shape = shaped(rows, rest, 2, half_depth), shaped(rows, rest // 2, half_depth)
     middle, send, keep, swap = call(
         middle_kernel,
         [flat_shape, send_shape, b_shape, b_shape],
@@ -440,15 +447,15 @@
             planes,
             pltpu.VMEM(flat_shape.shape, F32),
             pltpu.VMEM((rows, rest, half_depth, n1, LANES), BF16),
-            pltpu.VMEM((2,) + b_shape.shape, BF16),
-            pltpu.SemaphoreType.DMA((7,)),
+            pltpu.VMEM((rows, rest, half_depth, n1, LANES), BF16),
+            pltpu.SemaphoreType.DMA((6,)),
         ],
         proj_flops + gate_flops,
-        ordered, summed.reshape(rows, 2, rest, depth + 2 * shared, n1, LANES), gate, gain_cols, w_out, norm_in_gain, w_t,
+        ordered, summed.reshape(rows, rest, 2, depth + 2 * shared, n1, LANES), gate, gain_cols, w_out, norm_in_gain, w_t,
         spaces=[pltpu.HBM] * 4,
     )
     recv = lax.all_to_all(
-        send.reshape(ndev, half_depth, n1, LANES), ("row", "half", "rest"), 0, 0, tiled=True
+        send.reshape(ndev, half_depth, n1, LANES), ("row", "rest", "half"), 0, 0, tiled=True
     )
     (gate,) = call(
         gate_kernel, [flat_shape],
@@ -468,7 +475,7 @@
         [shaped(rows * rest, half_depth)], [pltpu.VMEM((cols * second, total), BF16)],
         tri_flops, recv, *dense,
     )
-    summed = lax.all_to_all(product, ("row", "rest"), 0, 0, tiled=True)
+    summed = lax.all_to_all(product, ("rest", "row"), 0, 0, tiled=True)
     (updated,) = call(
         last_kernel,
         [jax.ShapeDtypeStruct(pair.shape, F32)], [normal, padded, pltpu.SemaphoreType.DMA((1,))], gate_flops,

time: 105 us -> 102 us (0.971)
  waiting for transfers between devices: 26.3 us -> 20.1 us
  starting transfers between devices: 26.3 us -> 31 us
  blocking collectives: 34.5 us -> 32.9 us
    ppermute x16, starting transfers between devices: 16.2 us -> 20.6 us  [swapped(): lax.ppermute(x, axis, [(d, d ^ apart) for d in range(size)])]
    ppermute x16, waiting for transfers between devices: 22.8 us -> 18.9 us  [swapped(): lax.ppermute(x, axis, [(d, d ^ apart) for d in range(size)])]
    all_to_all x2, waiting for transfers between devices: 3.47 us -> 1.21 us  [the longest x1 1.21 us: body(): recv = lax.all_to_all(send, ('row', 'rest', 'half'), 0, 0, tiled=True)]
    all_to_all x2, blocking collectives: 34.5 us -> 32.9 us  [the longest x1 21 us: body(): summed = lax.all_to_all(product, ('row', 'rest', 'half'), 0, 0, tiled=True)]
where the time goes in v8:
time: 102 us; the launch traced here: 101 us
  blocking collectives  32.9 us (32%)
  starting transfers between devices  31 us (30%)
  waiting for transfers between devices  20.1 us (20%)
  Pallas kernels  16.6 us (16%)
    all_to_all x1, blocking collectives, body(): summed = lax.all_to_all(product, ('row', 'rest', 'half'), 0, 0, tiled=True)  21 us
    ppermute x16, starting transfers between devices, swapped(): lax.ppermute(x, axis, [(d, d ^ apart) for d in range(size)])  20.6 us
    ppermute x16, waiting for transfers between devices, swapped(): lax.ppermute(x, axis, [(d, d ^ apart) for d in range(size)])  18.9 us
    pallas_call x9, Pallas kernels, call(): pl.pallas_call(kernel, out_shape=outs, in_specs=in_specs, out_specs=out_s...  16.6 us
    all_to_all x1, blocking collectives, body(): summed = lax.all_to_all(product, ('rest', 'row'), 0, 0, tiled=True)  11.9 us
    all_to_all x1, starting transfers between devices, body(): recv = lax.all_to_all(send, ('row', 'rest', 'half'), 0, 0, tiled=True)  7.31 us
    all_to_all x1, starting transfers between devices, body(): lax.all_to_all(send.reshape(ndev, half_depth, n1, LANES), ('row', 'rest',...  3.07 us
  transfers between devices with their start and end apart: 18, of which 12 were waited for; matrix products, arithmetic and copies ran while one was open for 0% of the time, Pallas kernels for 7%

profile of v8, /device:TPU:0, one launch (start us, length us, event | category | flops | bytes accessed | tf_op | source)
XLA Modules:
  0.0 101.0 jit_solution(14922788793347087303)
XLA Ops:
  0.0 3.5 %shard_map.64 = (bf16[32,2,3,16,128]{4,3,2,1,0:T(8,128)(2,1)}, bf16[4,2,4,16,128]{4,3,2,1,0:T(8,128)(2,1)}, bf16[4,2,4,16,128]{4,3,2,1,0:T(8,128)(2,1)}) custom-call(f32[64,32,128]{2,1,0:T(8,128)} %pair_hbm.3, f32[2,128]{1,0:T(2,128)} %gain_ref.5, bf16[2,128,512]{2,1,0:T(8,128)(2,1)} %w_ref.1), custom_call_target="tpu_custom_call" | custom-call | flops 268435456 | bytes 2360320 | tf_op jit(solution)/shard_map/pallas_call | solution.py:343
  3.5 7.3 %all-to-all-start = ((bf16[32,2,3,16,128]{4,3,2,1,0:T(8,128)(2,1)}), bf16[32,2,3,16,128]{4,3,2,1,0:T(8,128)(2,1)S(1)}, u32[]{:S(2)}, u32[]{:S(2)}) async-start(bf16[32,2,3,16,128]{4,3,2,1,0:T(8,128)(2,1)} %get-tuple-element.25), calls=%async_computation | async-start | bytes 1572864 | tf_op jit(solution)/shard_map/all_to_all | solution.py:407
  12.3 1.8 %collective-permute-start.4 = (bf16[2,4,16,128]{3,2,1,0:T(8,128)(2,1)S(1)}, bf16[2,4,16,128]{3,2,1,0:T(8,128)(2,1)S(1)}, u32[]{:S(2)}, u32[]{:S(2)}) collective-permute-start(bf16[2,4,16,128]{3,2,1,0:T(8,128)(2,1)S(1)} %get-tuple-element.58), channel_id=1, source_target_pairs={{0,8},{8,0},{16,24},{24,16},{1,9},{9,1},{17,25},{25,17},{2,10},{10... | collective-permute-start | bytes 98312 | tf_op jit(solution)/shard_map/ppermute | solution.py:359
  14.1 1.5 %collective-permute-start.6 = (bf16[2,4,16,128]{3,2,1,0:T(8,128)(2,1)S(1)}, bf16[2,4,16,128]{3,2,1,0:T(8,128)(2,1)S(1)}, u32[]{:S(2)}, u32[]{:S(2)}) collective-permute-start(bf16[2,4,16,128]{3,2,1,0:T(8,128)(2,1)S(1)} %get-tuple-element.59), channel_id=1, source_target_pairs={{0,24},{8,16},{16,8},{24,0},{1,25},{9,17},{17,9},{25,1},{2,26},{10... | collective-permute-start | bytes 98312 | tf_op jit(solution)/shard_map/ppermute | solution.py:359
  15.9 3.1 %collective-permute-done.4 = bf16[2,4,16,128]{3,2,1,0:T(8,128)(2,1)S(1)} collective-permute-done((bf16[2,4,16,128]{3,2,1,0:T(8,128)(2,1)S(1)}, bf16[2,4,16,128]{3,2,1,0:T(8,128)(2,1)S(1)}, u32[]{:S(2)}, u32[]{:S(2)}) %collective-permute-start.4) | collective-permute-done | bytes 32800 | tf_op jit(solution)/shard_map/ppermute | solution.py:359
  18.9 1.6 %collective-permute-done.6 = bf16[2,4,16,128]{3,2,1,0:T(8,128)(2,1)S(1)} collective-permute-done((bf16[2,4,16,128]{3,2,1,0:T(8,128)(2,1)S(1)}, bf16[2,4,16,128]{3,2,1,0:T(8,128)(2,1)S(1)}, u32[]{:S(2)}, u32[]{:S(2)}) %collective-permute-start.6) | collective-permute-done | bytes 32800 | tf_op jit(solution)/shard_map/ppermute | solution.py:359
  20.8 1.3 %collective-permute-start.7 = (bf16[4,2,4,16,128]{4,3,2,1,0:T(8,128)(2,1)S(1)}, bf16[4,2,4,16,128]{4,3,2,1,0:T(8,128)(2,1)S(1)}, u32[]{:S(2)}, u32[]{:S(2)}) collective-permute-start(bf16[4,2,4,16,128]{4,3,2,1,0:T(8,128)(2,1)S(1)} %pad_maximum_fusion.1), channel_id=1, source_target_pairs={{0,2},{1,3},{2,0},{3,1},{4,6},{5,7},{6,4},{7,5},{8,10},{9,11},{10,... | collective-permute-start | bytes 393224 | tf_op jit(solution)/shard_map/ppermute | solution.py:359
  24.1 1.6 %collective-permute-start.3 = (bf16[2,4,16,128]{3,2,1,0:T(8,128)(2,1)S(1)}, bf16[2,4,16,128]{3,2,1,0:T(8,128)(2,1)S(1)}, u32[]{:S(2)}, u32[]{:S(2)}) collective-permute-start(bf16[2,4,16,128]{3,2,1,0:T(8,128)(2,1)S(1)} %get-tuple-element.57), channel_id=1, source_target_pairs={{0,24},{8,16},{16,8},{24,0},{1,25},{9,17},{17,9},{25,1},{2,26},{10... | collective-permute-start | bytes 98312 | tf_op jit(solution)/shard_map/ppermute | solution.py:359
  25.7 3.2 %shard_map.66 = (f32[2048,128]{1,0:T(8,128)}, f32[2048,128]{1,0:T(8,128)}, bf16[512,128]{1,0:T(8,128)(2,1)S(1)}, f32[2,128,128]{2,1,0:T(8,128)S(1)}) custom-call(f32[64,32,128]{2,1,0:T(8,128)} %pair_hbm.3, f32[2,128]{1,0:T(2,128)S(1)} %copy-done.7, bf16[2,128,128]{2,1,0:T(8,128)(2,1)S(1)} %copy-done.6, bf16[2,128,512]{2,1,0:T(8,128)(2,1)S(1)} %copy-done.4, ...), custom_call_target="tpu_custom_call" | custom-call | flops 67108864 | bytes 3737600 | tf_op jit(solution)/shard_map/pallas_call | solution.py:343
  30.1 1.2 %all-to-all-done.recv_ref = bf16[32,2,3,16,128]{4,3,2,1,0:T(8,128)(2,1)S(1)} async-done(((bf16[32,2,3,16,128]{4,3,2,1,0:T(8,128)(2,1)}), bf16[32,2,3,16,128]{4,3,2,1,0:T(8,128)(2,1)S(1)}, u32[]{:S(2)}, u32[]{:S(2)}) %all-to-all-start) | async-done | bytes 786464 | tf_op jit(solution)/shard_map/all_to_all | solution.py:407
  32.2 21.0 %all_to_all.20 = bf16[32,5,16,128]{3,2,1,0:T(8,128)(2,1)S(1)} all-to-all(bf16[32,5,16,128]{3,2,1,0:T(8,128)(2,1)S(1)} %shard_map.67), channel_id=1, replica_groups=mesh['row'=4,'half'=2,'rest'=4] {'row','rest','half'}, dimensions={0} | all-to-all | bytes 1310720 | tf_op jit(solution)/shard_map/all_to_all | solution.py:440
  53.1 3.2 %shard_map.68 = (f32[2048,128]{1,0:T(8,128)}, bf16[4,4,2,8,16,128]{5,4,3,2,1,0:T(8,128)(2,1)}, bf16[4,2,8,16,128]{4,3,2,1,0:T(8,128)(2,1)}, bf16[4,2,8,16,128]{4,3,2,1,0:T(8,128)(2,1)}) custom-call(f32[2048,128]{1,0:T(8,128)S(1)} %copy-done.2, bf16[4,4,2,5,16,128]{5,4,3,2,1,0:T(8,128)(2,1)S(1)} %bitcast.45, f32[2048,128]{1,0:T(8,128)S(1)} %copy-done.3, ...), custom_call_target="tpu_custom_call" | custom-call | flops 335544320 | bytes 5702656 | tf_op jit(solution)/shard_map/pallas_call | solution.py:343
  56.4 3.1 %all-to-all-start.2 = ((bf16[32,8,16,128]{3,2,1,0:T(8,128)(2,1)}), bf16[32,8,16,128]{3,2,1,0:T(8,128)(2,1)S(1)}, u32[]{:S(2)}, u32[]{:S(2)}) async-start(bf16[32,8,16,128]{3,2,1,0:T(8,128)(2,1)} %bitcast.47), calls=%async_computation.2 | async-start | bytes 2097152 | tf_op jit(solution)/shard_map/all_to_all | solution.py:457
  59.8 1.3 %collective-permute-done.8 = bf16[4,2,8,16,128]{4,3,2,1,0:T(8,128)(2,1)S(1)} collective-permute-done((bf16[4,2,8,16,128]{4,3,2,1,0:T(8,128)(2,1)S(1)}, bf16[4,2,8,16,128]{4,3,2,1,0:T(8,128)(2,1)S(1)}, u32[]{:S(2)}, u32[]{:S(2)}) %collective-permute-start.8) | collective-permute-done | bytes 262176 | tf_op jit(solution)/shard_map/ppermute | solution.py:359
  61.1 1.8 %collective-permute-start.12 = (bf16[2,8,16,128]{3,2,1,0:T(8,128)(2,1)S(1)}, bf16[2,8,16,128]{3,2,1,0:T(8,128)(2,1)S(1)}, u32[]{:S(2)}, u32[]{:S(2)}) collective-permute-start(bf16[2,8,16,128]{3,2,1,0:T(8,128)(2,1)S(1)} %get-tuple-element.50), channel_id=1, source_target_pairs={{0,8},{8,0},{16,24},{24,16},{1,9},{9,1},{17,25},{25,17},{2,10},{10... | collective-permute-start | bytes 196616 | tf_op jit(solution)/shard_map/ppermute | solution.py:359
  62.9 1.5 %collective-permute-start.14 = (bf16[2,8,16,128]{3,2,1,0:T(8,128)(2,1)S(1)}, bf16[2,8,16,128]{3,2,1,0:T(8,128)(2,1)S(1)}, u32[]{:S(2)}, u32[]{:S(2)}) collective-permute-start(bf16[2,8,16,128]{3,2,1,0:T(8,128)(2,1)S(1)} %get-tuple-element.51), channel_id=1, source_target_pairs={{0,24},{8,16},{16,8},{24,0},{1,25},{9,17},{17,9},{25,1},{2,26},{10... | collective-permute-start | bytes 196616 | tf_op jit(solution)/shard_map/ppermute | solution.py:359
  64.7 5.8 %collective-permute-done.12 = bf16[2,8,16,128]{3,2,1,0:T(8,128)(2,1)S(1)} collective-permute-done((bf16[2,8,16,128]{3,2,1,0:T(8,128)(2,1)S(1)}, bf16[2,8,16,128]{3,2,1,0:T(8,128)(2,1)S(1)}, u32[]{:S(2)}, u32[]{:S(2)}) %collective-permute-start.12) | collective-permute-done | bytes 65568 | tf_op jit(solution)/shard_map/ppermute | solution.py:359
  70.5 2.1 %collective-permute-done.14 = bf16[2,8,16,128]{3,2,1,0:T(8,128)(2,1)S(1)} collective-permute-done((bf16[2,8,16,128]{3,2,1,0:T(8,128)(2,1)S(1)}, bf16[2,8,16,128]{3,2,1,0:T(8,128)(2,1)S(1)}, u32[]{:S(2)}, u32[]{:S(2)}) %collective-permute-start.14) | collective-permute-done | bytes 65568 | tf_op jit(solution)/shard_map/ppermute | solution.py:359
  72.7 4.6 %collective-permute-start.15 = (bf16[4,2,8,16,128]{4,3,2,1,0:T(8,128)(2,1)S(1)}, bf16[4,2,8,16,128]{4,3,2,1,0:T(8,128)(2,1)S(1)}, u32[]{:S(2)}, u32[]{:S(2)}) collective-permute-start(bf16[4,2,8,16,128]{4,3,2,1,0:T(8,128)(2,1)S(1)} %pad_maximum_fusion), channel_id=1, source_target_pairs={{0,2},{1,3},{2,0},{3,1},{4,6},{5,7},{6,4},{7,5},{8,10},{9,11},{10,... | collective-permute-start | bytes 786440 | tf_op jit(solution)/shard_map/ppermute | solution.py:359
  78.0 2.7 %collective-permute-start.11 = (bf16[2,8,16,128]{3,2,1,0:T(8,128)(2,1)S(1)}, bf16[2,8,16,128]{3,2,1,0:T(8,128)(2,1)S(1)}, u32[]{:S(2)}, u32[]{:S(2)}) collective-permute-start(bf16[2,8,16,128]{3,2,1,0:T(8,128)(2,1)S(1)} %get-tuple-element.49), channel_id=1, source_target_pairs={{0,24},{8,16},{16,8},{24,0},{1,25},{9,17},{17,9},{25,1},{2,26},{10... | collective-permute-start | bytes 196616 | tf_op jit(solution)/shard_map/ppermute | solution.py:359
  80.8 3.0 %shard_map.69.gate_ref = f32[2048,128]{1,0:T(8,128)} custom-call(f32[2048,128]{1,0:T(8,128)} %get-tuple-element.38.first_hbm.first_ref, f32[2,128]{1,0:T(2,128)S(1)} %copy-done.7, bf16[2,128,128]{2,1,0:T(8,128)(2,1)S(1)} %copy-done.6), custom_call_target="tpu_custom_call" | custom-call | flops 67108864 | bytes 2163712 | tf_op jit(solution)/shard_map/pallas_call | solution.py:343
  84.9 1.6 %collective-permute-done.15.refs_4_ = bf16[4,2,8,16,128]{4,3,2,1,0:T(8,128)(2,1)S(1)} collective-permute-done((bf16[4,2,8,16,128]{4,3,2,1,0:T(8,128)(2,1)S(1)}, bf16[4,2,8,16,128]{4,3,2,1,0:T(8,128)(2,1)S(1)}, u32[]{:S(2)}, u32[]{:S(2)}) %collective-permute-start.15) | collective-permute-done | bytes 262176 | tf_op jit(solution)/shard_map/ppermute | solution.py:359
  87.4 11.9 %all_to_all.21 = bf16[16,8,16,128]{3,2,1,0:T(8,128)(2,1)S(1)} all-to-all(bf16[16,8,16,128]{3,2,1,0:T(8,128)(2,1)S(1)} %shard_map.71), channel_id=1, replica_groups=mesh['row'=4,'half'=2,'rest'=4] {'rest','row'}, dimensions={0} | all-to-all | bytes 1048576 | tf_op jit(solution)/shard_map/all_to_all | solution.py:478
  99.3 1.7 %shard_map.72 = f32[64,32,128]{2,1,0:T(8,128)} custom-call(f32[2048,128]{1,0:T(8,128)S(1)} %copy-done, bf16[128,16,128]{2,1,0:T(8,128)(2,1)S(1)} %bitcast.46, f32[2048,128]{1,0:T(8,128)S(1)} %copy-done.1, f32[2,128,128]{2,1,0:T(8,128)S(1)} %get-tuple-element.36.gain_cols_ref, bf16[2,128,128]{2,1,0:T(8,128)(2,1)S(1)} %copy-done.5), custom_call_target="tpu_custom_call" | custom-call | flops 67108864 | bytes 3866624 | tf_op jit(solution)/shard_map/pallas_call | solution.py:343
  (53 shorter events, 9.4 us)
Async XLA Ops:
  3.5 27.8 %all-to-all-start = ((bf16[32,2,3,16,128]{4,3,2,1,0:T(8,128)(2,1)}), bf16[32,2,3,16,128]{4,3,2,1,0:T(8,128)(2,1)S(1)}, u32[]{:S(2)}, u32[]{:S(2)}) async-start(bf16[32,2,3,16,128]{4,3,2,1,0:T(8,128)(2,1)} %get-tuple-element.25), calls=%async_computation | async-start | bytes 1572864 | tf_op jit(solution)/shard_map/all_to_all | solution.py:407
  10.8 1.4 %collective-permute-start = (bf16[4,2,4,16,128]{4,3,2,1,0:T(8,128)(2,1)S(1)}, bf16[4,2,4,16,128]{4,3,2,1,0:T(8,128)(2,1)S(1)}, u32[]{:S(2)}, u32[]{:S(2)}) collective-permute-start(bf16[4,2,4,16,128]{4,3,2,1,0:T(8,128)(2,1)S(1)} %copy-done.12), channel_id=1, source_target_pairs={{0,1},{1,0},{2,3},{3,2},{4,5},{5,4},{6,7},{7,6},{8,9},{9,8},{10,11... | collective-permute-start | bytes 393224 | tf_op jit(solution)/shard_map/ppermute | solution.py:359
  12.3 13.4 %copy-start.6 = (bf16[2,128,128]{2,1,0:T(8,128)(2,1)S(1)}, bf16[2,128,128]{2,1,0:T(8,128)(2,1)}, u32[]{:S(2)}) copy-start(bf16[2,128,128]{2,1,0:T(8,128)(2,1)} %w_gate_ref.3) | copy-start | bytes 196612
  12.3 13.4 %copy-start.4 = (bf16[2,128,512]{2,1,0:T(8,128)(2,1)S(1)}, bf16[2,128,512]{2,1,0:T(8,128)(2,1)}, u32[]{:S(2)}) copy-start(bf16[2,128,512]{2,1,0:T(8,128)(2,1)} %w_ref.1) | copy-start | bytes 786436
  12.3 6.6 %collective-permute-start.4 = (bf16[2,4,16,128]{3,2,1,0:T(8,128)(2,1)S(1)}, bf16[2,4,16,128]{3,2,1,0:T(8,128)(2,1)S(1)}, u32[]{:S(2)}, u32[]{:S(2)}) collective-permute-start(bf16[2,4,16,128]{3,2,1,0:T(8,128)(2,1)S(1)} %get-tuple-element.58), channel_id=1, source_target_pairs={{0,8},{8,0},{16,24},{24,16},{1,9},{9,1},{17,25},{25,17},{2,10},{10... | collective-permute-start | bytes 98312 | tf_op jit(solution)/shard_map/ppermute | solution.py:359
  14.1 6.4 %collective-permute-start.6 = (bf16[2,4,16,128]{3,2,1,0:T(8,128)(2,1)S(1)}, bf16[2,4,16,128]{3,2,1,0:T(8,128)(2,1)S(1)}, u32[]{:S(2)}, u32[]{:S(2)}) collective-permute-start(bf16[2,4,16,128]{3,2,1,0:T(8,128)(2,1)S(1)} %get-tuple-element.59), channel_id=1, source_target_pairs={{0,24},{8,16},{16,8},{24,0},{1,25},{9,17},{17,9},{25,1},{2,26},{10... | collective-permute-start | bytes 98312 | tf_op jit(solution)/shard_map/ppermute | solution.py:359
  15.6 5.2 %collective-permute-start.5 = (bf16[2,4,16,128]{3,2,1,0:T(8,128)(2,1)S(1)}, bf16[2,4,16,128]{3,2,1,0:T(8,128)(2,1)S(1)}, u32[]{:S(2)}, u32[]{:S(2)}) collective-permute-start(bf16[2,4,16,128]{3,2,1,0:T(8,128)(2,1)S(1)} %get-tuple-element.60), channel_id=1, source_target_pairs={{0,16},{8,24},{16,0},{24,8},{1,17},{9,25},{17,1},{25,9},{2,18},{10... | collective-permute-start | bytes 98312 | tf_op jit(solution)/shard_map/ppermute | solution.py:359
  20.8 8.8 %collective-permute-start.7 = (bf16[4,2,4,16,128]{4,3,2,1,0:T(8,128)(2,1)S(1)}, bf16[4,2,4,16,128]{4,3,2,1,0:T(8,128)(2,1)S(1)}, u32[]{:S(2)}, u32[]{:S(2)}) collective-permute-start(bf16[4,2,4,16,128]{4,3,2,1,0:T(8,128)(2,1)S(1)} %pad_maximum_fusion.1), channel_id=1, source_target_pairs={{0,2},{1,3},{2,0},{3,1},{4,6},{5,7},{6,4},{7,5},{8,10},{9,11},{10,... | collective-permute-start | bytes 393224 | tf_op jit(solution)/shard_map/ppermute | solution.py:359
  22.2 6.7 %collective-permute-start.1 = (bf16[2,4,16,128]{3,2,1,0:T(8,128)(2,1)S(1)}, bf16[2,4,16,128]{3,2,1,0:T(8,128)(2,1)S(1)}, u32[]{:S(2)}, u32[]{:S(2)}) collective-permute-start(bf16[2,4,16,128]{3,2,1,0:T(8,128)(2,1)S(1)} %get-tuple-element.55), channel_id=1, source_target_pairs={{0,8},{8,0},{16,24},{24,16},{1,9},{9,1},{17,25},{25,17},{2,10},{10... | collective-permute-start | bytes 98312 | tf_op jit(solution)/shard_map/ppermute | solution.py:359
  23.1 5.8 %collective-permute-start.2 = (bf16[2,4,16,128]{3,2,1,0:T(8,128)(2,1)S(1)}, bf16[2,4,16,128]{3,2,1,0:T(8,128)(2,1)S(1)}, u32[]{:S(2)}, u32[]{:S(2)}) collective-permute-start(bf16[2,4,16,128]{3,2,1,0:T(8,128)(2,1)S(1)} %get-tuple-element.56), channel_id=1, source_target_pairs={{0,16},{8,24},{16,0},{24,8},{1,17},{9,25},{17,1},{25,9},{2,18},{10... | collective-permute-start | bytes 98312 | tf_op jit(solution)/shard_map/ppermute | solution.py:359
  24.1 5.0 %collective-permute-start.3 = (bf16[2,4,16,128]{3,2,1,0:T(8,128)(2,1)S(1)}, bf16[2,4,16,128]{3,2,1,0:T(8,128)(2,1)S(1)}, u32[]{:S(2)}, u32[]{:S(2)}) collective-permute-start(bf16[2,4,16,128]{3,2,1,0:T(8,128)(2,1)S(1)} %get-tuple-element.57), channel_id=1, source_target_pairs={{0,24},{8,16},{16,8},{24,0},{1,25},{9,17},{17,9},{25,1},{2,26},{10... | collective-permute-start | bytes 98312 | tf_op jit(solution)/shard_map/ppermute | solution.py:359
  31.4 21.8 %copy-start.3 = (f32[2048,128]{1,0:T(8,128)S(1)}, f32[2048,128]{1,0:T(8,128)}, u32[]{:S(2)}) copy-start(f32[2048,128]{1,0:T(8,128)} %get-tuple-element.35.gate_ref) | copy-start | bytes 3145732
  32.1 21.0 %copy-start.2 = (f32[2048,128]{1,0:T(8,128)S(1)}, f32[2048,128]{1,0:T(8,128)}, u32[]{:S(2)}) copy-start(f32[2048,128]{1,0:T(8,128)} %get-tuple-element.32.ordered_ref) | copy-start | bytes 3145732
  32.1 21.0 %copy-start.5 = (bf16[2,128,128]{2,1,0:T(8,128)(2,1)S(1)}, bf16[2,128,128]{2,1,0:T(8,128)(2,1)}, u32[]{:S(2)}) copy-start(bf16[2,128,128]{2,1,0:T(8,128)(2,1)} %w_out_ref.3) | copy-start | bytes 196612
  56.4 30.4 %all-to-all-start.2 = ((bf16[32,8,16,128]{3,2,1,0:T(8,128)(2,1)}), bf16[32,8,16,128]{3,2,1,0:T(8,128)(2,1)S(1)}, u32[]{:S(2)}, u32[]{:S(2)}) async-start(bf16[32,8,16,128]{3,2,1,0:T(8,128)(2,1)} %bitcast.47), calls=%async_computation.2 | async-start | bytes 2097152 | tf_op jit(solution)/shard_map/all_to_all | solution.py:457
  59.5 1.6 %collective-permute-start.8 = (bf16[4,2,8,16,128]{4,3,2,1,0:T(8,128)(2,1)S(1)}, bf16[4,2,8,16,128]{4,3,2,1,0:T(8,128)(2,1)S(1)}, u32[]{:S(2)}, u32[]{:S(2)}) collective-permute-start(bf16[4,2,8,16,128]{4,3,2,1,0:T(8,128)(2,1)S(1)} %copy-done.11), channel_id=1, source_target_pairs={{0,1},{1,0},{2,3},{3,2},{4,5},{5,4},{6,7},{7,6},{8,9},{9,8},{10,11... | collective-permute-start | bytes 786440 | tf_op jit(solution)/shard_map/ppermute | solution.py:359
  61.1 9.4 %collective-permute-start.12 = (bf16[2,8,16,128]{3,2,1,0:T(8,128)(2,1)S(1)}, bf16[2,8,16,128]{3,2,1,0:T(8,128)(2,1)S(1)}, u32[]{:S(2)}, u32[]{:S(2)}) collective-permute-start(bf16[2,8,16,128]{3,2,1,0:T(8,128)(2,1)S(1)} %get-tuple-element.50), channel_id=1, source_target_pairs={{0,8},{8,0},{16,24},{24,16},{1,9},{9,1},{17,25},{25,17},{2,10},{10... | collective-permute-start | bytes 196616 | tf_op jit(solution)/shard_map/ppermute | solution.py:359
  62.9 9.7 %collective-permute-start.14 = (bf16[2,8,16,128]{3,2,1,0:T(8,128)(2,1)S(1)}, bf16[2,8,16,128]{3,2,1,0:T(8,128)(2,1)S(1)}, u32[]{:S(2)}, u32[]{:S(2)}) collective-permute-start(bf16[2,8,16,128]{3,2,1,0:T(8,128)(2,1)S(1)} %get-tuple-element.51), channel_id=1, source_target_pairs={{0,24},{8,16},{16,8},{24,0},{1,25},{9,17},{17,9},{25,1},{2,26},{10... | collective-permute-start | bytes 196616 | tf_op jit(solution)/shard_map/ppermute | solution.py:359
  64.4 8.2 %collective-permute-start.13 = (bf16[2,8,16,128]{3,2,1,0:T(8,128)(2,1)S(1)}, bf16[2,8,16,128]{3,2,1,0:T(8,128)(2,1)S(1)}, u32[]{:S(2)}, u32[]{:S(2)}) collective-permute-start(bf16[2,8,16,128]{3,2,1,0:T(8,128)(2,1)S(1)} %get-tuple-element.52), channel_id=1, source_target_pairs={{0,16},{8,24},{16,0},{24,8},{1,17},{9,25},{17,1},{25,9},{2,18},{10... | collective-permute-start | bytes 196616 | tf_op jit(solution)/shard_map/ppermute | solution.py:359
  72.7 13.8 %collective-permute-start.15 = (bf16[4,2,8,16,128]{4,3,2,1,0:T(8,128)(2,1)S(1)}, bf16[4,2,8,16,128]{4,3,2,1,0:T(8,128)(2,1)S(1)}, u32[]{:S(2)}, u32[]{:S(2)}) collective-permute-start(bf16[4,2,8,16,128]{4,3,2,1,0:T(8,128)(2,1)S(1)} %pad_maximum_fusion), channel_id=1, source_target_pairs={{0,2},{1,3},{2,0},{3,1},{4,6},{5,7},{6,4},{7,5},{8,10},{9,11},{10,... | collective-permute-start | bytes 786440 | tf_op jit(solution)/shard_map/ppermute | solution.py:359
  77.3 6.5 %collective-permute-start.9 = (bf16[2,8,16,128]{3,2,1,0:T(8,128)(2,1)S(1)}, bf16[2,8,16,128]{3,2,1,0:T(8,128)(2,1)S(1)}, u32[]{:S(2)}, u32[]{:S(2)}) collective-permute-start(bf16[2,8,16,128]{3,2,1,0:T(8,128)(2,1)S(1)} %get-tuple-element.47), channel_id=1, source_target_pairs={{0,8},{8,0},{16,24},{24,16},{1,9},{9,1},{17,25},{25,17},{2,10},{10... | collective-permute-start | bytes 196616 | tf_op jit(solution)/shard_map/ppermute | solution.py:359
  77.3 6.5 %collective-permute-start.10 = (bf16[2,8,16,128]{3,2,1,0:T(8,128)(2,1)S(1)}, bf16[2,8,16,128]{3,2,1,0:T(8,128)(2,1)S(1)}, u32[]{:S(2)}, u32[]{:S(2)}) collective-permute-start(bf16[2,8,16,128]{3,2,1,0:T(8,128)(2,1)S(1)} %get-tuple-element.48), channel_id=1, source_target_pairs={{0,16},{8,24},{16,0},{24,8},{1,17},{9,25},{17,1},{25,9},{2,18},{10... | collective-permute-start | bytes 196616 | tf_op jit(solution)/shard_map/ppermute | solution.py:359
  78.0 6.8 %collective-permute-start.11 = (bf16[2,8,16,128]{3,2,1,0:T(8,128)(2,1)S(1)}, bf16[2,8,16,128]{3,2,1,0:T(8,128)(2,1)S(1)}, u32[]{:S(2)}, u32[]{:S(2)}) collective-permute-start(bf16[2,8,16,128]{3,2,1,0:T(8,128)(2,1)S(1)} %get-tuple-element.49), channel_id=1, source_target_pairs={{0,24},{8,16},{16,8},{24,0},{1,25},{9,17},{17,9},{25,1},{2,26},{10... | collective-permute-start | bytes 196616 | tf_op jit(solution)/shard_map/ppermute | solution.py:359
  86.8 12.6 %copy-start.1 = (f32[2048,128]{1,0:T(8,128)S(1)}, f32[2048,128]{1,0:T(8,128)}, u32[]{:S(2)}) copy-start(f32[2048,128]{1,0:T(8,128)} %shard_map.69.gate_ref) | copy-start | bytes 3145732
  (7 other events, 41.0 us)

commit v9 on v8

--- a/solution.py
+++ b/solution.py
@@ -271,10 +271,15 @@
     scaled = center * lax.rsqrt(spread + 1e-05)
     for h in range(hidden):
         normal[h * pad : h * pad + n1, :] = scaled[h]
-    mixed = jnp.concatenate(
-        [(normal[pl.ds(s, hidden, stride=pad), :] * gain_cols).astype(BF16) for s in range(n1)], axis=1
-    )
-    return lax.dot_general(mixed, w, (((0,), (0,)), ((), ())), preferred_element_type=F32)
+    mixed = jnp.concatenate([normal[pl.ds(s, hidden, stride=pad), :] * gain_cols for s in range(n1)], axis=1)
+    high = mixed.astype(BF16)
+    low = (mixed - high.astype(F32)).astype(BF16)
+    return lax.dot_general(
+        jnp.concatenate([high, low], axis=0),
+        jnp.concatenate([w, w], axis=0),
+        (((0,), (0,)), ((), ())),
+        preferred_element_type=F32,
+    )
 
 
 def middle_kernel(

time: 102 us -> 102 us (level)
  no operation moved by 1% of the time
where the time goes in v9:
time: 102 us; the launch traced here: 101 us
  blocking collectives  32.9 us (32%)
  starting transfers between devices  31 us (30%)
  waiting for transfers between devices  20.1 us (20%)
  Pallas kernels  17.1 us (17%)
    all_to_all x1, blocking collectives, body(): summed = lax.all_to_all(product, ('row', 'rest', 'half'), 0, 0, tiled=True)  21 us
    ppermute x16, starting transfers between devices, swapped(): lax.ppermute(x, axis, [(d, d ^ apart) for d in range(size)])  20.6 us
    ppermute x16, waiting for transfers between devices, swapped(): lax.ppermute(x, axis, [(d, d ^ apart) for d in range(size)])  18.9 us
    pallas_call x9, Pallas kernels, call(): pl.pallas_call(kernel, out_shape=outs, in_specs=in_specs, out_specs=out_s...  17.1 us
    all_to_all x1, blocking collectives, body(): summed = lax.all_to_all(product, ('rest', 'row'), 0, 0, tiled=True)  11.9 us
    all_to_all x1, starting transfers between devices, body(): recv = lax.all_to_all(send, ('row', 'rest', 'half'), 0, 0, tiled=True)  7.31 us
    all_to_all x1, starting transfers between devices, body(): lax.all_to_all(send.reshape(ndev, half_depth, n1, LANES), ('row', 'rest',...  3.07 us
  transfers between devices with their start and end apart: 18, of which 12 were waited for; matrix products, arithmetic and copies ran while one was open for 0% of the time, Pallas kernels for 7%

profile of v9, /device:TPU:0, one launch (start us, length us, event | category | flops | bytes accessed | tf_op | source)
XLA Modules:
  0.0 101.5 jit_solution(3624254651596739883)
XLA Ops:
  0.0 3.5 %shard_map.64 = (bf16[32,2,3,16,128]{4,3,2,1,0:T(8,128)(2,1)}, bf16[4,2,4,16,128]{4,3,2,1,0:T(8,128)(2,1)}, bf16[4,2,4,16,128]{4,3,2,1,0:T(8,128)(2,1)}) custom-call(f32[64,32,128]{2,1,0:T(8,128)} %pair_hbm.3, f32[2,128]{1,0:T(2,128)} %gain_ref.5, bf16[2,128,512]{2,1,0:T(8,128)(2,1)} %w_ref.1), custom_call_target="tpu_custom_call" | custom-call | flops 268435456 | bytes 2360320 | tf_op jit(solution)/shard_map/pallas_call | solution.py:348
  3.5 7.3 %all-to-all-start = ((bf16[32,2,3,16,128]{4,3,2,1,0:T(8,128)(2,1)}), bf16[32,2,3,16,128]{4,3,2,1,0:T(8,128)(2,1)S(1)}, u32[]{:S(2)}, u32[]{:S(2)}) async-start(bf16[32,2,3,16,128]{4,3,2,1,0:T(8,128)(2,1)} %get-tuple-element.25), calls=%async_computation | async-start | bytes 1572864 | tf_op jit(solution)/shard_map/all_to_all | solution.py:412
  12.3 1.8 %collective-permute-start.4 = (bf16[2,4,16,128]{3,2,1,0:T(8,128)(2,1)S(1)}, bf16[2,4,16,128]{3,2,1,0:T(8,128)(2,1)S(1)}, u32[]{:S(2)}, u32[]{:S(2)}) collective-permute-start(bf16[2,4,16,128]{3,2,1,0:T(8,128)(2,1)S(1)} %get-tuple-element.58), channel_id=1, source_target_pairs={{0,8},{8,0},{16,24},{24,16},{1,9},{9,1},{17,25},{25,17},{2,10},{10... | collective-permute-start | bytes 98312 | tf_op jit(solution)/shard_map/ppermute | solution.py:364
  14.1 1.5 %collective-permute-start.6 = (bf16[2,4,16,128]{3,2,1,0:T(8,128)(2,1)S(1)}, bf16[2,4,16,128]{3,2,1,0:T(8,128)(2,1)S(1)}, u32[]{:S(2)}, u32[]{:S(2)}) collective-permute-start(bf16[2,4,16,128]{3,2,1,0:T(8,128)(2,1)S(1)} %get-tuple-element.59), channel_id=1, source_target_pairs={{0,24},{8,16},{16,8},{24,0},{1,25},{9,17},{17,9},{25,1},{2,26},{10... | collective-permute-start | bytes 98312 | tf_op jit(solution)/shard_map/ppermute | solution.py:364
  15.9 3.1 %collective-permute-done.4 = bf16[2,4,16,128]{3,2,1,0:T(8,128)(2,1)S(1)} collective-permute-done((bf16[2,4,16,128]{3,2,1,0:T(8,128)(2,1)S(1)}, bf16[2,4,16,128]{3,2,1,0:T(8,128)(2,1)S(1)}, u32[]{:S(2)}, u32[]{:S(2)}) %collective-permute-start.4) | collective-permute-done | bytes 32800 | tf_op jit(solution)/shard_map/ppermute | solution.py:364
  18.9 1.6 %collective-permute-done.6 = bf16[2,4,16,128]{3,2,1,0:T(8,128)(2,1)S(1)} collective-permute-done((bf16[2,4,16,128]{3,2,1,0:T(8,128)(2,1)S(1)}, bf16[2,4,16,128]{3,2,1,0:T(8,128)(2,1)S(1)}, u32[]{:S(2)}, u32[]{:S(2)}) %collective-permute-start.6) | collective-permute-done | bytes 32800 | tf_op jit(solution)/shard_map/ppermute | solution.py:364
  20.8 1.3 %collective-permute-start.7 = (bf16[4,2,4,16,128]{4,3,2,1,0:T(8,128)(2,1)S(1)}, bf16[4,2,4,16,128]{4,3,2,1,0:T(8,128)(2,1)S(1)}, u32[]{:S(2)}, u32[]{:S(2)}) collective-permute-start(bf16[4,2,4,16,128]{4,3,2,1,0:T(8,128)(2,1)S(1)} %pad_maximum_fusion.1), channel_id=1, source_target_pairs={{0,2},{1,3},{2,0},{3,1},{4,6},{5,7},{6,4},{7,5},{8,10},{9,11},{10,... | collective-permute-start | bytes 393224 | tf_op jit(solution)/shard_map/ppermute | solution.py:364
  24.1 1.6 %collective-permute-start.3 = (bf16[2,4,16,128]{3,2,1,0:T(8,128)(2,1)S(1)}, bf16[2,4,16,128]{3,2,1,0:T(8,128)(2,1)S(1)}, u32[]{:S(2)}, u32[]{:S(2)}) collective-permute-start(bf16[2,4,16,128]{3,2,1,0:T(8,128)(2,1)S(1)} %get-tuple-element.57), channel_id=1, source_target_pairs={{0,24},{8,16},{16,8},{24,0},{1,25},{9,17},{17,9},{25,1},{2,26},{10... | collective-permute-start | bytes 98312 | tf_op jit(solution)/shard_map/ppermute | solution.py:364
  25.7 3.2 %shard_map.66 = (f32[2048,128]{1,0:T(8,128)}, f32[2048,128]{1,0:T(8,128)}, bf16[512,128]{1,0:T(8,128)(2,1)S(1)}, f32[2,128,128]{2,1,0:T(8,128)S(1)}) custom-call(f32[64,32,128]{2,1,0:T(8,128)} %pair_hbm.3, f32[2,128]{1,0:T(2,128)S(1)} %copy-done.7, bf16[2,128,128]{2,1,0:T(8,128)(2,1)S(1)} %copy-done.6, bf16[2,128,512]{2,1,0:T(8,128)(2,1)S(1)} %copy-done.4, ...), custom_call_target="tpu_custom_call" | custom-call | flops 67108864 | bytes 3737600 | tf_op jit(solution)/shard_map/pallas_call | solution.py:348
  30.1 1.2 %all-to-all-done.recv_ref = bf16[32,2,3,16,128]{4,3,2,1,0:T(8,128)(2,1)S(1)} async-done(((bf16[32,2,3,16,128]{4,3,2,1,0:T(8,128)(2,1)}), bf16[32,2,3,16,128]{4,3,2,1,0:T(8,128)(2,1)S(1)}, u32[]{:S(2)}, u32[]{:S(2)}) %all-to-all-start) | async-done | bytes 786464 | tf_op jit(solution)/shard_map/all_to_all | solution.py:412
  32.2 21.0 %all_to_all.20 = bf16[32,5,16,128]{3,2,1,0:T(8,128)(2,1)S(1)} all-to-all(bf16[32,5,16,128]{3,2,1,0:T(8,128)(2,1)S(1)} %shard_map.67), channel_id=1, replica_groups=mesh['row'=4,'half'=2,'rest'=4] {'row','rest','half'}, dimensions={0} | all-to-all | bytes 1310720 | tf_op jit(solution)/shard_map/all_to_all | solution.py:445
  53.1 3.5 %shard_map.68 = (f32[2048,128]{1,0:T(8,128)}, bf16[4,4,2,8,16,128]{5,4,3,2,1,0:T(8,128)(2,1)}, bf16[4,2,8,16,128]{4,3,2,1,0:T(8,128)(2,1)}, bf16[4,2,8,16,128]{4,3,2,1,0:T(8,128)(2,1)}) custom-call(f32[2048,128]{1,0:T(8,128)S(1)} %copy-done.2, bf16[4,4,2,5,16,128]{5,4,3,2,1,0:T(8,128)(2,1)S(1)} %bitcast.45, f32[2048,128]{1,0:T(8,128)S(1)} %copy-done.3, ...), custom_call_target="tpu_custom_call" | custom-call | flops 335544320 | bytes 5702656 | tf_op jit(solution)/shard_map/pallas_call | solution.py:348
  56.7 3.1 %all-to-all-start.2 = ((bf16[32,8,16,128]{3,2,1,0:T(8,128)(2,1)}), bf16[32,8,16,128]{3,2,1,0:T(8,128)(2,1)S(1)}, u32[]{:S(2)}, u32[]{:S(2)}) async-start(bf16[32,8,16,128]{3,2,1,0:T(8,128)(2,1)} %bitcast.47), calls=%async_computation.2 | async-start | bytes 2097152 | tf_op jit(solution)/shard_map/all_to_all | solution.py:462
  60.1 1.3 %collective-permute-done.8 = bf16[4,2,8,16,128]{4,3,2,1,0:T(8,128)(2,1)S(1)} collective-permute-done((bf16[4,2,8,16,128]{4,3,2,1,0:T(8,128)(2,1)S(1)}, bf16[4,2,8,16,128]{4,3,2,1,0:T(8,128)(2,1)S(1)}, u32[]{:S(2)}, u32[]{:S(2)}) %collective-permute-start.8) | collective-permute-done | bytes 262176 | tf_op jit(solution)/shard_map/ppermute | solution.py:364
  61.4 1.8 %collective-permute-start.12 = (bf16[2,8,16,128]{3,2,1,0:T(8,128)(2,1)S(1)}, bf16[2,8,16,128]{3,2,1,0:T(8,128)(2,1)S(1)}, u32[]{:S(2)}, u32[]{:S(2)}) collective-permute-start(bf16[2,8,16,128]{3,2,1,0:T(8,128)(2,1)S(1)} %get-tuple-element.50), channel_id=1, source_target_pairs={{0,8},{8,0},{16,24},{24,16},{1,9},{9,1},{17,25},{25,17},{2,10},{10... | collective-permute-start | bytes 196616 | tf_op jit(solution)/shard_map/ppermute | solution.py:364
  63.3 1.5 %collective-permute-start.14 = (bf16[2,8,16,128]{3,2,1,0:T(8,128)(2,1)S(1)}, bf16[2,8,16,128]{3,2,1,0:T(8,128)(2,1)S(1)}, u32[]{:S(2)}, u32[]{:S(2)}) collective-permute-start(bf16[2,8,16,128]{3,2,1,0:T(8,128)(2,1)S(1)} %get-tuple-element.51), channel_id=1, source_target_pairs={{0,24},{8,16},{16,8},{24,0},{1,25},{9,17},{17,9},{25,1},{2,26},{10... | collective-permute-start | bytes 196616 | tf_op jit(solution)/shard_map/ppermute | solution.py:364
  65.0 5.8 %collective-permute-done.12 = bf16[2,8,16,128]{3,2,1,0:T(8,128)(2,1)S(1)} collective-permute-done((bf16[2,8,16,128]{3,2,1,0:T(8,128)(2,1)S(1)}, bf16[2,8,16,128]{3,2,1,0:T(8,128)(2,1)S(1)}, u32[]{:S(2)}, u32[]{:S(2)}) %collective-permute-start.12) | collective-permute-done | bytes 65568 | tf_op jit(solution)/shard_map/ppermute | solution.py:364
  70.8 2.1 %collective-permute-done.14 = bf16[2,8,16,128]{3,2,1,0:T(8,128)(2,1)S(1)} collective-permute-done((bf16[2,8,16,128]{3,2,1,0:T(8,128)(2,1)S(1)}, bf16[2,8,16,128]{3,2,1,0:T(8,128)(2,1)S(1)}, u32[]{:S(2)}, u32[]{:S(2)}) %collective-permute-start.14) | collective-permute-done | bytes 65568 | tf_op jit(solution)/shard_map/ppermute | solution.py:364
  73.0 4.6 %collective-permute-start.15 = (bf16[4,2,8,16,128]{4,3,2,1,0:T(8,128)(2,1)S(1)}, bf16[4,2,8,16,128]{4,3,2,1,0:T(8,128)(2,1)S(1)}, u32[]{:S(2)}, u32[]{:S(2)}) collective-permute-start(bf16[4,2,8,16,128]{4,3,2,1,0:T(8,128)(2,1)S(1)} %pad_maximum_fusion), channel_id=1, source_target_pairs={{0,2},{1,3},{2,0},{3,1},{4,6},{5,7},{6,4},{7,5},{8,10},{9,11},{10,... | collective-permute-start | bytes 786440 | tf_op jit(solution)/shard_map/ppermute | solution.py:364
  78.3 2.7 %collective-permute-start.11 = (bf16[2,8,16,128]{3,2,1,0:T(8,128)(2,1)S(1)}, bf16[2,8,16,128]{3,2,1,0:T(8,128)(2,1)S(1)}, u32[]{:S(2)}, u32[]{:S(2)}) collective-permute-start(bf16[2,8,16,128]{3,2,1,0:T(8,128)(2,1)S(1)} %get-tuple-element.49), channel_id=1, source_target_pairs={{0,24},{8,16},{16,8},{24,0},{1,25},{9,17},{17,9},{25,1},{2,26},{10... | collective-permute-start | bytes 196616 | tf_op jit(solution)/shard_map/ppermute | solution.py:364
  81.1 3.0 %shard_map.69.gate_ref = f32[2048,128]{1,0:T(8,128)} custom-call(f32[2048,128]{1,0:T(8,128)} %get-tuple-element.38.first_hbm.first_ref, f32[2,128]{1,0:T(2,128)S(1)} %copy-done.7, bf16[2,128,128]{2,1,0:T(8,128)(2,1)S(1)} %copy-done.6), custom_call_target="tpu_custom_call" | custom-call | flops 67108864 | bytes 2163712 | tf_op jit(solution)/shard_map/pallas_call | solution.py:348
  85.2 1.6 %collective-permute-done.15.refs_4_ = bf16[4,2,8,16,128]{4,3,2,1,0:T(8,128)(2,1)S(1)} collective-permute-done((bf16[4,2,8,16,128]{4,3,2,1,0:T(8,128)(2,1)S(1)}, bf16[4,2,8,16,128]{4,3,2,1,0:T(8,128)(2,1)S(1)}, u32[]{:S(2)}, u32[]{:S(2)}) %collective-permute-start.15) | collective-permute-done | bytes 262176 | tf_op jit(solution)/shard_map/ppermute | solution.py:364
  87.7 11.9 %all_to_all.21 = bf16[16,8,16,128]{3,2,1,0:T(8,128)(2,1)S(1)} all-to-all(bf16[16,8,16,128]{3,2,1,0:T(8,128)(2,1)S(1)} %shard_map.71), channel_id=1, replica_groups=mesh['row'=4,'half'=2,'rest'=4] {'rest','row'}, dimensions={0} | all-to-all | bytes 1048576 | tf_op jit(solution)/shard_map/all_to_all | solution.py:483
  99.7 1.8 %shard_map.72 = f32[64,32,128]{2,1,0:T(8,128)} custom-call(f32[2048,128]{1,0:T(8,128)S(1)} %copy-done, bf16[128,16,128]{2,1,0:T(8,128)(2,1)S(1)} %bitcast.46, f32[2048,128]{1,0:T(8,128)S(1)} %copy-done.1, f32[2,128,128]{2,1,0:T(8,128)S(1)} %get-tuple-element.36.gain_cols_ref, bf16[2,128,128]{2,1,0:T(8,128)(2,1)S(1)} %copy-done.5), custom_call_target="tpu_custom_call" | custom-call | flops 67108864 | bytes 3866624 | tf_op jit(solution)/shard_map/pallas_call | solution.py:348
  (53 shorter events, 9.4 us)
Async XLA Ops:
  3.5 27.8 %all-to-all-start = ((bf16[32,2,3,16,128]{4,3,2,1,0:T(8,128)(2,1)}), bf16[32,2,3,16,128]{4,3,2,1,0:T(8,128)(2,1)S(1)}, u32[]{:S(2)}, u32[]{:S(2)}) async-start(bf16[32,2,3,16,128]{4,3,2,1,0:T(8,128)(2,1)} %get-tuple-element.25), calls=%async_computation | async-start | bytes 1572864 | tf_op jit(solution)/shard_map/all_to_all | solution.py:412
  10.8 1.4 %collective-permute-start = (bf16[4,2,4,16,128]{4,3,2,1,0:T(8,128)(2,1)S(1)}, bf16[4,2,4,16,128]{4,3,2,1,0:T(8,128)(2,1)S(1)}, u32[]{:S(2)}, u32[]{:S(2)}) collective-permute-start(bf16[4,2,4,16,128]{4,3,2,1,0:T(8,128)(2,1)S(1)} %copy-done.12), channel_id=1, source_target_pairs={{0,1},{1,0},{2,3},{3,2},{4,5},{5,4},{6,7},{7,6},{8,9},{9,8},{10,11... | collective-permute-start | bytes 393224 | tf_op jit(solution)/shard_map/ppermute | solution.py:364
  12.3 13.4 %copy-start.6 = (bf16[2,128,128]{2,1,0:T(8,128)(2,1)S(1)}, bf16[2,128,128]{2,1,0:T(8,128)(2,1)}, u32[]{:S(2)}) copy-start(bf16[2,128,128]{2,1,0:T(8,128)(2,1)} %w_gate_ref.3) | copy-start | bytes 196612
  12.3 13.4 %copy-start.4 = (bf16[2,128,512]{2,1,0:T(8,128)(2,1)S(1)}, bf16[2,128,512]{2,1,0:T(8,128)(2,1)}, u32[]{:S(2)}) copy-start(bf16[2,128,512]{2,1,0:T(8,128)(2,1)} %w_ref.1) | copy-start | bytes 786436
  12.3 6.6 %collective-permute-start.4 = (bf16[2,4,16,128]{3,2,1,0:T(8,128)(2,1)S(1)}, bf16[2,4,16,128]{3,2,1,0:T(8,128)(2,1)S(1)}, u32[]{:S(2)}, u32[]{:S(2)}) collective-permute-start(bf16[2,4,16,128]{3,2,1,0:T(8,128)(2,1)S(1)} %get-tuple-element.58), channel_id=1, source_target_pairs={{0,8},{8,0},{16,24},{24,16},{1,9},{9,1},{17,25},{25,17},{2,10},{10... | collective-permute-start | bytes 98312 | tf_op jit(solution)/shard_map/ppermute | solution.py:364
  14.1 6.4 %collective-permute-start.6 = (bf16[2,4,16,128]{3,2,1,0:T(8,128)(2,1)S(1)}, bf16[2,4,16,128]{3,2,1,0:T(8,128)(2,1)S(1)}, u32[]{:S(2)}, u32[]{:S(2)}) collective-permute-start(bf16[2,4,16,128]{3,2,1,0:T(8,128)(2,1)S(1)} %get-tuple-element.59), channel_id=1, source_target_pairs={{0,24},{8,16},{16,8},{24,0},{1,25},{9,17},{17,9},{25,1},{2,26},{10... | collective-permute-start | bytes 98312 | tf_op jit(solution)/shard_map/ppermute | solution.py:364
  15.6 5.2 %collective-permute-start.5 = (bf16[2,4,16,128]{3,2,1,0:T(8,128)(2,1)S(1)}, bf16[2,4,16,128]{3,2,1,0:T(8,128)(2,1)S(1)}, u32[]{:S(2)}, u32[]{:S(2)}) collective-permute-start(bf16[2,4,16,128]{3,2,1,0:T(8,128)(2,1)S(1)} %get-tuple-element.60), channel_id=1, source_target_pairs={{0,16},{8,24},{16,0},{24,8},{1,17},{9,25},{17,1},{25,9},{2,18},{10... | collective-permute-start | bytes 98312 | tf_op jit(solution)/shard_map/ppermute | solution.py:364
  20.8 8.8 %collective-permute-start.7 = (bf16[4,2,4,16,128]{4,3,2,1,0:T(8,128)(2,1)S(1)}, bf16[4,2,4,16,128]{4,3,2,1,0:T(8,128)(2,1)S(1)}, u32[]{:S(2)}, u32[]{:S(2)}) collective-permute-start(bf16[4,2,4,16,128]{4,3,2,1,0:T(8,128)(2,1)S(1)} %pad_maximum_fusion.1), channel_id=1, source_target_pairs={{0,2},{1,3},{2,0},{3,1},{4,6},{5,7},{6,4},{7,5},{8,10},{9,11},{10,... | collective-permute-start | bytes 393224 | tf_op jit(solution)/shard_map/ppermute | solution.py:364
  22.2 6.7 %collective-permute-start.1 = (bf16[2,4,16,128]{3,2,1,0:T(8,128)(2,1)S(1)}, bf16[2,4,16,128]{3,2,1,0:T(8,128)(2,1)S(1)}, u32[]{:S(2)}, u32[]{:S(2)}) collective-permute-start(bf16[2,4,16,128]{3,2,1,0:T(8,128)(2,1)S(1)} %get-tuple-element.55), channel_id=1, source_target_pairs={{0,8},{8,0},{16,24},{24,16},{1,9},{9,1},{17,25},{25,17},{2,10},{10... | collective-permute-start | bytes 98312 | tf_op jit(solution)/shard_map/ppermute | solution.py:364
  23.1 5.8 %collective-permute-start.2 = (bf16[2,4,16,128]{3,2,1,0:T(8,128)(2,1)S(1)}, bf16[2,4,16,128]{3,2,1,0:T(8,128)(2,1)S(1)}, u32[]{:S(2)}, u32[]{:S(2)}) collective-permute-start(bf16[2,4,16,128]{3,2,1,0:T(8,128)(2,1)S(1)} %get-tuple-element.56), channel_id=1, source_target_pairs={{0,16},{8,24},{16,0},{24,8},{1,17},{9,25},{17,1},{25,9},{2,18},{10... | collective-permute-start | bytes 98312 | tf_op jit(solution)/shard_map/ppermute | solution.py:364
  24.1 5.0 %collective-permute-start.3 = (bf16[2,4,16,128]{3,2,1,0:T(8,128)(2,1)S(1)}, bf16[2,4,16,128]{3,2,1,0:T(8,128)(2,1)S(1)}, u32[]{:S(2)}, u32[]{:S(2)}) collective-permute-start(bf16[2,4,16,128]{3,2,1,0:T(8,128)(2,1)S(1)} %get-tuple-element.57), channel_id=1, source_target_pairs={{0,24},{8,16},{16,8},{24,0},{1,25},{9,17},{17,9},{25,1},{2,26},{10... | collective-permute-start | bytes 98312 | tf_op jit(solution)/shard_map/ppermute | solution.py:364
  31.4 21.8 %copy-start.3 = (f32[2048,128]{1,0:T(8,128)S(1)}, f32[2048,128]{1,0:T(8,128)}, u32[]{:S(2)}) copy-start(f32[2048,128]{1,0:T(8,128)} %get-tuple-element.35.gate_ref) | copy-start | bytes 3145732
  32.1 21.0 %copy-start.2 = (f32[2048,128]{1,0:T(8,128)S(1)}, f32[2048,128]{1,0:T(8,128)}, u32[]{:S(2)}) copy-start(f32[2048,128]{1,0:T(8,128)} %get-tuple-element.32.ordered_ref) | copy-start | bytes 3145732
  32.1 21.0 %copy-start.5 = (bf16[2,128,128]{2,1,0:T(8,128)(2,1)S(1)}, bf16[2,128,128]{2,1,0:T(8,128)(2,1)}, u32[]{:S(2)}) copy-start(bf16[2,128,128]{2,1,0:T(8,128)(2,1)} %w_out_ref.3) | copy-start | bytes 196612
  56.7 30.4 %all-to-all-start.2 = ((bf16[32,8,16,128]{3,2,1,0:T(8,128)(2,1)}), bf16[32,8,16,128]{3,2,1,0:T(8,128)(2,1)S(1)}, u32[]{:S(2)}, u32[]{:S(2)}) async-start(bf16[32,8,16,128]{3,2,1,0:T(8,128)(2,1)} %bitcast.47), calls=%async_computation.2 | async-start | bytes 2097152 | tf_op jit(solution)/shard_map/all_to_all | solution.py:462
  59.8 1.6 %collective-permute-start.8 = (bf16[4,2,8,16,128]{4,3,2,1,0:T(8,128)(2,1)S(1)}, bf16[4,2,8,16,128]{4,3,2,1,0:T(8,128)(2,1)S(1)}, u32[]{:S(2)}, u32[]{:S(2)}) collective-permute-start(bf16[4,2,8,16,128]{4,3,2,1,0:T(8,128)(2,1)S(1)} %copy-done.11), channel_id=1, source_target_pairs={{0,1},{1,0},{2,3},{3,2},{4,5},{5,4},{6,7},{7,6},{8,9},{9,8},{10,11... | collective-permute-start | bytes 786440 | tf_op jit(solution)/shard_map/ppermute | solution.py:364
  61.4 9.4 %collective-permute-start.12 = (bf16[2,8,16,128]{3,2,1,0:T(8,128)(2,1)S(1)}, bf16[2,8,16,128]{3,2,1,0:T(8,128)(2,1)S(1)}, u32[]{:S(2)}, u32[]{:S(2)}) collective-permute-start(bf16[2,8,16,128]{3,2,1,0:T(8,128)(2,1)S(1)} %get-tuple-element.50), channel_id=1, source_target_pairs={{0,8},{8,0},{16,24},{24,16},{1,9},{9,1},{17,25},{25,17},{2,10},{10... | collective-permute-start | bytes 196616 | tf_op jit(solution)/shard_map/ppermute | solution.py:364
  63.3 9.7 %collective-permute-start.14 = (bf16[2,8,16,128]{3,2,1,0:T(8,128)(2,1)S(1)}, bf16[2,8,16,128]{3,2,1,0:T(8,128)(2,1)S(1)}, u32[]{:S(2)}, u32[]{:S(2)}) collective-permute-start(bf16[2,8,16,128]{3,2,1,0:T(8,128)(2,1)S(1)} %get-tuple-element.51), channel_id=1, source_target_pairs={{0,24},{8,16},{16,8},{24,0},{1,25},{9,17},{17,9},{25,1},{2,26},{10... | collective-permute-start | bytes 196616 | tf_op jit(solution)/shard_map/ppermute | solution.py:364
  64.7 8.2 %collective-permute-start.13 = (bf16[2,8,16,128]{3,2,1,0:T(8,128)(2,1)S(1)}, bf16[2,8,16,128]{3,2,1,0:T(8,128)(2,1)S(1)}, u32[]{:S(2)}, u32[]{:S(2)}) collective-permute-start(bf16[2,8,16,128]{3,2,1,0:T(8,128)(2,1)S(1)} %get-tuple-element.52), channel_id=1, source_target_pairs={{0,16},{8,24},{16,0},{24,8},{1,17},{9,25},{17,1},{25,9},{2,18},{10... | collective-permute-start | bytes 196616 | tf_op jit(solution)/shard_map/ppermute | solution.py:364
  73.0 13.8 %collective-permute-start.15 = (bf16[4,2,8,16,128]{4,3,2,1,0:T(8,128)(2,1)S(1)}, bf16[4,2,8,16,128]{4,3,2,1,0:T(8,128)(2,1)S(1)}, u32[]{:S(2)}, u32[]{:S(2)}) collective-permute-start(bf16[4,2,8,16,128]{4,3,2,1,0:T(8,128)(2,1)S(1)} %pad_maximum_fusion), channel_id=1, source_target_pairs={{0,2},{1,3},{2,0},{3,1},{4,6},{5,7},{6,4},{7,5},{8,10},{9,11},{10,... | collective-permute-start | bytes 786440 | tf_op jit(solution)/shard_map/ppermute | solution.py:364
  77.6 6.5 %collective-permute-start.9 = (bf16[2,8,16,128]{3,2,1,0:T(8,128)(2,1)S(1)}, bf16[2,8,16,128]{3,2,1,0:T(8,128)(2,1)S(1)}, u32[]{:S(2)}, u32[]{:S(2)}) collective-permute-start(bf16[2,8,16,128]{3,2,1,0:T(8,128)(2,1)S(1)} %get-tuple-element.47), channel_id=1, source_target_pairs={{0,8},{8,0},{16,24},{24,16},{1,9},{9,1},{17,25},{25,17},{2,10},{10... | collective-permute-start | bytes 196616 | tf_op jit(solution)/shard_map/ppermute | solution.py:364
  77.6 6.5 %collective-permute-start.10 = (bf16[2,8,16,128]{3,2,1,0:T(8,128)(2,1)S(1)}, bf16[2,8,16,128]{3,2,1,0:T(8,128)(2,1)S(1)}, u32[]{:S(2)}, u32[]{:S(2)}) collective-permute-start(bf16[2,8,16,128]{3,2,1,0:T(8,128)(2,1)S(1)} %get-tuple-element.48), channel_id=1, source_target_pairs={{0,16},{8,24},{16,0},{24,8},{1,17},{9,25},{17,1},{25,9},{2,18},{10... | collective-permute-start | bytes 196616 | tf_op jit(solution)/shard_map/ppermute | solution.py:364
  78.3 6.8 %collective-permute-start.11 = (bf16[2,8,16,128]{3,2,1,0:T(8,128)(2,1)S(1)}, bf16[2,8,16,128]{3,2,1,0:T(8,128)(2,1)S(1)}, u32[]{:S(2)}, u32[]{:S(2)}) collective-permute-start(bf16[2,8,16,128]{3,2,1,0:T(8,128)(2,1)S(1)} %get-tuple-element.49), channel_id=1, source_target_pairs={{0,24},{8,16},{16,8},{24,0},{1,25},{9,17},{17,9},{25,1},{2,26},{10... | collective-permute-start | bytes 196616 | tf_op jit(solution)/shard_map/ppermute | solution.py:364
  87.1 12.6 %copy-start.1 = (f32[2048,128]{1,0:T(8,128)S(1)}, f32[2048,128]{1,0:T(8,128)}, u32[]{:S(2)}) copy-start(f32[2048,128]{1,0:T(8,128)} %shard_map.69.gate_ref) | copy-start | bytes 3145732
  (7 other events, 41.0 us)
